TPU v7x, 32 devices: a whole 2x2x4 slice. The times are simulated.
32 devices in a mesh: group: 4 (over y, x), lat: 4 (over z), lon: 2 (over core).
Axes of the slice: x: 2, y: 2, z: 4, core: 2. Of those that a mesh axis runs over, the one named last changes fastest.
Arguments:
- species_amounts: float32 [128, 4, 64, 256], P('group', None, 'lat', 'lon'), may hold values from -4 to 4
- zonal_cell_fraction: float32 [4, 64, 256], P('group', 'lat', 'lon'), may hold values from -0.3 to 0.3
- meridional_cell_fraction: float32 [4, 64, 256], P('group', 'lat', 'lon'), may hold values from -0.3 to 0.3
- updraft_cell_fraction: float32 [4, 64, 256], P('group', 'lat', 'lon'), may hold values from -0.3 to 0.3
- warmth_anomaly: float32 [4, 64, 256], P('group', 'lat', 'lon'), may hold values from -2 to 2
- mass_per_volume: float32 [4, 64, 256], P('group', 'lat', 'lon'), may hold values from 0.5 to 2
- chemistry_iterations: int32 [64, 256], P('lat', 'lon'), may hold values from 1 to 2, as said below
- companion_species: bfloat16 [512, 128], replicated, may hold values from -0.5 to 0.5
- stoichiometric_rate: bfloat16 [128, 512], replicated, may hold values from -0.25 to 0.25
- heat_yield: float32 [128], replicated, may hold values from -0.5 to 0.5
Outputs:
- tracers_out: float32 [128, 4, 64, 256], P('group', None, 'lat', 'lon')
- east_out: float32 [4, 64, 256], P('group', 'lat', 'lon')
- north_out: float32 [4, 64, 256], P('group', 'lat', 'lon')
- temp_out: float32 [4, 64, 256], P('group', 'lat', 'lon')
Inputs may be any that keep to these rules, and one draw needn't show every extreme that they name: `chemistry_iterations`: columns at latitude rows 48 and above hold 1 or 2, and the last row holds 2; all other columns hold 1.
All inputs are finite; a program needn't handle non-finite values.
Results may differ from a plain program's by a relative error of at most 0.0011.
Values sent between devices are 32-bit elements; how exact they have to be, the bound alone decides.
No kernel may reach another device: no remote copies, remote signals or barrier semaphores. Data moves between devices by JAX's collectives and lax.ppermute only.
A program may use at most 64 MiB of HBM per device.

v0:
```python
import jax
import jax.numpy as jnp
from jax import lax
from jax.sharding import PartitionSpec as P

diffusion = 0.1
pressure = 0.05
chem_step = 0.2
block_cells = 512


def extended(block, sides, width):
    for axis, dim in sides:
        count = lax.axis_size(axis)
        forward = [(i, i + 1) for i in range(count - 1)]
        backward = [(target, source) for source, target in forward]
        low = lax.ppermute(
            lax.slice_in_dim(block, block.shape[dim] - width, None, axis=dim), axis, forward
        )
        high = lax.ppermute(lax.slice_in_dim(block, 0, width, axis=dim), axis, backward)
        block = jnp.concatenate([low, block, high], axis=dim)
    return block


def transport(padded, east_pad, north_pad, upward):
    zonal_cells = padded[..., 1:-1, :]
    zonal_wind = east_pad[:, 1:-1, :]
    face_wind = 0.5 * (zonal_wind[..., :-1] + zonal_wind[..., 1:])
    face_flux = (
        jnp.maximum(face_wind, 0.0) * zonal_cells[..., :-1]
        + jnp.minimum(face_wind, 0.0) * zonal_cells[..., 1:]
    )
    change = face_flux[..., 1:] - face_flux[..., :-1]
    north_cells = padded[..., 1:-1]
    north_wind = north_pad[:, :, 1:-1]
    face_wind = 0.5 * (north_wind[:, :-1] + north_wind[:, 1:])
    face_flux = (
        jnp.maximum(face_wind, 0.0) * north_cells[..., :-1, :]
        + jnp.minimum(face_wind, 0.0) * north_cells[..., 1:, :]
    )
    change = change + (face_flux[..., 1:, :] - face_flux[..., :-1, :])
    centre = padded[..., 1:-1, 1:-1]
    face_wind = 0.5 * (upward[:-1] + upward[1:])
    face_flux = (
        jnp.maximum(face_wind, 0.0) * centre[..., :-1, :, :]
        + jnp.minimum(face_wind, 0.0) * centre[..., 1:, :, :]
    )
    closed = jnp.zeros_like(face_flux[..., :1, :, :])
    face_flux = jnp.concatenate([closed, face_flux, closed], axis=-3)
    change = change + (face_flux[..., 1:, :, :] - face_flux[..., :-1, :, :])
    return centre - change


def dynamics(padded):
    centre = padded[:, :, 1:-1, 1:-1]
    eastern = padded[:, :, 1:-1, 2:]
    western = padded[:, :, 1:-1, :-2]
    northern = padded[:, :, 2:, 1:-1]
    southern = padded[:, :, :-2, 1:-1]
    laplace = eastern + western + northern + southern - 4.0 * centre
    diffused = centre + diffusion * laplace
    zonal_axis_name = diffused[0] - pressure * (eastern[2] - western[2])
    meridional_axis_name = diffused[1] - pressure * (northern[2] - southern[2])
    return (zonal_axis_name, meridional_axis_name, diffused[2])


def react_block(
    tracer_block, rate_block, count_block, companion_species, stoichiometric_rate, heat_yield
):
    species = tracer_block.shape[0]
    width = tracer_block.shape[1]
    repeats = companion_species.shape[0] // species
    deepest = jnp.max(count_block)

    def keep_going(state_pair):
        return state_pair[0] < deepest

    def substep(state_pair):
        counter, current = state_pair
        narrow = current.astype(jnp.bfloat16)
        pair_terms = jnp.dot(companion_species, narrow, preferred_element_type=jnp.float32)
        quadratic = (
            (pair_terms.reshape(repeats, species, width) * current[None])
            .reshape(repeats * species, width)
            .astype(jnp.bfloat16)
        )
        tendency = (
            rate_block[None]
            * jnp.dot(stoichiometric_rate, quadratic, preferred_element_type=jnp.float32)
            - current
        )
        current = jnp.where(counter < count_block[None], current + chem_step * tendency, current)
        return (counter + 1, current)

    final = lax.while_loop(keep_going, substep, (jnp.zeros((), jnp.int32), tracer_block))[1]
    heating = jnp.dot(heat_yield[None], final - tracer_block, precision=lax.Precision.HIGHEST)[0]
    return (final, heating)


def react_cells(
    tracer_cells, rate_cells, count_cells, companion_species, stoichiometric_rate, heat_yield
):
    cell_count = tracer_cells.shape[1]
    sort_order = jnp.argsort(-count_cells, stable=True)
    inverse = jnp.argsort(sort_order)
    sorted_tracers = jnp.take(tracer_cells, sort_order, axis=1)
    sorted_rates = jnp.take(rate_cells, sort_order)
    sorted_counts = jnp.take(count_cells, sort_order)

    def one_block(block_index, outputs):
        offset = block_index * block_cells
        tracer_block = lax.dynamic_slice_in_dim(sorted_tracers, offset, block_cells, 1)
        rate_block = lax.dynamic_slice_in_dim(sorted_rates, offset, block_cells, 0)
        count_block = lax.dynamic_slice_in_dim(sorted_counts, offset, block_cells, 0)
        final, heating = react_block(
            tracer_block,
            rate_block,
            count_block,
            companion_species,
            stoichiometric_rate,
            heat_yield,
        )
        return (
            lax.dynamic_update_slice_in_dim(outputs[0], final, offset, 1),
            lax.dynamic_update_slice_in_dim(outputs[1], heating, offset, 0),
        )

    reacted, heated = lax.fori_loop(
        0,
        cell_count // block_cells,
        one_block,
        (jnp.zeros_like(sorted_tracers), jnp.zeros_like(sorted_rates)),
    )
    return (jnp.take(reacted, inverse, axis=1), jnp.take(heated, inverse))


def scattered(
    advected,
    reaction_rate,
    chemistry_iterations,
    companion_species,
    stoichiometric_rate,
    heat_yield,
):
    groups = lax.axis_size("group")
    own_group = lax.axis_index("group")
    stratum_total = advected.shape[1]
    meridian_span = advected.shape[2]
    parallel_span = advected.shape[3]
    column_part = parallel_span // groups
    count_field = jnp.broadcast_to(
        chemistry_iterations.astype(jnp.float32)[None],
        (stratum_total, meridian_span, parallel_span),
    )
    own_rates = lax.dynamic_slice_in_dim(reaction_rate, own_group * column_part, column_part, 2)
    own_counts = lax.dynamic_slice_in_dim(count_field, own_group * column_part, column_part, 2)
    cell_info = jnp.concatenate([own_rates, own_counts], axis=2)[None, :, None]
    arrived, info_in = (
        lax.all_to_all(
            lax.all_to_all(advected[:, :, None], "group", split_axis=1, concat_axis=0, tiled=True),
            "lat",
            split_axis=3,
            concat_axis=2,
            tiled=True,
        ),
        lax.all_to_all(
            lax.all_to_all(cell_info, "group", split_axis=1, concat_axis=0, tiled=True),
            "lat",
            split_axis=3,
            concat_axis=2,
            tiled=True,
        ),
    )
    species = arrived.shape[0]
    cell_shape = arrived.shape[1:]
    cell_data = info_in.reshape(groups, cell_shape[0], cell_shape[1], cell_shape[2], 2, column_part)
    cell_data = cell_data.transpose(4, 1, 2, 3, 0, 5).reshape(2, -1)
    reacted, heating = react_cells(
        arrived.reshape(species, -1),
        cell_data[0],
        cell_data[1].astype(jnp.int32),
        companion_species,
        stoichiometric_rate,
        heat_yield,
    )
    heat_copies = jnp.broadcast_to(heating.reshape((1,) + cell_shape), (groups,) + cell_shape)
    returned, heat_back = (
        lax.all_to_all(
            lax.all_to_all(
                reacted.reshape(arrived.shape), "group", split_axis=0, concat_axis=1, tiled=True
            ),
            "lat",
            split_axis=2,
            concat_axis=3,
            tiled=True,
        ),
        lax.all_to_all(
            lax.all_to_all(heat_copies, "group", split_axis=0, concat_axis=1, tiled=True),
            "lat",
            split_axis=2,
            concat_axis=3,
            tiled=True,
        ),
    )
    return (returned[:, :, 0], heat_back[0, :, 0])


def local(
    species_amounts,
    zonal_cell_fraction,
    meridional_cell_fraction,
    updraft_cell_fraction,
    warmth_anomaly,
    mass_per_volume,
    chemistry_iterations,
    companion_species,
    stoichiometric_rate,
    heat_yield,
):
    own_group = lax.axis_index("group")
    local_strata = warmth_anomaly.shape[0]
    owned_tracers = species_amounts.shape[0]
    columns = lax.all_gather(
        jnp.stack(
            [
                zonal_cell_fraction,
                meridional_cell_fraction,
                updraft_cell_fraction,
                warmth_anomaly,
                mass_per_volume,
            ]
        ),
        "group",
        axis=1,
        tiled=True,
    )
    zonal_axis_name, meridional_axis_name, upward, heat_snapshot, air_density = (
        columns[0],
        columns[1],
        columns[2],
        columns[3],
        columns[4],
    )
    stacked = jnp.concatenate(
        [species_amounts, jnp.stack([zonal_axis_name, meridional_axis_name, heat_snapshot])], axis=0
    )
    padded = extended(stacked, (("lat", 2), ("lon", 3)), 1)
    advected = transport(
        padded[:owned_tracers], padded[owned_tracers], padded[owned_tracers + 1], upward
    )
    new_east, new_north, warmed = dynamics(padded[owned_tracers:])
    reaction_rate = jax.nn.sigmoid(2.0 * heat_snapshot)
    reacted, heating = scattered(
        advected,
        reaction_rate,
        chemistry_iterations,
        companion_species,
        stoichiometric_rate,
        heat_yield,
    )
    heat_snapshot = warmed + heating / air_density
    start_level = own_group * local_strata
    east_mine = lax.dynamic_slice_in_dim(new_east, start_level, local_strata, 0)
    north_mine = lax.dynamic_slice_in_dim(new_north, start_level, local_strata, 0)
    thermal_mine = lax.dynamic_slice_in_dim(heat_snapshot, start_level, local_strata, 0)
    return (reacted, east_mine, north_mine, thermal_mine)


def solution(mesh):
    return jax.shard_map(
        local,
        mesh=mesh,
        in_specs=(
            P("group", None, "lat", "lon"),
            P("group", "lat", "lon"),
            P("group", "lat", "lon"),
            P("group", "lat", "lon"),
            P("group", "lat", "lon"),
            P("group", "lat", "lon"),
            P("lat", "lon"),
            P(),
            P(),
            P(),
        ),
        out_specs=(
            P("group", None, "lat", "lon"),
            P("group", "lat", "lon"),
            P("group", "lat", "lon"),
            P("group", "lat", "lon"),
        ),
        check_vma=False,
    )
```

profile of v0, /device:TPU:0, one launch (start us, length us, event | category | flops | bytes accessed | tf_op | source)
XLA Modules:
  0.0 233.8 jit_solution(8297542561840097252)
XLA Ops:
  4.2 10.0 %all_gather.3 = f32[5,4,16,128]{3,2,1,0:T(8,128)S(1)} all-gather(f32[5,1,16,128]{3,2,1,0:T(8,128)S(1)} %constant_dynamic-update-slice_fusion.1), channel_id=1, replica_groups=mesh['group'=4,'lat'=4,'lon'=2] {'group'}, dimensions={1}, use_global_device_ids=true | all-gather | bytes 204800 | tf_op jit(solution)/shard_map/all_gather | solution.py:223
  15.9 3.2 %all-to-all-start.2 = ((f32[4,1,1024]{2,1,0:T(1,128)}), f32[4,1,1024]{2,1,0:T(1,128)S(1)}, u32[]{:S(2)}, u32[]{:S(2)}) async-start(f32[4,1,1024]{2,1,0:T(1,128)} %reshape.163), calls=%async_computation.2 | async-start | bytes 32768 | tf_op jit(solution)/shard_map/all_to_all | solution.py:167
  19.2 1.3 pad_maximum_fusion.13
  20.5 3.5 %collective-permute-start = (f32[35,4,1,128]{3,2,1,0:T(1,128)S(1)}, f32[35,4,1,128]{3,2,1,0:T(1,128)S(1)}, u32[]{:S(2)}, u32[]{:S(2)}) collective-permute-start(f32[35,4,1,128]{3,2,1,0:T(1,128)S(1)} %get-tuple-element.273), channel_id=1, source_target_pairs={{0,2},{2,4},{4,6},{1,3},{3,5},{5,7},{8,10},{10,12},{12,14},{9,11},... | collective-permute-start | bytes 215048 | tf_op jit(solution)/shard_map/ppermute | solution.py:17
  24.0 1.3 collective-permute-start.1
  26.3 3.9 %collective-permute-done.1 = f32[35,4,1,128]{3,2,1,0:T(1,128)S(1)} collective-permute-done((f32[35,4,1,128]{3,2,1,0:T(1,128)S(1)}, f32[35,4,1,128]{3,2,1,0:T(1,128)S(1)}, u32[]{:S(2)}, u32[]{:S(2)}) %collective-permute-start.1) | collective-permute-done | bytes 71712 | tf_op jit(solution)/shard_map/ppermute | solution.py:20
  30.6 1.8 fusion.54
  32.4 2.2 copy.114
  35.5 1.3 collective-permute-start.3
  36.8 3.0 %collective-permute-start.2 = (f32[35,4,18,1]{0,1,3,2:T(4,128)S(1)}, f32[35,4,18,1]{0,1,3,2:T(4,128)S(1)}, u32[]{:S(2)}, u32[]{:S(2)}) collective-permute-start(f32[35,4,18,1]{0,1,3,2:T(4,128)S(1)} %copy.114), channel_id=1, source_target_pairs={{0,1},{2,3},{4,5},{6,7},{8,9},{10,11},{12,13},{14,15},{16,17},{18,... | collective-permute-start | bytes 30248 | tf_op jit(solution)/shard_map/ppermute | solution.py:17
  39.8 2.2 maximum_maximum_fusion.1
  42.0 1.5 copy.116
  43.6 2.7 %copy.117 = f32[35,4,18,1]{3,2,1,0:T(8,128)} copy(f32[35,4,18,1]{0,1,3,2:T(4,128)S(1)} %collective-permute-done.3) | data formatting | bytes 20160 | tf_op jit(solution)/shard_map/ppermute | solution.py:20
  46.2 1.1 pad_maximum_fusion.9
  47.7 3.2 %maximum_maximum_fusion = (f32[35,4,18,129]{3,2,1,0:T(8,128)S(1)}, f32[35,4,18,129]{3,2,1,0:T(8,128)S(1)}) fusion(f32[35,4,1,128]{3,2,1,0:T(1,128)S(1)} %collective-permute-done.1, f32[1,4,16,128]{3,2,1,0:T(8,128)S(1)} %get-tuple-element.276, f32[2,4,16,128]{3,2,1,0:T(8,128)S(1)} %slice.229, f32[32,4,16,128]{3,2,1,0:T(8,128)S(1)} %copy-done, ...), kind=kLoop, calls=%fused_computation.21 | loop fusion | flops 3250800 | bytes 3911040 | tf_op jit(solution)/shard_map/concatenate | solution.py:21
  54.7 1.1 copy.126
  55.7 4.1 %all-to-all-start = ((f32[32,4,1,16,128]{4,3,0,2,1:T(8,128)}), f32[32,4,1,16,128]{4,3,0,2,1:T(8,128)S(1)}, u32[]{:S(2)}, u32[]{:S(2)}) async-start(f32[32,4,1,16,128]{4,3,0,2,1:T(8,128)} %copy.126), calls=%async_computation | async-start | bytes 2097152 | tf_op jit(solution)/shard_map/all_to_all | solution.py:160
  61.9 11.2 %all-to-all-done = f32[32,4,1,16,128]{4,3,0,2,1:T(8,128)S(1)} async-done(((f32[32,4,1,16,128]{4,3,0,2,1:T(8,128)}), f32[32,4,1,16,128]{4,3,0,2,1:T(8,128)S(1)}, u32[]{:S(2)}, u32[]{:S(2)}) %all-to-all-start) | async-done | bytes 1048608 | tf_op jit(solution)/shard_map/all_to_all | solution.py:160
  73.0 3.9 %all-to-all-start.3 = ((f32[4,1,1024]{2,1,0:T(1,128)}), f32[4,1,1024]{2,1,0:T(1,128)S(1)}, u32[]{:S(2)}, u32[]{:S(2)}) async-start(f32[4,1,1024]{2,1,0:T(1,128)} %reshape.165), calls=%async_computation.3 | async-start | bytes 32768 | tf_op jit(solution)/shard_map/all_to_all | solution.py:166
  76.9 1.3 copy.127
  78.2 4.3 %all-to-all-done.3 = f32[4,1,1024]{2,1,0:T(1,128)S(1)} async-done(((f32[4,1,1024]{2,1,0:T(1,128)}), f32[4,1,1024]{2,1,0:T(1,128)S(1)}, u32[]{:S(2)}, u32[]{:S(2)}) %all-to-all-start.3) | async-done | bytes 16416 | tf_op jit(solution)/shard_map/all_to_all | solution.py:166
  82.5 3.7 %all-to-all-start.1 = ((f32[128,1,1,16,128]{4,0,2,1,3:T(8,128)}), f32[128,1,1,16,128]{4,0,2,1,3:T(8,128)S(1)}, u32[]{:S(2)}, u32[]{:S(2)}) async-start(f32[128,1,1,16,128]{4,0,2,1,3:T(8,128)} %copy.127), calls=%async_computation.1 | async-start | bytes 2097152 | tf_op jit(solution)/shard_map/all_to_all | solution.py:159
  87.3 5.0 %sort.34 = (s32[2048]{0:T(1024)}, s32[2048]{0:T(1024)S(1)}) sort(s32[2048]{0:T(1024)S(1)} %neg.8, s32[2048]{0:T(1024)S(1)} %iota.8), dimensions={0}, to_apply=%region_0.0 | sort | flops 22528 | bytes 32768 | tf_op jit(solution)/shard_map/jit(argsort)/sort | solution.py:104
  92.4 11.8 %gather_fusion = s32[2048]{0:T(1024)S(1)} fusion(s32[2048]{0:T(1024)S(1)} %convert_element_type.17, s32[2048]{0:T(1024)S(1)} %fusion.51), kind=kCustom, calls=%fused_computation.4 | custom fusion | bytes 24576 | tf_op jit(solution)/shard_map/jit(_take)/gather | solution.py:108
  104.2 11.8 %gather_fusion.2 = f32[2048]{0:T(1024)S(1)} fusion(f32[2048]{0:T(1024)S(1)} %squeeze.35, s32[2048]{0:T(1024)S(1)} %fusion.51), kind=kCustom, calls=%fused_computation.1.clone | custom fusion | bytes 24576 | tf_op jit(solution)/shard_map/jit(_take)/gather | solution.py:107
  116.0 5.0 %sort.35 = (s32[2048]{0:T(1024)}, s32[2048]{0:T(1024)S(1)}) sort(s32[2048]{0:T(1024)S(1)} %get-tuple-element.201, s32[2048]{0:T(1024)S(1)} %iota.9), dimensions={0}, to_apply=%region_6.9 | sort | flops 22528 | bytes 32768 | tf_op jit(solution)/shard_map/jit(argsort)/sort | solution.py:105
  121.4 7.6 %gather_fusion.1 = f32[2048,128]{1,0:T(8,128)} fusion(f32[128,2048]{0,1:T(8,128)S(1)} %bitcast.99, s32[2048]{0:T(1024)S(1)} %fusion.51), kind=kCustom, calls=%fused_computation.clone | custom fusion | bytes 2105344 | tf_op jit(solution)/shard_map/jit(_take)/gather | solution.py:106
  129.0 2.6 %select_bitcast_fusion = f32[128,2048]{0,1:T(8,128)} fusion(f32[2048,128]{1,0:T(8,128)} %gather_fusion.1, pred[2048]{0:T(1024)(128)(4,1)S(1)} %get-tuple-element.262), kind=kLoop, calls=%fused_computation.38 | loop fusion | flops 262144 | bytes 2099200 | tf_op jit(solution)/shard_map/jit(_take)/select_n | solution.py:106
  131.6 1.0 broadcast_in_dim.69
  132.7 23.4 %while.38 = (s32[]{:T(128)}, f32[128,2048]{0,1:T(8,128)}, f32[2048]{0:T(1024)S(1)}, f32[128,2048]{0,1:T(8,128)}, s32[2048]{0:T(1024)S(1)}, /*index=5*/f32[2048]{...) while((s32[]{:T(128)}, f32[128,2048]{0,1:T(8,128)}, ...), condition=%wide.region_5.8_spmd, body=%wide.region_1.7_spmd.sunk | while | flops 135988224 | bytes 6311812 | solution.py:128
  134.5 4.0 %while.39 = (s32[]{:T(128)}, f32[128,512]{0,1:T(8,128)S(1)}, s32[]{:T(128)}, s32[512]{0:T(512)S(1)}, f32[512]{0:T(512)S(1)}, /*index=5*/bf16[512,128]{1,0:T(8,128)(2,1)S(1)}, bf16[128,512]{1,0:T(8,128)(2,1)S(1)}, s32[]{:T(128)}) while((s32[]{:T(128)}, f32[128,512]{0,1:T(8,128)S(1)}, s32[]{:T(128)}, s32[512]{0:T(512)S(1)}, f32[512]{0:T(512)S(1)}, ...), condition=%wide.region_4.6_spmd, body=%wide.region_3.5_spmd.sunk | while | flops 135135744 | bytes 4199521 | solution.py:95
  141.6 2.3 %while.39 = (s32[]{:T(128)}, f32[128,512]{0,1:T(8,128)S(1)}, s32[]{:T(128)}, s32[512]{0:T(512)S(1)}, f32[512]{0:T(512)S(1)}, /*index=5*/bf16[512,128]{1,0:T(8,128)(2,1)S(1)}, bf16[128,512]{1,0:T(8,128)(2,1)S(1)}, s32[]{:T(128)}) while((s32[]{:T(128)}, f32[128,512]{0,1:T(8,128)S(1)}, s32[]{:T(128)}, s32[512]{0:T(512)S(1)}, f32[512]{0:T(512)S(1)}, ...), condition=%wide.region_4.6_spmd, body=%wide.region_3.5_spmd.sunk | while | flops 135135744 | bytes 4199521 | solution.py:95
  147.0 2.3 %while.39 = (s32[]{:T(128)}, f32[128,512]{0,1:T(8,128)S(1)}, s32[]{:T(128)}, s32[512]{0:T(512)S(1)}, f32[512]{0:T(512)S(1)}, /*index=5*/bf16[512,128]{1,0:T(8,128)(2,1)S(1)}, bf16[128,512]{1,0:T(8,128)(2,1)S(1)}, s32[]{:T(128)}) while((s32[]{:T(128)}, f32[128,512]{0,1:T(8,128)S(1)}, s32[]{:T(128)}, s32[512]{0:T(512)S(1)}, f32[512]{0:T(512)S(1)}, ...), condition=%wide.region_4.6_spmd, body=%wide.region_3.5_spmd.sunk | while | flops 135135744 | bytes 4199521 | solution.py:95
  152.5 2.3 %while.39 = (s32[]{:T(128)}, f32[128,512]{0,1:T(8,128)S(1)}, s32[]{:T(128)}, s32[512]{0:T(512)S(1)}, f32[512]{0:T(512)S(1)}, /*index=5*/bf16[512,128]{1,0:T(8,128)(2,1)S(1)}, bf16[128,512]{1,0:T(8,128)(2,1)S(1)}, s32[]{:T(128)}) while((s32[]{:T(128)}, f32[128,512]{0,1:T(8,128)S(1)}, s32[]{:T(128)}, s32[512]{0:T(512)S(1)}, f32[512]{0:T(512)S(1)}, ...), condition=%wide.region_4.6_spmd, body=%wide.region_3.5_spmd.sunk | while | flops 135135744 | bytes 4199521 | solution.py:95
  156.1 11.8 %gather_fusion.4 = f32[2048]{0:T(1024)S(1)} fusion(f32[2048]{0:T(1024)S(1)} %get-tuple-element.498, s32[2048]{0:T(1024)S(1)} %fusion.52), kind=kCustom, calls=%fused_computation.3.clone | custom fusion | bytes 24576 | tf_op jit(solution)/shard_map/jit(_take)/gather | solution.py:134
  167.9 5.5 %gather_fusion.3 = f32[2048,128]{1,0:T(8,128)S(1)} fusion(f32[128,2048]{0,1:T(8,128)S(1)} %copy-done.1, s32[2048]{0:T(1024)S(1)} %fusion.52), kind=kCustom, calls=%fused_computation.2.clone | custom fusion | bytes 2105344 | tf_op jit(solution)/shard_map/jit(_take)/gather | solution.py:134
  174.0 3.3 %all-to-all-start.6 = ((f32[4,1,4,4,128]{4,3,2,1,0:T(4,128)}), f32[4,1,4,4,128]{4,3,2,1,0:T(4,128)S(1)}, u32[]{:S(2)}, u32[]{:S(2)}) async-start(f32[4,1,4,4,128]{4,3,2,1,0:T(4,128)} %broadcast_in_dim.77), calls=%async_computation.6 | async-start | bytes 65536 | tf_op jit(solution)/shard_map/all_to_all | solution.py:198
  177.6 1.4 copy.129
  179.0 3.0 %all-to-all-done.6 = f32[4,1,4,4,128]{4,3,2,1,0:T(4,128)S(1)} async-done(((f32[4,1,4,4,128]{4,3,2,1,0:T(4,128)}), f32[4,1,4,4,128]{4,3,2,1,0:T(4,128)S(1)}, u32[]{:S(2)}, u32[]{:S(2)}) %all-to-all-start.6) | async-done | bytes 32800 | tf_op jit(solution)/shard_map/all_to_all | solution.py:198
  182.0 3.5 %all-to-all-start.4 = ((f32[128,1,4,4,128]{4,3,2,1,0:T(4,128)}), f32[128,1,4,4,128]{4,3,2,1,0:T(4,128)S(1)}, u32[]{:S(2)}, u32[]{:S(2)}) async-start(f32[128,1,4,4,128]{4,3,2,1,0:T(4,128)} %copy.129), calls=%async_computation.4 | async-start | bytes 2097152 | tf_op jit(solution)/shard_map/all_to_all | solution.py:189
  186.1 9.9 %all-to-all-done.4 = f32[128,1,4,4,128]{4,3,2,1,0:T(4,128)S(1)} async-done(((f32[128,1,4,4,128]{4,3,2,1,0:T(4,128)}), f32[128,1,4,4,128]{4,3,2,1,0:T(4,128)S(1)}, u32[]{:S(2)}, u32[]{:S(2)}) %all-to-all-start.4) | async-done | bytes 1048608 | tf_op jit(solution)/shard_map/all_to_all | solution.py:189
  196.0 4.6 %all-to-all-start.7 = ((f32[1,4,4,4,128]{4,3,1,0,2:T(4,128)}), f32[1,4,4,4,128]{4,3,1,0,2:T(4,128)S(1)}, u32[]{:S(2)}, u32[]{:S(2)}) async-start(f32[1,4,4,4,128]{4,3,1,0,2:T(4,128)} %copy.131), calls=%async_computation.7 | async-start | bytes 65536 | tf_op jit(solution)/shard_map/all_to_all | solution.py:197
  200.6 1.3 copy.130
  201.9 4.4 %all-to-all-done.7 = f32[1,4,4,4,128]{4,3,1,0,2:T(4,128)S(1)} async-done(((f32[1,4,4,4,128]{4,3,1,0,2:T(4,128)}), f32[1,4,4,4,128]{4,3,1,0,2:T(4,128)S(1)}, u32[]{:S(2)}, u32[]{:S(2)}) %all-to-all-start.7) | async-done | bytes 32800 | tf_op jit(solution)/shard_map/all_to_all | solution.py:197
  206.3 4.3 %all-to-all-start.5 = ((f32[32,4,4,4,128]{4,0,1,3,2:T(8,128)}), f32[32,4,4,4,128]{4,0,1,3,2:T(8,128)}, u32[]{:S(2)}, u32[]{:S(2)}) async-start(f32[32,4,4,4,128]{4,0,1,3,2:T(8,128)} %bitcast.101), calls=%async_computation.5 | async-start | bytes 2097152 | tf_op jit(solution)/shard_map/all_to_all | solution.py:188
  210.7 1.2 fusion.21
  213.5 17.5 %all-to-all-done.5 = f32[32,4,4,4,128]{4,0,1,3,2:T(8,128)} async-done(((f32[32,4,4,4,128]{4,0,1,3,2:T(8,128)}), f32[32,4,4,4,128]{4,0,1,3,2:T(8,128)}, u32[]{:S(2)}, u32[]{:S(2)}) %all-to-all-start.5) | async-done | bytes 1048608 | tf_op jit(solution)/shard_map/all_to_all | solution.py:188
  231.0 2.8 %copy.133 = f32[32,4,16,128]{3,2,1,0:T(8,128)} copy(f32[32,4,16,128]{3,0,1,2:T(8,128)} %bitcast.28) | data formatting | bytes 2097152
  (138 shorter events, 35.4 us)
Async XLA Ops:
  0.6 24.7 %copy-start = (f32[32,4,16,128]{3,2,1,0:T(8,128)S(1)}, f32[32,4,16,128]{3,2,1,0:T(8,128)}, u32[]{:S(2)}) copy-start(f32[32,4,16,128]{3,2,1,0:T(8,128)} %param.18) | copy-start | bytes 3145732
  15.9 39.8 %all-to-all-start.2 = ((f32[4,1,1024]{2,1,0:T(1,128)}), f32[4,1,1024]{2,1,0:T(1,128)S(1)}, u32[]{:S(2)}, u32[]{:S(2)}) async-start(f32[4,1,1024]{2,1,0:T(1,128)} %reshape.163), calls=%async_computation.2 | async-start | bytes 32768 | tf_op jit(solution)/shard_map/all_to_all | solution.py:167
  20.5 5.8 %collective-permute-start = (f32[35,4,1,128]{3,2,1,0:T(1,128)S(1)}, f32[35,4,1,128]{3,2,1,0:T(1,128)S(1)}, u32[]{:S(2)}, u32[]{:S(2)}) collective-permute-start(f32[35,4,1,128]{3,2,1,0:T(1,128)S(1)} %get-tuple-element.273), channel_id=1, source_target_pairs={{0,2},{2,4},{4,6},{1,3},{3,5},{5,7},{8,10},{10,12},{12,14},{9,11},... | collective-permute-start | bytes 215048 | tf_op jit(solution)/shard_map/ppermute | solution.py:17
  24.0 6.2 %collective-permute-start.1 = (f32[35,4,1,128]{3,2,1,0:T(1,128)S(1)}, f32[35,4,1,128]{3,2,1,0:T(1,128)S(1)}, u32[]{:S(2)}, u32[]{:S(2)}) collective-permute-start(f32[35,4,1,128]{3,2,1,0:T(1,128)S(1)} %get-tuple-element.274), channel_id=1, source_target_pairs={{2,0},{4,2},{6,4},{3,1},{5,3},{7,5},{10,8},{12,10},{14,12},{11,9},... | collective-permute-start | bytes 215048 | tf_op jit(solution)/shard_map/ppermute | solution.py:20
  35.5 8.1 %collective-permute-start.3 = (f32[35,4,18,1]{0,1,3,2:T(4,128)S(1)}, f32[35,4,18,1]{0,1,3,2:T(4,128)S(1)}, u32[]{:S(2)}, u32[]{:S(2)}) collective-permute-start(f32[35,4,18,1]{0,1,3,2:T(4,128)S(1)} %copy.115), channel_id=1, source_target_pairs={{1,0},{3,2},{5,4},{7,6},{9,8},{11,10},{13,12},{15,14},{17,16},{19,... | collective-permute-start | bytes 30248 | tf_op jit(solution)/shard_map/ppermute | solution.py:20
  36.8 5.2 %collective-permute-start.2 = (f32[35,4,18,1]{0,1,3,2:T(4,128)S(1)}, f32[35,4,18,1]{0,1,3,2:T(4,128)S(1)}, u32[]{:S(2)}, u32[]{:S(2)}) collective-permute-start(f32[35,4,18,1]{0,1,3,2:T(4,128)S(1)} %copy.114), channel_id=1, source_target_pairs={{0,1},{2,3},{4,5},{6,7},{8,9},{10,11},{12,13},{14,15},{16,17},{18,... | collective-permute-start | bytes 30248 | tf_op jit(solution)/shard_map/ppermute | solution.py:17
  43.5 4.2 %copy-start.4 = (f32[35,4,18,1]{3,2,1,0:T(8,128)}, f32[35,4,18,1]{3,2,1,0:T(8,128)S(1)}, u32[]{:S(2)}) copy-start(f32[35,4,18,1]{3,2,1,0:T(8,128)S(1)} %copy.116) | copy-start | bytes 30244
  46.2 1.5 copy-start.6
  50.9 1.5 copy-start.8
  50.9 2.0 copy-start.9
  52.9 1.1 copy-start.10
  55.7 17.3 %all-to-all-start = ((f32[32,4,1,16,128]{4,3,0,2,1:T(8,128)}), f32[32,4,1,16,128]{4,3,0,2,1:T(8,128)S(1)}, u32[]{:S(2)}, u32[]{:S(2)}) async-start(f32[32,4,1,16,128]{4,3,0,2,1:T(8,128)} %copy.126), calls=%async_computation | async-start | bytes 2097152 | tf_op jit(solution)/shard_map/all_to_all | solution.py:160
  73.0 9.5 %all-to-all-start.3 = ((f32[4,1,1024]{2,1,0:T(1,128)}), f32[4,1,1024]{2,1,0:T(1,128)S(1)}, u32[]{:S(2)}, u32[]{:S(2)}) async-start(f32[4,1,1024]{2,1,0:T(1,128)} %reshape.165), calls=%async_computation.3 | async-start | bytes 32768 | tf_op jit(solution)/shard_map/all_to_all | solution.py:166
  82.5 38.5 %all-to-all-start.1 = ((f32[128,1,1,16,128]{4,0,2,1,3:T(8,128)}), f32[128,1,1,16,128]{4,0,2,1,3:T(8,128)S(1)}, u32[]{:S(2)}, u32[]{:S(2)}) async-start(f32[128,1,1,16,128]{4,0,2,1,3:T(8,128)} %copy.127), calls=%async_computation.1 | async-start | bytes 2097152 | tf_op jit(solution)/shard_map/all_to_all | solution.py:159
  129.0 3.6 %copy-start.2 = (bf16[512,128]{1,0:T(8,128)(2,1)S(1)}, bf16[512,128]{1,0:T(8,128)(2,1)}, u32[]{:S(2)}) copy-start(bf16[512,128]{1,0:T(8,128)(2,1)} %param.25) | copy-start | bytes 393220
  129.0 3.6 %copy-start.3 = (bf16[128,512]{1,0:T(8,128)(2,1)S(1)}, bf16[128,512]{1,0:T(8,128)(2,1)}, u32[]{:S(2)}) copy-start(bf16[128,512]{1,0:T(8,128)(2,1)} %param.26) | copy-start | bytes 393220
  129.0 3.6 %copy-start.11 = (f32[128]{0:T(128)S(1)}, f32[128]{0:T(128)}, u32[]{:S(2)}) copy-start(f32[128]{0:T(128)} %param.27) | copy-start | bytes 1540
  156.1 11.8 %copy-start.1 = (f32[128,2048]{0,1:T(8,128)S(1)}, f32[128,2048]{0,1:T(8,128)}, u32[]{:S(2)}) copy-start(f32[128,2048]{0,1:T(8,128)} %get-tuple-element.497) | copy-start | bytes 3145732
  174.0 8.0 %all-to-all-start.6 = ((f32[4,1,4,4,128]{4,3,2,1,0:T(4,128)}), f32[4,1,4,4,128]{4,3,2,1,0:T(4,128)S(1)}, u32[]{:S(2)}, u32[]{:S(2)}) async-start(f32[4,1,4,4,128]{4,3,2,1,0:T(4,128)} %broadcast_in_dim.77), calls=%async_computation.6 | async-start | bytes 65536 | tf_op jit(solution)/shard_map/all_to_all | solution.py:198
  182.0 14.0 %all-to-all-start.4 = ((f32[128,1,4,4,128]{4,3,2,1,0:T(4,128)}), f32[128,1,4,4,128]{4,3,2,1,0:T(4,128)S(1)}, u32[]{:S(2)}, u32[]{:S(2)}) async-start(f32[128,1,4,4,128]{4,3,2,1,0:T(4,128)} %copy.129), calls=%async_computation.4 | async-start | bytes 2097152 | tf_op jit(solution)/shard_map/all_to_all | solution.py:189
  196.0 10.3 %all-to-all-start.7 = ((f32[1,4,4,4,128]{4,3,1,0,2:T(4,128)}), f32[1,4,4,4,128]{4,3,1,0,2:T(4,128)S(1)}, u32[]{:S(2)}, u32[]{:S(2)}) async-start(f32[1,4,4,4,128]{4,3,1,0,2:T(4,128)} %copy.131), calls=%async_computation.7 | async-start | bytes 65536 | tf_op jit(solution)/shard_map/all_to_all | solution.py:197
  201.9 8.7 %copy-start.5 = (f32[35,4,18,1]{3,2,1,0:T(8,128)S(1)}, f32[35,4,18,1]{3,2,1,0:T(8,128)}, u32[]{:S(2)}) copy-start(f32[35,4,18,1]{3,2,1,0:T(8,128)} %copy-done.4) | copy-start | bytes 30244
  206.3 24.7 %all-to-all-start.5 = ((f32[32,4,4,4,128]{4,0,1,3,2:T(8,128)}), f32[32,4,4,4,128]{4,0,1,3,2:T(8,128)}, u32[]{:S(2)}, u32[]{:S(2)}) async-start(f32[32,4,4,4,128]{4,0,1,3,2:T(8,128)} %bitcast.101), calls=%async_computation.5 | async-start | bytes 2097152 | tf_op jit(solution)/shard_map/all_to_all | solution.py:188
  210.6 1.5 copy-start.7
where the time goes:
time: 235 us; the launch traced here: 234 us
  local copies, waits for them, and re-layouts  86 us (37%)
  waiting for transfers between devices  54.2 us (23%)
  starting transfers between devices  39.7 us (17%)
  other arithmetic  31.7 us (13%)
  blocking collectives  10 us (4%)
  loops' own time  6.19 us (3%)
  matrix products  4.96 us (2%)
    all_to_all x1, waiting for transfers between devices, scattered(): lax.all_to_all(lax.all_to_all(reacted.reshape(arrived.shape), 'group', sp...  17.5 us
    gather x2, local copies, waits for them, and re-layouts, react_cells(): return (jnp.take(reacted, inverse, axis=1), jnp.take(heated, inverse))  17.2 us
    gather x1, local copies, waits for them, and re-layouts, react_cells(): sorted_rates = jnp.take(rate_cells, sort_order)  11.8 us
    gather x1, local copies, waits for them, and re-layouts, react_cells(): sorted_counts = jnp.take(count_cells, sort_order)  11.8 us
    all_to_all x1, waiting for transfers between devices, scattered(): lax.all_to_all(advected[:, :, None], 'group', split_axis=1, concat_axis=0...  11.2 us
    all_gather x1, blocking collectives, local(): lax.all_gather(jnp.stack([zonal_cell_fraction, meridional_cell_fraction,...  10 us
    all_to_all x1, waiting for transfers between devices, scattered(): lax.all_to_all(reacted.reshape(arrived.shape), 'group', split_axis=0, con...  9.9 us
    unnamed x33, local copies, waits for them, and re-layouts  9.68 us
  transfers between devices with their start and end apart: 12, of which 7 were waited for; matrix products, arithmetic and copies ran while one was open for 28% of the time, Pallas kernels for 0%

commit v1 on v0

v1 whole, which is shorter than its diff:
```python
import functools

import jax
import jax.numpy as jnp
from jax import lax
from jax.experimental import pallas as pl
from jax.experimental.pallas import tpu as pltpu
from jax.sharding import PartitionSpec as P

diffusion = 0.1
pressure = 0.05
chem_step = 0.2

VMEM = pl.BlockSpec(memory_space=pltpu.VMEM)
SMEM = pl.BlockSpec(memory_space=pltpu.SMEM)
F32 = jnp.float32


def struct(*shape, dtype=F32):
    return jax.ShapeDtypeStruct(shape, dtype)


def call(kernel, out_shape, n_in, flops=0, touched=0, scratch=()):
    return pl.pallas_call(
        kernel,
        out_shape=out_shape,
        in_specs=[SMEM] + [VMEM] * (n_in - 1),
        out_specs=jax.tree.map(lambda _: VMEM, out_shape),
        scratch_shapes=list(scratch),
        compiler_params=pltpu.CompilerParams(vmem_limit_bytes=40 * 1024 * 1024),
        cost_estimate=pl.CostEstimate(flops=flops, bytes_accessed=touched, transcendentals=0),
    )


def even_pairs(count):
    return [(i, i ^ 1) for i in range(count) if (i ^ 1) < count]


def odd_pairs(count):
    pairs = []
    for i in range(1, count - 1, 2):
        pairs += [(i, i + 1), (i + 1, i)]
    return pairs


def neighbours(messages, axis):
    count = lax.axis_size(axis)
    return [
        lax.ppermute(m, axis, pairs)
        for m, pairs in zip(messages, (even_pairs(count), odd_pairs(count)))
    ]


def partner_swap(block, hop):
    return lax.ppermute(block, "group", [(i, i ^ hop) for i in range(lax.axis_size("group"))])


def lane_ids(shape):
    return lax.broadcasted_iota(jnp.int32, shape, len(shape) - 1)


def row_ids(shape):
    return lax.broadcasted_iota(jnp.int32, shape, len(shape) - 2)


def pack_columns(ids, species, east, north, warmth, *messages):
    tracers, strata, rows, width = species.shape
    lane = lane_ids((rows, width))
    for at, message in enumerate(messages):
        high = ids[2] == at
        edge = jnp.where(high, width - 1, 0)

        def one(t, acc):
            for k in range(strata):
                place = t * strata + k
                turned = pltpu.roll(species[t, k], lax.rem(place - edge + width, width), 1)
                acc = jnp.where(lane == place, turned, acc)
            return acc

        message[0:rows] = lax.fori_loop(0, tracers, one, jnp.zeros((rows, width), F32), unroll=4)
        fields = jnp.zeros((rows, width), F32)
        for place, field in enumerate((east, north, warmth)):
            turned = pltpu.roll(field[0], lax.rem(place - edge + width, width), 1)
            fields = jnp.where(lane == place, turned, fields)
        message[rows:2 * rows] = fields


def middle(value):
    quarter = value.shape[0] // 4
    return value[quarter:3 * quarter]


def rims(value):
    quarter = value.shape[0] // 4
    return jnp.concatenate([value[:quarter], value[3 * quarter:]], axis=0)


def faces(low, high):
    wind = 0.5 * (low + high)
    return jnp.maximum(wind, 0.0), jnp.minimum(wind, 0.0)


def rim_lanes(even, got, place):
    columns = [g[:, place:place + 1] for g in got]
    if len(columns) == 1:
        columns.append(jnp.zeros_like(columns[0]))
    return (
        jnp.where(even, columns[1], columns[0]),
        jnp.where(even, columns[0], columns[1]),
    )


def transport_kernel(chunk, n_lon, n_lat, slots, ids, species, *refs):
    refs = list(refs)
    winds = [refs.pop(0) for _ in range(slots)]
    lon_in = [refs.pop(0) for _ in range(n_lon)]
    lat_in = [refs.pop(0) for _ in range(n_lat)] if chunk else []
    outs = [refs.pop(0) for _ in range(slots)]
    lat_out = [] if chunk else [refs.pop(0) for _ in range(n_lat)]
    upward = refs.pop(0)
    tracers, strata, rows, width = species.shape
    half = rows // 2
    quarter = rows // 4
    me, lat_even, lon_even = ids[0], ids[1] == 0, ids[2] == 0
    pick = rims if chunk else middle
    lane = lane_ids((half, width))
    row = row_ids((half, width))
    whole_lane = lane_ids((rows, width))
    whole_row = row_ids((rows, width))

    for slot in range(slots):
        upward[me ^ slot] = winds[slot][2]

    def north_rims(level):
        if not chunk:
            zero = jnp.zeros((1, width), F32)
            return zero, zero
        got = [m[pl.ds(tracers * strata + level, 1), :] for m in lat_in]
        if len(got) == 1:
            got.append(jnp.zeros_like(got[0]))
        return jnp.where(lat_even, got[1], got[0]), jnp.where(lat_even, got[0], got[1])

    coefficients = []
    for slot in range(slots):
        level = me ^ slot
        east, north, up = winds[slot][0], winds[slot][1], winds[slot][2]
        low, high = rim_lanes(lon_even, [winds[slot][3 + at] for at in range(n_lon)], 0)
        east_next = jnp.where(whole_lane == width - 1, high, pltpu.roll(east, width - 1, 1))
        east_last = jnp.where(whole_lane == 0, low, pltpu.roll(east, 1, 1))
        low, high = north_rims(level)
        north_next = jnp.where(whole_row == rows - 1, high, pltpu.roll(north, rows - 1, 0))
        north_last = jnp.where(whole_row == 0, low, pltpu.roll(north, 1, 0))
        above = upward[jnp.minimum(level + 1, strata - 1)]
        below = upward[jnp.maximum(level - 1, 0)]
        has_above = jnp.where(level < strata - 1, 1.0, 0.0)
        has_below = jnp.where(level > 0, 1.0, 0.0)
        east_out, east_in = faces(east, east_next)
        west_in, west_out = faces(east_last, east)
        north_out, north_in = faces(north, north_next)
        south_in, south_out = faces(north_last, north)
        up_out, up_in = [has_above * f for f in faces(up, above)]
        down_in, down_out = [has_below * f for f in faces(below, up)]
        stay = 1.0 - (
            (east_out - west_out) + (north_out - south_out) + (up_out - down_out)
        )
        coefficients.append(
            [pick(f) for f in (stay, -east_in, west_in, -north_in, south_in, -up_in, down_in)]
        )

    columns = [pick(m[0:rows]) for m in lon_in]
    if n_lon == 2:
        columns = [jnp.where(lon_even, columns[1], columns[0]), jnp.where(lon_even, columns[0], columns[1])]
    else:
        missing = jnp.where(lon_even, 0, width - 1)
        for c in coefficients:
            at = 2 if False else None
            c[1] = jnp.where((lane == width - 1) & (missing == width - 1), 0.0, c[1])
            c[2] = jnp.where((lane == 0) & (missing == 0), 0.0, c[2])

    def one(t, carry):
        for slot in range(slots):
            level = me ^ slot
            stay, east_in, west_in, north_in, south_in, up_in, down_in = coefficients[slot]
            place = t * strata + level
            if n_lon == 2:
                low = pltpu.roll(columns[0], lax.rem(width - place, width), 1)
                high = pltpu.roll(columns[1], width - 1 - place, 1)
            else:
                edge = jnp.where(lon_even, width - 1, 0)
                low = high = pltpu.roll(columns[0], lax.rem(width + edge - place, width), 1)
            above = jnp.minimum(level + 1, strata - 1)
            below = jnp.maximum(level - 1, 0)
            if chunk:
                first, last = species[t, level, 0:half], species[t, level, half:rows]
                here = jnp.where(row < quarter, first, last)
                got = [m[pl.ds(place, 1), :] for m in lat_in]
                if len(got) == 1:
                    got.append(jnp.zeros_like(got[0]))
                south_rim = jnp.where(lat_even, got[1], got[0])
                north_rim = jnp.where(lat_even, got[0], got[1])
                south = jnp.where(row < quarter - 1, first, last)
                south = jnp.where(row == 0, south_rim, pltpu.roll(south, 1, 0))
                north = jnp.where(row < quarter + 1, first, last)
                north = jnp.where(row == half - 1, north_rim, pltpu.roll(north, half - 1, 0))
                up = jnp.where(row < quarter, species[t, above, 0:half], species[t, above, half:rows])
                down = jnp.where(row < quarter, species[t, below, 0:half], species[t, below, half:rows])
            else:
                here = species[t, level, quarter:3 * quarter]
                south = species[t, level, quarter - 1:3 * quarter - 1]
                north = species[t, level, quarter + 1:3 * quarter + 1]
                up = species[t, above, quarter:3 * quarter]
                down = species[t, below, quarter:3 * quarter]
            east = jnp.where(lane == width - 1, high, pltpu.roll(here, width - 1, 1))
            west = jnp.where(lane == 0, low, pltpu.roll(here, 1, 1))
            value = (
                (stay * here + east_in * east)
                + (west_in * west + north_in * north)
                + (south_in * south + up_in * up)
                + down_in * down
            )
            outs[slot][pl.ds(t, half, stride=tracers), :] = value
        return carry

    lax.fori_loop(0, tracers, one, 0, unroll=2)

    for at, message in enumerate(lat_out):
        top = ids[1] == at
        edge = jnp.where(top, rows - 1, 0)

        def pack(t, carry):
            block = [species[t, k, pl.ds(edge, 1), :] for k in range(strata)]
            for k in range(strata):
                message[pl.ds(t * strata + k, 1), :] = block[k]
            return carry

        lax.fori_loop(0, tracers, pack, 0, unroll=4)
        base = tracers * strata
        for slot in range(slots):
            message[pl.ds(base + (me ^ slot), 1), :] = winds[slot][1, pl.ds(edge, 1), :]
        message[base + strata:base + strata + 1] = winds[0][0, pl.ds(edge, 1), :]
        message[base + strata + 1:base + strata + 2] = winds[0][3 + n_lon, pl.ds(edge, 1), :]


def chemistry_kernel(chunk, slots, ids, deepest, *refs):
    refs = list(refs)
    advected = [refs.pop(0) for _ in range(slots)]
    warmth, counts, companion, stoichiometry, yields = [refs.pop(0) for _ in range(5)]
    outs = [refs.pop(0) for _ in range(slots)]
    heat = refs.pop(0)
    current = refs.pop(0)
    start = refs.pop(0)
    half, owned, width = advected[0].shape
    species = slots * owned
    repeats = companion.shape[0] // species
    me = ids[0]
    pick = rims if chunk else middle
    for slot in range(slots):
        first = pl.multiple_of((me ^ slot) * owned, owned)
        current[:, pl.ds(first, owned), :] = advected[slot][...]
        start[:, pl.ds(first, owned), :] = advected[slot][...]
    rate = jax.nn.sigmoid(2.0 * pick(warmth[0]))
    many = pick(counts[...])
    pair = 2

    def substep(s, carry):
        for r in range(0, half, pair):
            now = jnp.concatenate([current[r + p] for p in range(pair)], axis=1)
            pairs = jnp.dot(companion[...], now.astype(jnp.bfloat16), preferred_element_type=F32)
            quad = (pairs.reshape(repeats, species, pair * width) * now[None]).astype(jnp.bfloat16)
            made = jnp.dot(
                stoichiometry[...],
                quad.reshape(repeats * species, pair * width),
                preferred_element_type=F32,
            )
            row_rate = jnp.concatenate([rate[r + p:r + p + 1] for p in range(pair)], axis=1)
            row_many = jnp.concatenate([many[r + p:r + p + 1] for p in range(pair)], axis=1)
            after = now + chem_step * (row_rate * made - now)
            after = jnp.where(s < row_many, after, now)
            for p in range(pair):
                current[r + p] = after[:, p * width:(p + 1) * width]
        return carry

    lax.fori_loop(0, deepest[0], substep, 0)
    weight = jnp.broadcast_to(yields[...], (species, species)).T[:, 0:1]
    for r in range(half):
        heat[r:r + 1] = jnp.sum(weight * (current[r] - start[r]), axis=0, keepdims=True)
    for slot in range(slots):
        first = pl.multiple_of((me ^ slot) * owned, owned)
        outs[slot][...] = current[:, pl.ds(first, owned), :]


def dynamics_kernel(n_lon, n_lat, base, strata, ids, fields, *refs):
    refs = list(refs)
    lon_in = [refs.pop(0) for _ in range(n_lon)]
    lat_in = [refs.pop(0) for _ in range(n_lat)]
    east_out, north_out, warmed = refs
    rows, width = warmed.shape[1:]
    me, lat_even, lon_even = ids[0], ids[1] == 0, ids[2] == 0
    lane = lane_ids((rows, width))
    row = row_ids((rows, width))

    def around(value, place, rim_row):
        low, high = rim_lanes(lon_even, [m[rows:2 * rows] for m in lon_in], place)
        east = jnp.where(lane == width - 1, high, pltpu.roll(value, width - 1, 1))
        west = jnp.where(lane == 0, low, pltpu.roll(value, 1, 1))
        got = [m[pl.ds(rim_row, 1), :] for m in lat_in]
        if len(got) == 1:
            got.append(jnp.zeros_like(got[0]))
        low, high = jnp.where(lat_even, got[1], got[0]), jnp.where(lat_even, got[0], got[1])
        north = jnp.where(row == rows - 1, high, pltpu.roll(value, rows - 1, 0))
        south = jnp.where(row == 0, low, pltpu.roll(value, 1, 0))
        laplace = east + west + north + south - 4.0 * value
        return value + diffusion * laplace, east - west, north - south

    east, _, _ = around(fields[0], 0, base + strata)
    north, _, _ = around(fields[1], 1, base + me)
    heat, zonal, meridional = around(fields[3 + n_lon], 2, base + strata + 1)
    east_out[0] = east - pressure * zonal
    north_out[0] = north - pressure * meridional
    warmed[0] = heat


def result_kernel(slots, ids, *refs):
    refs = list(refs)
    centre = [refs.pop(0) for _ in range(slots)]
    edges = [refs.pop(0) for _ in range(slots)]
    heat_centre, heat_edges, warmed, density, out, temp = refs
    tracers, strata, rows, width = out.shape
    half, quarter = rows // 2, rows // 4
    me = ids[0]

    def one(t, carry):
        for slot in range(slots):
            level = me ^ slot
            mid = centre[slot][pl.ds(t, half, stride=tracers), :]
            rim = edges[slot][pl.ds(t, half, stride=tracers), :]
            out[t, level, quarter:3 * quarter] = mid
            out[t, level, 0:quarter] = rim[:quarter]
            out[t, level, 3 * quarter:rows] = rim[quarter:]
        return carry

    lax.fori_loop(0, tracers, one, 0, unroll=2)
    rim = heat_edges[...]
    heating = jnp.concatenate([rim[:quarter], heat_centre[...], rim[quarter:]], axis=0)
    temp[0] = warmed[0] + heating / density[0]


def local(
    species_amounts,
    zonal_cell_fraction,
    meridional_cell_fraction,
    updraft_cell_fraction,
    warmth_anomaly,
    mass_per_volume,
    chemistry_iterations,
    companion_species,
    stoichiometric_rate,
    heat_yield,
):
    slots = lax.axis_size("group")
    n_lat = min(2, lax.axis_size("lat") - 1)
    n_lon = min(2, lax.axis_size("lon") - 1)
    tracers, strata, rows, width = species_amounts.shape
    half = rows // 2
    base = tracers * strata
    ids = jnp.stack(
        [
            lax.axis_index("group"),
            lax.rem(lax.axis_index("lat"), 2),
            lax.rem(lax.axis_index("lon"), 2),
        ]
    ).astype(jnp.int32)
    deepest = jnp.max(chemistry_iterations).reshape(1)

    lon_out = call(
        pack_columns,
        [struct(2 * rows, width)] * n_lon,
        5,
        touched=4 * species_amounts.size,
    )(ids, species_amounts, zonal_cell_fraction, meridional_cell_fraction, warmth_anomaly)
    lon_in = neighbours(lon_out, "lon")
    fields = jnp.concatenate(
        [zonal_cell_fraction, meridional_cell_fraction, updraft_cell_fraction]
        + [m[rows:][None] for m in lon_in]
        + [warmth_anomaly],
        axis=0,
    )
    payload = fields[:3 + n_lon]
    winds = [fields] + [partner_swap(payload, hop) for hop in range(slots - 1, 0, -1)][::-1]

    def transport(chunk, lat_in):
        out_shape = [struct(half * tracers, width)] * slots
        if not chunk:
            out_shape = out_shape + [struct(base + strata + 4, width)] * n_lat
        got = call(
            functools.partial(transport_kernel, chunk, n_lon, n_lat, slots),
            out_shape,
            2 + slots + n_lon + len(lat_in),
            flops=14 * species_amounts.size // 2,
            touched=8 * species_amounts.size,
            scratch=[pltpu.VMEM((strata, rows, width), F32)],
        )(ids, species_amounts, *winds, *lon_in, *lat_in)
        return got[:slots], got[slots:]

    def swap_slots(blocks):
        swapped = {hop: partner_swap(blocks[hop], hop) for hop in range(slots - 1, 0, -1)}
        return [blocks[0]] + [swapped[hop] for hop in range(1, slots)]

    def chemistry(chunk, advected):
        got = pl.pallas_call(
            functools.partial(chemistry_kernel, chunk, slots),
            out_shape=[struct(half, tracers, width)] * slots + [struct(half, width)],
            in_specs=[SMEM, SMEM] + [VMEM] * (slots + 5),
            out_specs=[VMEM] * (slots + 1),
            scratch_shapes=[pltpu.VMEM((half, slots * tracers, width), F32)] * 2,
            compiler_params=pltpu.CompilerParams(vmem_limit_bytes=40 * 1024 * 1024),
            cost_estimate=pl.CostEstimate(
                flops=4 * half * width * companion_species.size,
                bytes_accessed=8 * species_amounts.size,
                transcendentals=0,
            ),
        )(
            ids,
            deepest,
            *[a.reshape(half, tracers, width) for a in advected],
            warmth_anomaly,
            chemistry_iterations,
            companion_species,
            stoichiometric_rate,
            heat_yield[None],
        )
        return [g.reshape(half * tracers, width) for g in got[:slots]], got[slots]

    adv_mid, lat_out = transport(0, [])
    mid = swap_slots(adv_mid)
    lat_in = neighbours(lat_out, "lat")
    adv_rim, _ = transport(1, lat_in)
    rim = swap_slots(adv_rim)
    east_out, north_out, warmed = call(
        functools.partial(dynamics_kernel, n_lon, n_lat, base, strata),
        [struct(1, rows, width)] * 3,
        2 + n_lon + n_lat,
    )(ids, fields, *lon_in, *lat_in)
    mid, heat_mid = chemistry(0, mid)
    mid = swap_slots(mid)
    rim, heat_rim = chemistry(1, rim)
    rim = swap_slots(rim)
    tracers_out, temp_out = call(
        functools.partial(result_kernel, slots),
        [struct(tracers, strata, rows, width), struct(1, rows, width)],
        1 + 2 * slots + 4,
        touched=8 * species_amounts.size,
    )(ids, *mid, *rim, heat_mid, heat_rim, warmed, mass_per_volume)
    return (tracers_out, east_out, north_out, temp_out)


def solution(mesh):
    return jax.shard_map(
        local,
        mesh=mesh,
        in_specs=(
            P("group", None, "lat", "lon"),
            P("group", "lat", "lon"),
            P("group", "lat", "lon"),
            P("group", "lat", "lon"),
            P("group", "lat", "lon"),
            P("group", "lat", "lon"),
            P("lat", "lon"),
            P(),
            P(),
            P(),
        ),
        out_specs=(
            P("group", None, "lat", "lon"),
            P("group", "lat", "lon"),
            P("group", "lat", "lon"),
            P("group", "lat", "lon"),
        ),
        check_vma=False,
    )
```

time: 235 us -> 52.7 us (0.22)
  the two profiles are of different devices: /device:TPU:0 before, /device:TPU:18 now
where the time goes in v1:
time: 52.7 us; the launch traced here: 52.3 us
  starting transfers between devices  21.2 us (40%)
  Pallas kernels  15.7 us (30%)
  waiting for transfers between devices  10.7 us (20%)
  local copies, waits for them, and re-layouts  3.2 us (6%)
  between operations  0.8 us (2%)
  other arithmetic  0.71 us (1%)
    ppermute x15, starting transfers between devices, partner_swap(): lax.ppermute(block, 'group', [(i, i ^ hop) for i in range(lax.axis_size('...  17.7 us
    ppermute x15, waiting for transfers between devices, partner_swap(): lax.ppermute(block, 'group', [(i, i ^ hop) for i in range(lax.axis_size('...  6.58 us
    pallas_call x2, Pallas kernels, chemistry(): pl.pallas_call(functools.partial(chemistry_kernel, chunk, slots), out_sha...  5.5 us
    pallas_call x2, Pallas kernels, transport(): call(functools.partial(transport_kernel, chunk, n_lon, n_lat, slots), out...  5.19 us
    ppermute x3, waiting for transfers between devices, neighbours(): lax.ppermute(m, axis, pairs)  4.08 us
    ppermute x3, starting transfers between devices, neighbours(): lax.ppermute(m, axis, pairs)  3.51 us
    unnamed x26, local copies, waits for them, and re-layouts  3.2 us
    pallas_call x1, Pallas kernels, local(): call(functools.partial(result_kernel, slots), [struct(tracers, strata, ro...  2.33 us
  transfers between devices with their start and end apart: 18, of which 9 were waited for; matrix products, arithmetic and copies ran while one was open for 1% of the time, Pallas kernels for 18%

profile of v1, /device:TPU:18, one launch (start us, length us, event | category | flops | bytes accessed | tf_op | source)
XLA Modules:
  0.0 52.3 jit_solution(17722945195945803854)
XLA Ops:
  0.7 0.1 pad_add_fusion.ids
  0.7 0.6 %copy-done.4 = f32[1,16,128]{2,1,0:T(8,128)S(1)} copy-done((f32[1,16,128]{2,1,0:T(8,128)S(1)}, f32[1,16,128]{2,1,0:T(8,128)}, u32[]{:S(2)}) %copy-start.4) | copy-done | bytes 8216
  1.3 0.0 copy-done.3
  1.4 0.0 copy-done.2
  1.4 1.2 %copy-done = f32[32,4,16,128]{3,2,1,0:T(8,128)S(1)} copy-done((f32[32,4,16,128]{3,2,1,0:T(8,128)S(1)}, f32[32,4,16,128]{3,2,1,0:T(8,128)}, u32[]{:S(2)}) %copy-start) | copy-done | bytes 1048600
  2.6 1.5 %shard_map.129 = f32[32,128]{1,0:T(8,128)S(1)} custom-call(s32[3]{0:T(128)S(1)} %pad_add_fusion.ids, f32[32,4,16,128]{3,2,1,0:T(8,128)S(1)} %copy-done, f32[1,16,128]{2,1,0:T(8,128)S(1)} %copy-done.2, f32[1,16,128]{2,1,0:T(8,128)S(1)} %copy-done.3, f32[1,16,128]{2,1,0:T(8,128)S(1)} %copy-done.4), custom_call_target="tpu_custom_call" | custom-call | bytes 1048576 | tf_op jit(solution)/shard_map/pallas_call | solution.py:375
  4.1 0.0 collective-permute-start
  4.1 0.0 copy-start.10
  4.1 0.7 %copy-done.10 = f32[1,16,128]{2,1,0:T(8,128)S(1)} copy-done((f32[1,16,128]{2,1,0:T(8,128)S(1)}, f32[1,16,128]{2,1,0:T(8,128)}, u32[]{:S(2)}) %copy-start.10) | copy-done | bytes 8216
  4.8 0.5 collective-permute-done.refs_4_.refs_0_
  5.3 1.5 %collective-permute-start.3 = (f32[4,16,128]{2,1,0:T(8,128)S(1)}, f32[4,16,128]{2,1,0:T(8,128)S(1)}, u32[]{:S(2)}, u32[]{:S(2)}) collective-permute-start(f32[4,16,128]{2,1,0:T(8,128)S(1)} %pad_maximum_fusion), channel_id=1, source_target_pairs={{0,24},{8,16},{16,8},{24,0},{1,25},{9,17},{17,9},{25,1},{2,26},{10... | collective-permute-start | bytes 98312 | tf_op jit(solution)/shard_map/ppermute | solution.py:55
  6.8 0.5 collective-permute-start.2
  7.3 1.5 %collective-permute-start.1 = (f32[4,16,128]{2,1,0:T(8,128)S(1)}, f32[4,16,128]{2,1,0:T(8,128)S(1)}, u32[]{:S(2)}, u32[]{:S(2)}) collective-permute-start(f32[4,16,128]{2,1,0:T(8,128)S(1)} %pad_maximum_fusion), channel_id=1, source_target_pairs={{0,8},{8,0},{16,24},{24,16},{1,9},{9,1},{17,25},{25,17},{2,10},{10... | collective-permute-start | bytes 98312 | tf_op jit(solution)/shard_map/ppermute | solution.py:55
  8.8 1.3 %collective-permute-done.3.refs_3_ = f32[4,16,128]{2,1,0:T(8,128)S(1)} collective-permute-done((f32[4,16,128]{2,1,0:T(8,128)S(1)}, f32[4,16,128]{2,1,0:T(8,128)S(1)}, u32[]{:S(2)}, u32[]{:S(2)}) %collective-permute-start.3) | collective-permute-done | bytes 32800 | tf_op jit(solution)/shard_map/ppermute | solution.py:55
  10.1 0.6 %collective-permute-done.2.refs_2_ = f32[4,16,128]{2,1,0:T(8,128)S(1)} collective-permute-done((f32[4,16,128]{2,1,0:T(8,128)S(1)}, f32[4,16,128]{2,1,0:T(8,128)S(1)}, u32[]{:S(2)}, u32[]{:S(2)}) %collective-permute-start.2) | collective-permute-done | bytes 32800 | tf_op jit(solution)/shard_map/ppermute | solution.py:55
  10.7 0.5 collective-permute-done.1.refs_1_
  11.2 2.8 %shard_map.130 = (f32[256,128]{1,0:T(8,128)S(1)}, f32[256,128]{1,0:T(8,128)S(1)}, f32[256,128]{1,0:T(8,128)S(1)}, f32[256,128]{1,0:T(8,128)S(1)}, f32[136,128]{1,0:T(8,128)S(1)}, /*index=5*/f32[136,128]{1,0:T(8,128)S(1)}) custom-call(s32[3]{0:T(128)S(1)} %pad_add_fusion.ids, f32[32,4,16,128]{3,2,1,0:T(8,128)S(1)} %copy-done, ...), custom_call_target="tpu_custom_call" | custom-call | flops 1835008 | bytes 2097152 | tf_op jit(solution)/shard_map/pallas_call | solution.py:395
  14.0 0.0 copy-start.6
  14.0 1.6 %collective-permute-start.4 = (f32[256,128]{1,0:T(8,128)S(1)}, f32[256,128]{1,0:T(8,128)S(1)}, u32[]{:S(2)}, u32[]{:S(2)}) collective-permute-start(f32[256,128]{1,0:T(8,128)S(1)} %get-tuple-element.30), channel_id=1, source_target_pairs={{0,8},{8,0},{16,24},{24,16},{1,9},{9,1},{17,25},{25,17},{2,10},{10... | collective-permute-start | bytes 393224 | tf_op jit(solution)/shard_map/ppermute | solution.py:55
  15.6 1.5 %collective-permute-start.5 = (f32[256,128]{1,0:T(8,128)S(1)}, f32[256,128]{1,0:T(8,128)S(1)}, u32[]{:S(2)}, u32[]{:S(2)}) collective-permute-start(f32[256,128]{1,0:T(8,128)S(1)} %get-tuple-element.31), channel_id=1, source_target_pairs={{0,16},{8,24},{16,0},{24,8},{1,17},{9,25},{17,1},{25,9},{2,18},{10... | collective-permute-start | bytes 393224 | tf_op jit(solution)/shard_map/ppermute | solution.py:55
  17.1 0.5 collective-permute-start.6
  17.5 1.6 %collective-permute-start.10 = (f32[136,128]{1,0:T(8,128)S(1)}, f32[136,128]{1,0:T(8,128)S(1)}, u32[]{:S(2)}, u32[]{:S(2)}) collective-permute-start(f32[136,128]{1,0:T(8,128)S(1)} %get-tuple-element.37), channel_id=1, source_target_pairs={{0,2},{2,0},{4,6},{6,4},{1,3},{3,1},{5,7},{7,5},{8,10},{10,8},{12,... | collective-permute-start | bytes 208904 | tf_op jit(solution)/shard_map/ppermute | solution.py:49
  19.1 1.9 %collective-permute-start.11 = (f32[136,128]{1,0:T(8,128)S(1)}, f32[136,128]{1,0:T(8,128)S(1)}, u32[]{:S(2)}, u32[]{:S(2)}) collective-permute-start(f32[136,128]{1,0:T(8,128)S(1)} %get-tuple-element.38), channel_id=1, source_target_pairs={{2,4},{4,2},{3,5},{5,3},{10,12},{12,10},{11,13},{13,11},{18,20},{2... | collective-permute-start | bytes 208904 | tf_op jit(solution)/shard_map/ppermute | solution.py:49
  21.0 0.6 %reduce_max.9 = s32[]{:T(128)} reduce(s32[16,128]{1,0:T(8,128)S(1)} %copy-done.6, s32[]{:T(128)} %constant.19.clone.1), dimensions={0,1}, to_apply=%region_0.0 | reduce | flops 2047 | bytes 8200 | tf_op jit(solution)/shard_map/reduce_max | solution.py:373
  21.7 0.2 collective-permute-done.10.refs_5_.refs_1_
  21.8 3.5 %collective-permute-done.11.refs_6_.refs_2_ = f32[136,128]{1,0:T(8,128)S(1)} collective-permute-done((f32[136,128]{1,0:T(8,128)S(1)}, f32[136,128]{1,0:T(8,128)S(1)}, u32[]{:S(2)}, u32[]{:S(2)}) %collective-permute-start.11) | collective-permute-done | bytes 69664 | tf_op jit(solution)/shard_map/ppermute | solution.py:49
  25.3 2.4 %shard_map.132 = (f32[256,128]{1,0:T(8,128)S(1)}, f32[256,128]{1,0:T(8,128)S(1)}, f32[256,128]{1,0:T(8,128)S(1)}, f32[256,128]{1,0:T(8,128)S(1)}) custom-call(s32[3]{0:T(128)S(1)} %pad_add_fusion.ids, f32[32,4,16,128]{3,2,1,0:T(8,128)S(1)} %copy-done.1, f32[5,16,128]{2,1,0:T(8,128)S(1)} %constant_dynamic-update-slice_fusion.refs_0_.fields, ...), custom_call_target="tpu_custom_call" | custom-call | flops 1835008 | bytes 2097152 | tf_op jit(solution)/shard_map/pallas_call | solution.py:395
  27.7 1.6 %collective-permute-start.12 = (f32[256,128]{1,0:T(8,128)S(1)}, f32[256,128]{1,0:T(8,128)S(1)}, u32[]{:S(2)}, u32[]{:S(2)}) collective-permute-start(f32[256,128]{1,0:T(8,128)S(1)} %get-tuple-element.40), channel_id=1, source_target_pairs={{0,8},{8,0},{16,24},{24,16},{1,9},{9,1},{17,25},{25,17},{2,10},{10... | collective-permute-start | bytes 393224 | tf_op jit(solution)/shard_map/ppermute | solution.py:55
  29.3 1.5 %collective-permute-start.13 = (f32[256,128]{1,0:T(8,128)S(1)}, f32[256,128]{1,0:T(8,128)S(1)}, u32[]{:S(2)}, u32[]{:S(2)}) collective-permute-start(f32[256,128]{1,0:T(8,128)S(1)} %get-tuple-element.41), channel_id=1, source_target_pairs={{0,16},{8,24},{16,0},{24,8},{1,17},{9,25},{17,1},{25,9},{2,18},{10... | collective-permute-start | bytes 393224 | tf_op jit(solution)/shard_map/ppermute | solution.py:55
  30.8 0.0 collective-permute-done.4
  30.8 0.5 collective-permute-start.14
  31.3 0.0 collective-permute-done.5
  31.3 0.0 collective-permute-done.6
  31.3 0.6 %copy-done.9 = f32[128]{0:T(128)S(1)} copy-done((f32[128]{0:T(128)S(1)}, f32[128]{0:T(128)}, u32[]{:S(2)}) %copy-start.9) | copy-done | bytes 536
  32.0 2.7 %shard_map.131 = (f32[8,32,128]{2,1,0:T(8,128)S(1)}, f32[8,32,128]{2,1,0:T(8,128)S(1)}, f32[8,32,128]{2,1,0:T(8,128)S(1)}, f32[8,32,128]{2,1,0:T(8,128)S(1)}, f32[8,128]{1,0:T(8,128)S(1)}) custom-call(s32[3]{0:T(128)S(1)} %pad_add_fusion.ids, s32[1]{0:T(128)} %bitcast.3.deepest, f32[8,32,128]{2,1,0:T(8,128)S(1)} %bitcast.29, f32[8,32,128]{2,1,0:T(8,128)S(1)} %bitcast.31, ...), custom_call_target="tpu_custom_call" | custom-call | flops 268435456 | bytes 2097152 | tf_op jit(solution)/shard_map/pallas_call | solution.py:410
  34.7 1.6 %collective-permute-start.7 = (f32[256,128]{1,0:T(8,128)S(1)}, f32[256,128]{1,0:T(8,128)S(1)}, u32[]{:S(2)}, u32[]{:S(2)}) collective-permute-start(f32[256,128]{1,0:T(8,128)S(1)} %bitcast.37), channel_id=1, source_target_pairs={{0,8},{8,0},{16,24},{24,16},{1,9},{9,1},{17,25},{25,17},{2,10},{10... | collective-permute-start | bytes 393224 | tf_op jit(solution)/shard_map/ppermute | solution.py:55
  36.3 1.5 %collective-permute-start.8 = (f32[256,128]{1,0:T(8,128)S(1)}, f32[256,128]{1,0:T(8,128)S(1)}, u32[]{:S(2)}, u32[]{:S(2)}) collective-permute-start(f32[256,128]{1,0:T(8,128)S(1)} %bitcast.30), channel_id=1, source_target_pairs={{0,16},{8,24},{16,0},{24,8},{1,17},{9,25},{17,1},{25,9},{2,18},{10... | collective-permute-start | bytes 393224 | tf_op jit(solution)/shard_map/ppermute | solution.py:55
  37.8 0.5 collective-permute-start.9
  38.3 2.8 %shard_map.133 = (f32[8,32,128]{2,1,0:T(8,128)S(1)}, f32[8,32,128]{2,1,0:T(8,128)S(1)}, f32[8,32,128]{2,1,0:T(8,128)S(1)}, f32[8,32,128]{2,1,0:T(8,128)S(1)}, f32[8,128]{1,0:T(8,128)S(1)}) custom-call(s32[3]{0:T(128)S(1)} %pad_add_fusion.ids, s32[1]{0:T(128)} %bitcast.3.deepest, f32[8,32,128]{2,1,0:T(8,128)S(1)} %bitcast.28, f32[8,32,128]{2,1,0:T(8,128)S(1)} %bitcast.32, ...), custom_call_target="tpu_custom_call" | custom-call | flops 268435456 | bytes 2097152 | tf_op jit(solution)/shard_map/pallas_call | solution.py:410
  41.0 1.6 %collective-permute-start.15 = (f32[256,128]{1,0:T(8,128)S(1)}, f32[256,128]{1,0:T(8,128)S(1)}, u32[]{:S(2)}, u32[]{:S(2)}) collective-permute-start(f32[256,128]{1,0:T(8,128)S(1)} %bitcast.40), channel_id=1, source_target_pairs={{0,8},{8,0},{16,24},{24,16},{1,9},{9,1},{17,25},{25,17},{2,10},{10... | collective-permute-start | bytes 393224 | tf_op jit(solution)/shard_map/ppermute | solution.py:55
  42.6 1.5 %collective-permute-start.16 = (f32[256,128]{1,0:T(8,128)S(1)}, f32[256,128]{1,0:T(8,128)S(1)}, u32[]{:S(2)}, u32[]{:S(2)}) collective-permute-start(f32[256,128]{1,0:T(8,128)S(1)} %bitcast.39), channel_id=1, source_target_pairs={{0,16},{8,24},{16,0},{24,8},{1,17},{9,25},{17,1},{25,9},{2,18},{10... | collective-permute-start | bytes 393224 | tf_op jit(solution)/shard_map/ppermute | solution.py:55
  44.1 0.0 collective-permute-done.7.refs_1_
  44.1 0.5 collective-permute-start.17
  44.6 1.2 %shard_map.134 = (f32[1,16,128]{2,1,0:T(8,128)}, f32[1,16,128]{2,1,0:T(8,128)}, f32[1,16,128]{2,1,0:T(8,128)S(1)}) custom-call(s32[3]{0:T(128)S(1)} %pad_add_fusion.ids, f32[5,16,128]{2,1,0:T(8,128)S(1)} %constant_dynamic-update-slice_fusion.refs_0_.fields, f32[32,128]{1,0:T(8,128)S(1)} %collective-permute-done.refs_4_.refs_0_, ...), custom_call_target="tpu_custom_call" | custom-call | tf_op jit(solution)/shard_map/pallas_call | solution.py:439
  45.8 0.2 collective-permute-done.15.refs_5_
  46.1 1.5 %collective-permute-done.16.refs_6_ = f32[256,128]{1,0:T(8,128)S(1)} collective-permute-done((f32[256,128]{1,0:T(8,128)S(1)}, f32[256,128]{1,0:T(8,128)S(1)}, u32[]{:S(2)}, u32[]{:S(2)}) %collective-permute-start.16) | collective-permute-done | bytes 131104 | tf_op jit(solution)/shard_map/ppermute | solution.py:55
  47.6 2.4 %collective-permute-done.17.refs_7_ = f32[256,128]{1,0:T(8,128)S(1)} collective-permute-done((f32[256,128]{1,0:T(8,128)S(1)}, f32[256,128]{1,0:T(8,128)S(1)}, u32[]{:S(2)}, u32[]{:S(2)}) %collective-permute-start.17) | collective-permute-done | bytes 131104 | tf_op jit(solution)/shard_map/ppermute | solution.py:55
  50.0 2.3 %shard_map.135 = (f32[32,4,16,128]{3,2,1,0:T(8,128)}, f32[1,16,128]{2,1,0:T(8,128)}) custom-call(s32[3]{0:T(128)S(1)} %pad_add_fusion.ids, f32[256,128]{1,0:T(8,128)S(1)} %bitcast.25, f32[256,128]{1,0:T(8,128)S(1)} %collective-permute-done.7.refs_1_, f32[256,128]{1,0:T(8,128)S(1)} %collective-permute-done.8.refs_2_, ...), custom_call_target="tpu_custom_call" | custom-call | bytes 2097152 | tf_op jit(solution)/shard_map/pallas_call | solution.py:448
  (26 shorter events, 0.1 us)
Async XLA Ops:
  0.6 0.7 %copy-start.4 = (f32[1,16,128]{2,1,0:T(8,128)S(1)}, f32[1,16,128]{2,1,0:T(8,128)}, u32[]{:S(2)}) copy-start(f32[1,16,128]{2,1,0:T(8,128)} %refs_4_.3) | copy-start | bytes 24580
  0.6 0.7 %copy-start.3 = (f32[1,16,128]{2,1,0:T(8,128)S(1)}, f32[1,16,128]{2,1,0:T(8,128)}, u32[]{:S(2)}) copy-start(f32[1,16,128]{2,1,0:T(8,128)} %north.1) | copy-start | bytes 24580
  0.7 0.7 %copy-start.2 = (f32[1,16,128]{2,1,0:T(8,128)S(1)}, f32[1,16,128]{2,1,0:T(8,128)}, u32[]{:S(2)}) copy-start(f32[1,16,128]{2,1,0:T(8,128)} %east.1) | copy-start | bytes 24580
  1.4 1.2 %copy-start = (f32[32,4,16,128]{3,2,1,0:T(8,128)S(1)}, f32[32,4,16,128]{3,2,1,0:T(8,128)}, u32[]{:S(2)}) copy-start(f32[32,4,16,128]{3,2,1,0:T(8,128)} %species.5) | copy-start | bytes 3145732
  2.6 22.7 %copy-start.1 = (f32[32,4,16,128]{3,2,1,0:T(8,128)S(1)}, f32[32,4,16,128]{3,2,1,0:T(8,128)}, u32[]{:S(2)}) copy-start(f32[32,4,16,128]{3,2,1,0:T(8,128)} %species.5) | copy-start | bytes 3145732
  4.1 1.2 %collective-permute-start = (f32[32,128]{1,0:T(8,128)S(1)}, f32[32,128]{1,0:T(8,128)S(1)}, u32[]{:S(2)}, u32[]{:S(2)}) collective-permute-start(f32[32,128]{1,0:T(8,128)S(1)} %shard_map.129), channel_id=1, source_target_pairs={{0,1},{1,0},{2,3},{3,2},{4,5},{5,4},{6,7},{7,6},{8,9},{9,8},{10,11... | collective-permute-start | bytes 49160 | tf_op jit(solution)/shard_map/ppermute | solution.py:49
  4.1 0.7 %copy-start.10 = (f32[1,16,128]{2,1,0:T(8,128)S(1)}, f32[1,16,128]{2,1,0:T(8,128)}, u32[]{:S(2)}) copy-start(f32[1,16,128]{2,1,0:T(8,128)} %param.13) | copy-start | bytes 24580
  5.3 4.8 %collective-permute-start.3 = (f32[4,16,128]{2,1,0:T(8,128)S(1)}, f32[4,16,128]{2,1,0:T(8,128)S(1)}, u32[]{:S(2)}, u32[]{:S(2)}) collective-permute-start(f32[4,16,128]{2,1,0:T(8,128)S(1)} %pad_maximum_fusion), channel_id=1, source_target_pairs={{0,24},{8,16},{16,8},{24,0},{1,25},{9,17},{17,9},{25,1},{2,26},{10... | collective-permute-start | bytes 98312 | tf_op jit(solution)/shard_map/ppermute | solution.py:55
  6.8 3.9 %collective-permute-start.2 = (f32[4,16,128]{2,1,0:T(8,128)S(1)}, f32[4,16,128]{2,1,0:T(8,128)S(1)}, u32[]{:S(2)}, u32[]{:S(2)}) collective-permute-start(f32[4,16,128]{2,1,0:T(8,128)S(1)} %pad_maximum_fusion), channel_id=1, source_target_pairs={{0,16},{8,24},{16,0},{24,8},{1,17},{9,25},{17,1},{25,9},{2,18},{10... | collective-permute-start | bytes 98312 | tf_op jit(solution)/shard_map/ppermute | solution.py:55
  7.3 3.9 %collective-permute-start.1 = (f32[4,16,128]{2,1,0:T(8,128)S(1)}, f32[4,16,128]{2,1,0:T(8,128)S(1)}, u32[]{:S(2)}, u32[]{:S(2)}) collective-permute-start(f32[4,16,128]{2,1,0:T(8,128)S(1)} %pad_maximum_fusion), channel_id=1, source_target_pairs={{0,8},{8,0},{16,24},{24,16},{1,9},{9,1},{17,25},{25,17},{2,10},{10... | collective-permute-start | bytes 98312 | tf_op jit(solution)/shard_map/ppermute | solution.py:55
  14.0 7.1 %copy-start.6 = (s32[16,128]{1,0:T(8,128)S(1)}, s32[16,128]{1,0:T(8,128)}, u32[]{:S(2)}) copy-start(s32[16,128]{1,0:T(8,128)} %refs_5_.3) | copy-start | bytes 24580
  14.0 16.8 %collective-permute-start.4 = (f32[256,128]{1,0:T(8,128)S(1)}, f32[256,128]{1,0:T(8,128)S(1)}, u32[]{:S(2)}, u32[]{:S(2)}) collective-permute-start(f32[256,128]{1,0:T(8,128)S(1)} %get-tuple-element.30), channel_id=1, source_target_pairs={{0,8},{8,0},{16,24},{24,16},{1,9},{9,1},{17,25},{25,17},{2,10},{10... | collective-permute-start | bytes 393224 | tf_op jit(solution)/shard_map/ppermute | solution.py:55
  15.6 15.7 %collective-permute-start.5 = (f32[256,128]{1,0:T(8,128)S(1)}, f32[256,128]{1,0:T(8,128)S(1)}, u32[]{:S(2)}, u32[]{:S(2)}) collective-permute-start(f32[256,128]{1,0:T(8,128)S(1)} %get-tuple-element.31), channel_id=1, source_target_pairs={{0,16},{8,24},{16,0},{24,8},{1,17},{9,25},{17,1},{25,9},{2,18},{10... | collective-permute-start | bytes 393224 | tf_op jit(solution)/shard_map/ppermute | solution.py:55
  17.1 14.2 %collective-permute-start.6 = (f32[256,128]{1,0:T(8,128)S(1)}, f32[256,128]{1,0:T(8,128)S(1)}, u32[]{:S(2)}, u32[]{:S(2)}) collective-permute-start(f32[256,128]{1,0:T(8,128)S(1)} %get-tuple-element.32), channel_id=1, source_target_pairs={{0,24},{8,16},{16,8},{24,0},{1,25},{9,17},{17,9},{25,1},{2,26},{10... | collective-permute-start | bytes 393224 | tf_op jit(solution)/shard_map/ppermute | solution.py:55
  17.5 4.3 %collective-permute-start.10 = (f32[136,128]{1,0:T(8,128)S(1)}, f32[136,128]{1,0:T(8,128)S(1)}, u32[]{:S(2)}, u32[]{:S(2)}) collective-permute-start(f32[136,128]{1,0:T(8,128)S(1)} %get-tuple-element.37), channel_id=1, source_target_pairs={{0,2},{2,0},{4,6},{6,4},{1,3},{3,1},{5,7},{7,5},{8,10},{10,8},{12,... | collective-permute-start | bytes 208904 | tf_op jit(solution)/shard_map/ppermute | solution.py:49
  19.1 6.2 %collective-permute-start.11 = (f32[136,128]{1,0:T(8,128)S(1)}, f32[136,128]{1,0:T(8,128)S(1)}, u32[]{:S(2)}, u32[]{:S(2)}) collective-permute-start(f32[136,128]{1,0:T(8,128)S(1)} %get-tuple-element.38), channel_id=1, source_target_pairs={{2,4},{4,2},{3,5},{5,3},{10,12},{12,10},{11,13},{13,11},{18,20},{2... | collective-permute-start | bytes 208904 | tf_op jit(solution)/shard_map/ppermute | solution.py:49
  21.7 9.6 %copy-start.7 = (bf16[512,128]{1,0:T(8,128)(2,1)S(1)}, bf16[512,128]{1,0:T(8,128)(2,1)}, u32[]{:S(2)}) copy-start(bf16[512,128]{1,0:T(8,128)(2,1)} %refs_6_.3) | copy-start | bytes 393220
  21.7 9.6 %copy-start.8 = (bf16[128,512]{1,0:T(8,128)(2,1)S(1)}, bf16[128,512]{1,0:T(8,128)(2,1)}, u32[]{:S(2)}) copy-start(bf16[128,512]{1,0:T(8,128)(2,1)} %refs_7_.3) | copy-start | bytes 393220
  27.7 10.1 %collective-permute-start.12 = (f32[256,128]{1,0:T(8,128)S(1)}, f32[256,128]{1,0:T(8,128)S(1)}, u32[]{:S(2)}, u32[]{:S(2)}) collective-permute-start(f32[256,128]{1,0:T(8,128)S(1)} %get-tuple-element.40), channel_id=1, source_target_pairs={{0,8},{8,0},{16,24},{24,16},{1,9},{9,1},{17,25},{25,17},{2,10},{10... | collective-permute-start | bytes 393224 | tf_op jit(solution)/shard_map/ppermute | solution.py:55
  29.3 9.0 %collective-permute-start.13 = (f32[256,128]{1,0:T(8,128)S(1)}, f32[256,128]{1,0:T(8,128)S(1)}, u32[]{:S(2)}, u32[]{:S(2)}) collective-permute-start(f32[256,128]{1,0:T(8,128)S(1)} %get-tuple-element.41), channel_id=1, source_target_pairs={{0,16},{8,24},{16,0},{24,8},{1,17},{9,25},{17,1},{25,9},{2,18},{10... | collective-permute-start | bytes 393224 | tf_op jit(solution)/shard_map/ppermute | solution.py:55
  30.8 7.4 %collective-permute-start.14 = (f32[256,128]{1,0:T(8,128)S(1)}, f32[256,128]{1,0:T(8,128)S(1)}, u32[]{:S(2)}, u32[]{:S(2)}) collective-permute-start(f32[256,128]{1,0:T(8,128)S(1)} %get-tuple-element.42), channel_id=1, source_target_pairs={{0,24},{8,16},{16,8},{24,0},{1,25},{9,17},{17,9},{25,1},{2,26},{10... | collective-permute-start | bytes 393224 | tf_op jit(solution)/shard_map/ppermute | solution.py:55
  31.3 0.7 %copy-start.9 = (f32[128]{0:T(128)S(1)}, f32[128]{0:T(128)}, u32[]{:S(2)}) copy-start(f32[128]{0:T(128)} %param.19) | copy-start | bytes 1540
  34.7 9.4 %collective-permute-start.7 = (f32[256,128]{1,0:T(8,128)S(1)}, f32[256,128]{1,0:T(8,128)S(1)}, u32[]{:S(2)}, u32[]{:S(2)}) collective-permute-start(f32[256,128]{1,0:T(8,128)S(1)} %bitcast.37), channel_id=1, source_target_pairs={{0,8},{8,0},{16,24},{24,16},{1,9},{9,1},{17,25},{25,17},{2,10},{10... | collective-permute-start | bytes 393224 | tf_op jit(solution)/shard_map/ppermute | solution.py:55
  36.3 9.6 %collective-permute-start.8 = (f32[256,128]{1,0:T(8,128)S(1)}, f32[256,128]{1,0:T(8,128)S(1)}, u32[]{:S(2)}, u32[]{:S(2)}) collective-permute-start(f32[256,128]{1,0:T(8,128)S(1)} %bitcast.30), channel_id=1, source_target_pairs={{0,16},{8,24},{16,0},{24,8},{1,17},{9,25},{17,1},{25,9},{2,18},{10... | collective-permute-start | bytes 393224 | tf_op jit(solution)/shard_map/ppermute | solution.py:55
  37.8 8.0 %collective-permute-start.9 = (f32[256,128]{1,0:T(8,128)S(1)}, f32[256,128]{1,0:T(8,128)S(1)}, u32[]{:S(2)}, u32[]{:S(2)}) collective-permute-start(f32[256,128]{1,0:T(8,128)S(1)} %bitcast.27), channel_id=1, source_target_pairs={{0,24},{8,16},{16,8},{24,0},{1,25},{9,17},{17,9},{25,1},{2,26},{10... | collective-permute-start | bytes 393224 | tf_op jit(solution)/shard_map/ppermute | solution.py:55
  41.0 5.0 %collective-permute-start.15 = (f32[256,128]{1,0:T(8,128)S(1)}, f32[256,128]{1,0:T(8,128)S(1)}, u32[]{:S(2)}, u32[]{:S(2)}) collective-permute-start(f32[256,128]{1,0:T(8,128)S(1)} %bitcast.40), channel_id=1, source_target_pairs={{0,8},{8,0},{16,24},{24,16},{1,9},{9,1},{17,25},{25,17},{2,10},{10... | collective-permute-start | bytes 393224 | tf_op jit(solution)/shard_map/ppermute | solution.py:55
  42.6 5.0 %collective-permute-start.16 = (f32[256,128]{1,0:T(8,128)S(1)}, f32[256,128]{1,0:T(8,128)S(1)}, u32[]{:S(2)}, u32[]{:S(2)}) collective-permute-start(f32[256,128]{1,0:T(8,128)S(1)} %bitcast.39), channel_id=1, source_target_pairs={{0,16},{8,24},{16,0},{24,8},{1,17},{9,25},{17,1},{25,9},{2,18},{10... | collective-permute-start | bytes 393224 | tf_op jit(solution)/shard_map/ppermute | solution.py:55
  44.1 5.9 %collective-permute-start.17 = (f32[256,128]{1,0:T(8,128)S(1)}, f32[256,128]{1,0:T(8,128)S(1)}, u32[]{:S(2)}, u32[]{:S(2)}) collective-permute-start(f32[256,128]{1,0:T(8,128)S(1)} %bitcast.38), channel_id=1, source_target_pairs={{0,24},{8,16},{16,8},{24,0},{1,25},{9,17},{17,9},{25,1},{2,26},{10... | collective-permute-start | bytes 393224 | tf_op jit(solution)/shard_map/ppermute | solution.py:55
  45.8 4.2 %copy-start.5 = (f32[1,16,128]{2,1,0:T(8,128)S(1)}, f32[1,16,128]{2,1,0:T(8,128)}, u32[]{:S(2)}) copy-start(f32[1,16,128]{2,1,0:T(8,128)} %refs_11_.1) | copy-start | bytes 24580

commit v2 on v1

v2 whole, which is shorter than its diff:
```python
import functools

import jax
import jax.numpy as jnp
from jax import lax
from jax.experimental import pallas as pl
from jax.experimental.pallas import tpu as pltpu
from jax.sharding import PartitionSpec as P

diffusion = 0.1
pressure = 0.05
chem_step = 0.2

VMEM = pl.BlockSpec(memory_space=pltpu.VMEM)
SMEM = pl.BlockSpec(memory_space=pltpu.SMEM)
ANY = pl.BlockSpec(memory_space=pl.ANY)
HBM = pl.BlockSpec(memory_space=pltpu.HBM)
LIMIT = 40 * 1024 * 1024
F32 = jnp.float32


def struct(*shape, dtype=F32):
    return jax.ShapeDtypeStruct(shape, dtype)


def call(kernel, out_shape, n_in, flops=0, touched=0, scratch=()):
    return pl.pallas_call(
        kernel,
        out_shape=out_shape,
        in_specs=[SMEM] + [VMEM] * (n_in - 1),
        out_specs=jax.tree.map(lambda _: VMEM, out_shape),
        scratch_shapes=list(scratch),
        compiler_params=pltpu.CompilerParams(vmem_limit_bytes=LIMIT),
        cost_estimate=pl.CostEstimate(flops=flops, bytes_accessed=touched, transcendentals=0),
    )


def even_pairs(count):
    return [(i, i ^ 1) for i in range(count) if (i ^ 1) < count]


def odd_pairs(count):
    pairs = []
    for i in range(1, count - 1, 2):
        pairs += [(i, i + 1), (i + 1, i)]
    return pairs


def neighbours(messages, axis):
    count = lax.axis_size(axis)
    return [
        lax.ppermute(m, axis, pairs)
        for m, pairs in zip(messages, (even_pairs(count), odd_pairs(count)))
    ]


def partner_swap(block, hop):
    return lax.ppermute(block, "group", [(i, i ^ hop) for i in range(lax.axis_size("group"))])


def lane_ids(shape):
    return lax.broadcasted_iota(jnp.int32, shape, len(shape) - 1)


def row_ids(shape):
    return lax.broadcasted_iota(jnp.int32, shape, len(shape) - 2)


def pack_kernel(n_lon, n_lat, ids, species_hbm, *refs):
    *outs, species, sem = refs
    copy = pltpu.make_async_copy(species_hbm, species, sem)
    copy.start()
    tracers, strata, rows, width = species.shape
    lane = lane_ids((rows, width))
    flat = species.reshape(tracers * strata * rows, width)
    base = tracers * strata
    copy.wait()
    for at, message in enumerate(outs[n_lon:n_lon + n_lat]):
        edge = jnp.where(ids[1] == at, rows - 1, 0)
        message[...] = flat[pl.ds(edge, base, stride=rows), :]
    for at, message in enumerate(outs[:n_lon]):
        edge = jnp.where(ids[2] == at, width - 1, 0)

        def one(t, acc):
            for k in range(strata):
                place = t * strata + k
                turned = pltpu.roll(species[t, k], lax.rem(place - edge + width, width), 1)
                acc = jnp.where(lane == place, turned, acc)
            return acc

        message[...] = lax.fori_loop(
            0, tracers, one, jnp.zeros((rows, width), F32), unroll=tracers
        )


def both_sides(even, got):
    if len(got) == 1:
        got = [got[0], jnp.zeros_like(got[0])]
    return jnp.where(even, got[1], got[0]), jnp.where(even, got[0], got[1])


def beside(value, even, got):
    width = value.shape[1]
    lane = lane_ids(value.shape)
    low, high = both_sides(even, got)
    west = pltpu.roll(jnp.where(lane == width - 1, low, value), 1, 1)
    east = pltpu.roll(jnp.where(lane == 0, high, value), width - 1, 1)
    return west, east


def beyond(value, even, got):
    rows = value.shape[0]
    row = row_ids(value.shape)
    low, high = both_sides(even, got)
    south = jnp.where(row == 0, low, pltpu.roll(value, 1, 0))
    north = jnp.where(row == rows - 1, high, pltpu.roll(value, rows - 1, 0))
    return south, north


def middle(value):
    quarter = value.shape[0] // 4
    return value[quarter:3 * quarter]


def ends(value):
    quarter = value.shape[0] // 4
    return jnp.concatenate([value[:quarter], value[3 * quarter:]], axis=0)


def faces(low, high):
    wind = 0.5 * (low + high)
    return jnp.maximum(wind, 0.0), jnp.minimum(wind, 0.0)


def transport_kernel(chunk, n_lon, n_lat, slots, ids, species, *refs):
    refs = list(refs)
    winds = [refs.pop(0) for _ in range(slots)]
    lon_in = [refs.pop(0) for _ in range(n_lon)]
    lat_in = [refs.pop(0) for _ in range(n_lat)] if chunk else []
    if chunk:
        counts, yields = refs.pop(0), refs.pop(0)
    outs = [refs.pop(0) for _ in range(slots)]
    if chunk:
        weight, deepest = refs.pop(0), refs.pop(0)
        weight[...] = jnp.broadcast_to(yields[...], weight.shape[::-1]).T
        deepest[0] = jnp.max(counts[...])
    upward = refs.pop(0)
    tracers, strata, rows, width = species.shape
    half = rows // 2
    quarter = rows // 4
    base = tracers * strata
    me, lat_even, lon_even = ids[0], ids[1] == 0, ids[2] == 0
    pick = ends if chunk else middle
    lane = lane_ids((half, width))
    row = row_ids((half, width))
    for slot in range(slots):
        upward[me ^ slot] = winds[slot][2 * rows:3 * rows]

    coefficients = []
    for slot in range(slots):
        level = me ^ slot
        east = winds[slot][0:rows]
        at = (1 + slot) * rows
        east_last, east_next = beside(east, lon_even, [m[at:at + rows] for m in lon_in])
        north = winds[slot][rows:2 * rows]
        rim = [m[base + slot:base + slot + 1] for m in lat_in] or [jnp.zeros((1, width), F32)]
        north_last, north_next = beyond(north, lat_even, rim)
        up = upward[level]
        above = upward[jnp.minimum(level + 1, strata - 1)]
        below = upward[jnp.maximum(level - 1, 0)]
        has_above = jnp.where(level < strata - 1, 1.0, 0.0)
        has_below = jnp.where(level > 0, 1.0, 0.0)
        east_out, east_in = faces(east, east_next)
        west_in, west_out = faces(east_last, east)
        north_out, north_in = faces(north, north_next)
        south_in, south_out = faces(north_last, north)
        up_out, up_in = [has_above * f for f in faces(up, above)]
        down_in, down_out = [has_below * f for f in faces(below, up)]
        stay = 1.0 - (
            (east_out - west_out) + (north_out - south_out) + (up_out - down_out)
        )
        stay, east_in, west_in, north_in, south_in, up_in, down_in = [
            pick(f) for f in (stay, -east_in, west_in, -north_in, south_in, -up_in, down_in)
        ]
        if n_lon < 2:
            east_in = jnp.where((lane == width - 1) & (ids[2] == 1), 0.0, east_in)
            west_in = jnp.where((lane == 0) & (ids[2] == 0), 0.0, west_in)
        coefficients.append((stay, east_in, west_in, north_in, south_in, up_in, down_in))

    columns = [pick(m[0:rows]) for m in lon_in]
    if n_lon == 2:
        columns = both_sides(lon_even, columns)
    edge = jnp.where(lon_even, width - 1, 0)

    def one(t, carry):
        for slot in range(slots):
            level = me ^ slot
            stay, east_in, west_in, north_in, south_in, up_in, down_in = coefficients[slot]
            place = t * strata + level
            if n_lon == 2:
                low = pltpu.roll(columns[0], lax.rem(width - place, width), 1)
                high = pltpu.roll(columns[1], width - 1 - place, 1)
            else:
                low = high = pltpu.roll(columns[0], lax.rem(width + edge - place, width), 1)
            above = jnp.minimum(level + 1, strata - 1)
            below = jnp.maximum(level - 1, 0)
            if chunk:
                first, last = species[t, level, 0:half], species[t, level, half:rows]
                here = jnp.where(row < quarter, first, last)
                low_row, high_row = both_sides(lat_even, [m[pl.ds(place, 1), :] for m in lat_in])
                south = pltpu.roll(jnp.where(row < quarter - 1, first, last), 1, 0)
                south = jnp.where(row == 0, low_row, south)
                north = pltpu.roll(jnp.where(row < quarter + 1, first, last), half - 1, 0)
                north = jnp.where(row == half - 1, high_row, north)
                up = jnp.where(
                    row < quarter, species[t, above, 0:half], species[t, above, half:rows]
                )
                down = jnp.where(
                    row < quarter, species[t, below, 0:half], species[t, below, half:rows]
                )
            else:
                here = species[t, level, quarter:3 * quarter]
                south = species[t, level, quarter - 1:3 * quarter - 1]
                north = species[t, level, quarter + 1:3 * quarter + 1]
                up = species[t, above, quarter:3 * quarter]
                down = species[t, below, quarter:3 * quarter]
            east = jnp.where(lane == width - 1, high, pltpu.roll(here, width - 1, 1))
            west = jnp.where(lane == 0, low, pltpu.roll(here, 1, 1))
            value = (
                (stay * here + east_in * east)
                + (west_in * west + north_in * north)
                + (south_in * south + up_in * up)
                + down_in * down
            )
            outs[slot][pl.ds(t, half, stride=tracers), :] = value
        return carry

    lax.fori_loop(0, tracers, one, 0, unroll=8)


def chemistry_kernel(chunk, slots, ids, deepest, *refs):
    refs = list(refs)
    advected = [refs.pop(0) for _ in range(slots)]
    warmth, counts, companion, stoichiometry, weight = [refs.pop(0) for _ in range(5)]
    outs = [refs.pop(0) for _ in range(slots)]
    heat, current = refs
    half, owned, width = advected[0].shape
    species = slots * owned
    repeats = companion.shape[0] // species
    pick = ends if chunk else middle
    place = [pl.ds(pl.multiple_of((ids[0] ^ slot) * owned, owned), owned) for slot in range(slots)]
    for slot in range(slots):
        current[:, place[slot], :] = advected[slot][...]
    line = lambda field: jnp.concatenate([field[r:r + 1] for r in range(half)], axis=1)
    rate = line(jax.nn.sigmoid(2.0 * pick(warmth[...])))
    many = line(pick(counts[...]))

    def substep(s, carry):
        now = jnp.concatenate([current[r] for r in range(half)], axis=1)
        pairs = jnp.dot(companion[...], now.astype(jnp.bfloat16), preferred_element_type=F32)
        quad = (pairs.reshape(repeats, species, half * width) * now[None]).astype(jnp.bfloat16)
        made = jnp.dot(
            stoichiometry[...],
            quad.reshape(repeats * species, half * width),
            preferred_element_type=F32,
        )
        after = now + chem_step * (rate * made - now)
        after = jnp.where(s < many, after, now)
        for r in range(half):
            current[r] = after[:, r * width:(r + 1) * width]
        return carry

    lax.fori_loop(0, deepest[0], substep, 0)
    total = None
    for slot in range(slots):
        final = current[:, place[slot], :]
        for r in range(half):
            outs[slot][pl.ds(r, owned, stride=half), :] = final[r]
        part = jnp.sum(weight[place[slot], :][None] * (final - advected[slot][...]), axis=1)
        total = part if total is None else total + part
    heat[...] = total


def dynamics_kernel(n_lon, n_lat, base, slots, ids, east, north, warmth, density, *refs):
    refs = list(refs)
    lon_in = [refs.pop(0) for _ in range(n_lon)]
    lat_in = [refs.pop(0) for _ in range(n_lat)]
    heat_middle, heat_ends, east_out, north_out, temp_out = refs
    rows = temp_out.shape[1]
    quarter = rows // 4
    lat_even, lon_even = ids[1] == 0, ids[2] == 0

    def around(value, tile, line):
        west, east = beside(value, lon_even, [m[tile * rows:(tile + 1) * rows] for m in lon_in])
        south, north = beyond(value, lat_even, [m[base + line:base + line + 1] for m in lat_in])
        laplace = east + west + north + south - 4.0 * value
        return value + diffusion * laplace, east - west, north - south

    new_east, _, _ = around(east[0], 1, slots)
    new_north, _, _ = around(north[0], 1 + slots, 0)
    warmed, zonal, meridional = around(warmth[0], 2 + slots, slots + 1)
    heating = jnp.concatenate(
        [heat_ends[:quarter], heat_middle[...], heat_ends[quarter:]], axis=0
    )
    east_out[0] = new_east - pressure * zonal
    north_out[0] = new_north - pressure * meridional
    temp_out[0] = warmed + heating / density[0]


def place_kernel(chunk, slots, ids, *refs):
    got, out, sems = refs[:slots], refs[-2], refs[-1]
    rows = out.shape[2]
    quarter = rows // 4
    starts = (0, 3 * quarter) if chunk else (quarter, 2 * quarter)
    copies = [
        pltpu.make_async_copy(
            got[slot].at[:, part * quarter:(part + 1) * quarter, :],
            out.at[:, ids[0] ^ slot, start:start + quarter, :],
            sems.at[slot, part],
        )
        for slot in range(slots)
        for part, start in enumerate(starts)
    ]
    for copy in copies:
        copy.start()
    for copy in copies:
        copy.wait()


def local(
    species_amounts,
    zonal_cell_fraction,
    meridional_cell_fraction,
    updraft_cell_fraction,
    warmth_anomaly,
    mass_per_volume,
    chemistry_iterations,
    companion_species,
    stoichiometric_rate,
    heat_yield,
):
    slots = lax.axis_size("group")
    n_lat = min(2, lax.axis_size("lat") - 1)
    n_lon = min(2, lax.axis_size("lon") - 1)
    tracers, strata, rows, width = species_amounts.shape
    half = rows // 2
    base = tracers * strata
    ids = jnp.stack(
        [
            lax.axis_index("group"),
            lax.rem(lax.axis_index("lat"), 2),
            lax.rem(lax.axis_index("lon"), 2),
        ]
    ).astype(jnp.int32)

    payload = jnp.concatenate(
        [
            zonal_cell_fraction[0],
            meridional_cell_fraction[0],
            updraft_cell_fraction[0],
            warmth_anomaly[0],
        ],
        axis=0,
    )
    payload = lax.optimization_barrier(payload)
    east, north, warmth = payload[:rows], payload[rows:2 * rows], payload[3 * rows:]
    gathered = {hop: partner_swap(payload, hop) for hop in range(slots - 1, 0, -1)}
    winds = [payload] + [gathered[hop] for hop in range(1, slots)]

    packed = pl.pallas_call(
        functools.partial(pack_kernel, n_lon, n_lat),
        out_shape=[struct(rows, width)] * n_lon
        + [struct(base, width)] * n_lat
        + [struct(tracers, strata, rows, width)],
        in_specs=[SMEM, HBM],
        out_specs=[VMEM] * (n_lon + n_lat + 1),
        scratch_shapes=[pltpu.SemaphoreType.DMA],
        compiler_params=pltpu.CompilerParams(vmem_limit_bytes=52 * 1024 * 1024),
        cost_estimate=pl.CostEstimate(
            flops=species_amounts.size, bytes_accessed=4 * species_amounts.size, transcendentals=0
        ),
    )(ids, species_amounts)
    species = packed[n_lon + n_lat]
    lon_out = [
        jnp.concatenate([m] + [w[:rows] for w in winds] + [north, warmth], axis=0)
        for m in packed[:n_lon]
    ]
    lat_out = []
    for at, m in enumerate(packed[n_lon:n_lon + n_lat]):
        top = ids[1] == at
        lines = [w[rows:2 * rows] for w in winds] + [east, warmth]
        lines = jnp.concatenate([jnp.where(top, f[rows - 1:], f[:1]) for f in lines], axis=0)
        lines = jnp.pad(lines, ((0, -lines.shape[0] % 8), (0, 0)))
        lat_out.append(jnp.concatenate([m, lines], axis=0))
    lon_in = neighbours(lon_out, "lon")
    lat_out, lon_in = lax.optimization_barrier((lat_out, lon_in))
    lat_in = neighbours(lat_out, "lat")

    def transport(chunk, lat_in=()):
        more = [*lat_in, chemistry_iterations, heat_yield[None]] if chunk else []
        return pl.pallas_call(
            functools.partial(transport_kernel, chunk, n_lon, n_lat, slots),
            out_shape=[struct(half * tracers, width)] * slots
            + [struct(slots * tracers, width), struct(1, dtype=jnp.int32)] * chunk,
            in_specs=[SMEM] + [VMEM] * (1 + slots + n_lon + len(more)),
            out_specs=[VMEM] * slots + [VMEM, SMEM] * chunk,
            scratch_shapes=[pltpu.VMEM((strata, rows, width), F32)],
            compiler_params=pltpu.CompilerParams(vmem_limit_bytes=LIMIT),
            cost_estimate=pl.CostEstimate(
                flops=7 * species_amounts.size if chunk else 1,
                bytes_accessed=256 * species_amounts.size if chunk else 1,
                transcendentals=0,
            ),
        )(ids, species, *winds, *lon_in, *more)

    def swap_slots(blocks):
        swapped = {hop: partner_swap(blocks[hop], hop) for hop in range(slots - 1, 0, -1)}
        return [blocks[0]] + [swapped[hop] for hop in range(1, slots)]

    def chemistry(chunk, advected):
        got = pl.pallas_call(
            functools.partial(chemistry_kernel, chunk, slots),
            out_shape=[struct(tracers * half, width)] * slots + [struct(half, width)],
            in_specs=[SMEM, SMEM] + [VMEM] * (slots + 5),
            out_specs=[VMEM] * (slots + 1),
            scratch_shapes=[pltpu.VMEM((half, slots * tracers, width), F32)],
            compiler_params=pltpu.CompilerParams(vmem_limit_bytes=LIMIT),
            cost_estimate=pl.CostEstimate(
                flops=4 * half * width * companion_species.size,
                bytes_accessed=8 * species_amounts.size,
                transcendentals=0,
            ),
        )(
            ids,
            deepest,
            *[a.reshape(half, tracers, width) for a in advected],
            warmth,
            chemistry_iterations,
            companion_species,
            stoichiometric_rate,
            weight,
        )
        return got[:slots], got[slots]

    def put(chunk, blocks, partial):
        return pl.pallas_call(
            functools.partial(place_kernel, chunk, slots),
            out_shape=struct(tracers, strata, rows, width),
            in_specs=[SMEM] + [VMEM] * slots + [ANY] * len(partial),
            out_specs=ANY,
            scratch_shapes=[pltpu.SemaphoreType.DMA((slots, 2))],
            input_output_aliases={1 + slots: 0} if partial else {},
            compiler_params=pltpu.CompilerParams(vmem_limit_bytes=LIMIT),
            cost_estimate=pl.CostEstimate(
                flops=0, bytes_accessed=4 * species_amounts.size, transcendentals=0
            ),
        )(ids, *[b.reshape(tracers, half, width) for b in blocks], *partial)

    mid = list(transport(0))
    mid[1], mid[2], lat_in = lax.optimization_barrier((mid[1], mid[2], lat_in))
    mid = swap_slots(mid)
    *end, weight, deepest = transport(1, lat_in)
    end = swap_slots(end)
    mid, heat_mid = chemistry(0, mid)
    mid = swap_slots(mid)
    end, heat_end = chemistry(1, end)
    end = swap_slots(end)
    east_out, north_out, temp_out = call(
        functools.partial(dynamics_kernel, n_lon, n_lat, base, slots),
        [struct(1, rows, width)] * 3,
        7 + n_lon + n_lat,
    )(
        ids,
        zonal_cell_fraction,
        meridional_cell_fraction,
        warmth_anomaly,
        mass_per_volume,
        *lon_in,
        *lat_in,
        heat_mid,
        heat_end,
    )
    tracers_out = put(1, end, [put(0, mid, [])])
    return (tracers_out, east_out, north_out, temp_out)


def solution(mesh):
    return jax.shard_map(
        local,
        mesh=mesh,
        in_specs=(
            P("group", None, "lat", "lon"),
            P("group", "lat", "lon"),
            P("group", "lat", "lon"),
            P("group", "lat", "lon"),
            P("group", "lat", "lon"),
            P("group", "lat", "lon"),
            P("lat", "lon"),
            P(),
            P(),
            P(),
        ),
        out_specs=(
            P("group", None, "lat", "lon"),
            P("group", "lat", "lon"),
            P("group", "lat", "lon"),
            P("group", "lat", "lon"),
        ),
        check_vma=False,
    )
```

time: 52.7 us -> 44 us (0.83)
  the two profiles are of different devices: /device:TPU:18 before, /device:TPU:8 now
where the time goes in v2:
time: 44 us; the launch traced here: 43.7 us
  starting transfers between devices  22.9 us (52%)
  Pallas kernels  14.1 us (32%)
  waiting for transfers between devices  4.95 us (11%)
  other arithmetic  0.87 us (2%)
  between operations  0.85 us (2%)
    ppermute x15, starting transfers between devices, partner_swap(): lax.ppermute(block, 'group', [(i, i ^ hop) for i in range(lax.axis_size('...  17.8 us
    ppermute x3, starting transfers between devices, neighbours(): lax.ppermute(m, axis, pairs)  5.12 us
    pallas_call x2, Pallas kernels, chemistry(): pl.pallas_call(functools.partial(chemistry_kernel, chunk, slots), out_sha...  3.98 us
    pallas_call x2, Pallas kernels, transport(): pl.pallas_call(functools.partial(transport_kernel, chunk, n_lon, n_lat, s...  3.89 us
    ppermute x15, waiting for transfers between devices, partner_swap(): lax.ppermute(block, 'group', [(i, i ^ hop) for i in range(lax.axis_size('...  3.83 us
    pallas_call x2, Pallas kernels, put(): pl.pallas_call(functools.partial(place_kernel, chunk, slots), out_shape=s...  2.78 us
    pallas_call x1, Pallas kernels, local(): pl.pallas_call(functools.partial(pack_kernel, n_lon, n_lat), out_shape=[s...  2.19 us
    pallas_call x1, Pallas kernels, local(): call(functools.partial(dynamics_kernel, n_lon, n_lat, base, slots), [stru...  1.24 us
  transfers between devices with their start and end apart: 18, of which 6 were waited for; matrix products, arithmetic and copies ran while one was open for 0% of the time, Pallas kernels for 29%

profile of v2, /device:TPU:8, one launch (start us, length us, event | category | flops | bytes accessed | tf_op | source)
XLA Modules:
  0.0 43.7 jit_solution(17615414917218292248)
XLA Ops:
  0.6 0.8 %pad_maximum_fusion.refs_0_ = f32[64,128]{1,0:T(8,128)S(1)} fusion(f32[16,128]{1,0:T(8,128)} %bitcast.32, f32[16,128]{1,0:T(8,128)} %bitcast.44, f32[16,128]{1,0:T(8,128)} %bitcast.33, f32[16,128]{1,0:T(8,128)} %bitcast.34), kind=kLoop, calls=%fused_computation.3 | loop fusion | flops 24576 | bytes 65536 | tf_op jit(solution)/shard_map/concatenate | solution.py:356
  1.4 2.4 %collective-permute-start.2 = (f32[64,128]{1,0:T(8,128)S(1)}, f32[64,128]{1,0:T(8,128)S(1)}, u32[]{:S(2)}, u32[]{:S(2)}) collective-permute-start(f32[64,128]{1,0:T(8,128)S(1)} %pad_maximum_fusion.refs_0_), channel_id=1, source_target_pairs={{0,24},{8,16},{16,8},{24,0},{1,25},{9,17},{17,9},{25,1},{2,26},{10... | collective-permute-start | bytes 98312 | tf_op jit(solution)/shard_map/ppermute | solution.py:58
  3.8 0.5 %collective-permute-start.1 = (f32[64,128]{1,0:T(8,128)S(1)}, f32[64,128]{1,0:T(8,128)S(1)}, u32[]{:S(2)}, u32[]{:S(2)}) collective-permute-start(f32[64,128]{1,0:T(8,128)S(1)} %pad_maximum_fusion.refs_0_), channel_id=1, source_target_pairs={{0,16},{8,24},{16,0},{24,8},{1,17},{9,25},{17,1},{25,9},{2,18},{10... | collective-permute-start | bytes 98312 | tf_op jit(solution)/shard_map/ppermute | solution.py:58
  4.3 0.5 %collective-permute-start = (f32[64,128]{1,0:T(8,128)S(1)}, f32[64,128]{1,0:T(8,128)S(1)}, u32[]{:S(2)}, u32[]{:S(2)}) collective-permute-start(f32[64,128]{1,0:T(8,128)S(1)} %pad_maximum_fusion.refs_0_), channel_id=1, source_target_pairs={{0,8},{8,0},{16,24},{24,16},{1,9},{9,1},{17,25},{25,17},{2,10},{10... | collective-permute-start | bytes 98312 | tf_op jit(solution)/shard_map/ppermute | solution.py:58
  4.9 0.1 pad_add_fusion.ids
  4.9 2.2 %shard_map.129 = (f32[16,128]{1,0:T(8,128)S(1)}, f32[128,128]{1,0:T(8,128)S(1)}, f32[128,128]{1,0:T(8,128)S(1)}, f32[32,4,16,128]{3,2,1,0:T(8,128)S(1)}) custom-call(s32[3]{0:T(128)S(1)} %pad_add_fusion.ids, f32[32,4,16,128]{3,2,1,0:T(8,128)} %species_hbm.1), custom_call_target="tpu_custom_call" | custom-call | flops 262144 | bytes 1048576 | tf_op jit(solution)/shard_map/pallas_call | solution.py:370
  7.2 1.1 %collective-permute-done.refs_1_ = f32[64,128]{1,0:T(8,128)S(1)} collective-permute-done((f32[64,128]{1,0:T(8,128)S(1)}, f32[64,128]{1,0:T(8,128)S(1)}, u32[]{:S(2)}, u32[]{:S(2)}) %collective-permute-start) | collective-permute-done | bytes 32800 | tf_op jit(solution)/shard_map/ppermute | solution.py:58
  8.3 0.0 collective-permute-done.1.refs_2_
  8.3 0.0 collective-permute-done.2.refs_3_
  8.3 0.1 collective-permute-start.3
  8.5 1.1 %collective-permute-done.3.refs_4_.refs_0_ = f32[112,128]{1,0:T(8,128)S(1)} collective-permute-done((f32[112,128]{1,0:T(8,128)S(1)}, f32[112,128]{1,0:T(8,128)S(1)}, u32[]{:S(2)}, u32[]{:S(2)}) %collective-permute-start.3) | collective-permute-done | bytes 57376 | tf_op jit(solution)/shard_map/ppermute | solution.py:52
  9.6 0.4 %collective-permute-start.4 = (f32[136,128]{1,0:T(8,128)S(1)}, f32[136,128]{1,0:T(8,128)S(1)}, u32[]{:S(2)}, u32[]{:S(2)}) collective-permute-start(f32[136,128]{1,0:T(8,128)S(1)} %get-tuple-element.45), channel_id=1, source_target_pairs={{0,2},{2,0},{4,6},{6,4},{1,3},{3,1},{5,7},{7,5},{8,10},{10,8},{12,... | collective-permute-start | bytes 208904 | tf_op jit(solution)/shard_map/ppermute | solution.py:52
  10.1 4.6 %collective-permute-start.5 = (f32[136,128]{1,0:T(8,128)S(1)}, f32[136,128]{1,0:T(8,128)S(1)}, u32[]{:S(2)}, u32[]{:S(2)}) collective-permute-start(f32[136,128]{1,0:T(8,128)S(1)} %get-tuple-element.46), channel_id=1, source_target_pairs={{2,4},{4,2},{3,5},{5,3},{10,12},{12,10},{11,13},{13,11},{18,20},{2... | collective-permute-start | bytes 208904 | tf_op jit(solution)/shard_map/ppermute | solution.py:52
  14.7 0.0 copy-start.3
  14.7 1.7 %shard_map.130 = (f32[256,128]{1,0:T(8,128)S(1)}, f32[256,128]{1,0:T(8,128)S(1)}, f32[256,128]{1,0:T(8,128)S(1)}, f32[256,128]{1,0:T(8,128)S(1)}) custom-call(s32[3]{0:T(128)S(1)} %pad_add_fusion.ids, f32[32,4,16,128]{3,2,1,0:T(8,128)S(1)} %get-tuple-element.38.species, f32[64,128]{1,0:T(8,128)S(1)} %pad_maximum_fusion.refs_0_, ...), custom_call_target="tpu_custom_call" | custom-call | flops 1 | bytes 1 | tf_op jit(solution)/shard_map/pallas_call | solution.py:401
  16.4 1.6 %collective-permute-start.14 = (f32[256,128]{1,0:T(8,128)S(1)}, f32[256,128]{1,0:T(8,128)S(1)}, u32[]{:S(2)}, u32[]{:S(2)}) collective-permute-start(f32[256,128]{1,0:T(8,128)S(1)} %get-tuple-element.62), channel_id=1, source_target_pairs={{0,24},{8,16},{16,8},{24,0},{1,25},{9,17},{17,9},{25,1},{2,26},{10... | collective-permute-start | bytes 393224 | tf_op jit(solution)/shard_map/ppermute | solution.py:58
  18.0 0.0 collective-permute-done.4.refs_5_.refs_1_
  18.0 0.0 collective-permute-done.5.refs_6_.refs_2_
  18.0 1.6 %collective-permute-start.12 = (f32[256,128]{1,0:T(8,128)S(1)}, f32[256,128]{1,0:T(8,128)S(1)}, u32[]{:S(2)}, u32[]{:S(2)}) collective-permute-start(f32[256,128]{1,0:T(8,128)S(1)} %get-tuple-element.60), channel_id=1, source_target_pairs={{0,8},{8,0},{16,24},{24,16},{1,9},{9,1},{17,25},{25,17},{2,10},{10... | collective-permute-start | bytes 393224 | tf_op jit(solution)/shard_map/ppermute | solution.py:58
  19.5 0.5 %collective-permute-start.13 = (f32[256,128]{1,0:T(8,128)S(1)}, f32[256,128]{1,0:T(8,128)S(1)}, u32[]{:S(2)}, u32[]{:S(2)}) collective-permute-start(f32[256,128]{1,0:T(8,128)S(1)} %get-tuple-element.61), channel_id=1, source_target_pairs={{0,16},{8,24},{16,0},{24,8},{1,17},{9,25},{17,1},{25,9},{2,18},{10... | collective-permute-start | bytes 393224 | tf_op jit(solution)/shard_map/ppermute | solution.py:58
  20.0 2.2 %shard_map.131 = (f32[256,128]{1,0:T(8,128)S(1)}, f32[256,128]{1,0:T(8,128)S(1)}, f32[256,128]{1,0:T(8,128)S(1)}, f32[256,128]{1,0:T(8,128)S(1)}, f32[128,128]{1,0:T(8,128)S(1)}, /*index=5*/s32[1]{0:T(128)}) custom-call(s32[3]{0:T(128)S(1)} %pad_add_fusion.ids, f32[32,4,16,128]{3,2,1,0:T(8,128)S(1)} %get-tuple-element.38.species, ...), custom_call_target="tpu_custom_call" | custom-call | flops 1835008 | bytes 67108864 | tf_op jit(solution)/shard_map/pallas_call | solution.py:401
  22.2 0.6 %collective-permute-start.6 = (f32[256,128]{1,0:T(8,128)S(1)}, f32[256,128]{1,0:T(8,128)S(1)}, u32[]{:S(2)}, u32[]{:S(2)}) collective-permute-start(f32[256,128]{1,0:T(8,128)S(1)} %get-tuple-element.51), channel_id=1, source_target_pairs={{0,8},{8,0},{16,24},{24,16},{1,9},{9,1},{17,25},{25,17},{2,10},{10... | collective-permute-start | bytes 393224 | tf_op jit(solution)/shard_map/ppermute | solution.py:58
  22.8 1.5 %collective-permute-start.7 = (f32[256,128]{1,0:T(8,128)S(1)}, f32[256,128]{1,0:T(8,128)S(1)}, u32[]{:S(2)}, u32[]{:S(2)}) collective-permute-start(f32[256,128]{1,0:T(8,128)S(1)} %get-tuple-element.52), channel_id=1, source_target_pairs={{0,16},{8,24},{16,0},{24,8},{1,17},{9,25},{17,1},{25,9},{2,18},{10... | collective-permute-start | bytes 393224 | tf_op jit(solution)/shard_map/ppermute | solution.py:58
  24.3 0.0 collective-permute-done.14
  24.3 1.4 %collective-permute-start.8 = (f32[256,128]{1,0:T(8,128)S(1)}, f32[256,128]{1,0:T(8,128)S(1)}, u32[]{:S(2)}, u32[]{:S(2)}) collective-permute-start(f32[256,128]{1,0:T(8,128)S(1)} %get-tuple-element.53), channel_id=1, source_target_pairs={{0,24},{8,16},{16,8},{24,0},{1,25},{9,17},{17,9},{25,1},{2,26},{10... | collective-permute-start | bytes 393224 | tf_op jit(solution)/shard_map/ppermute | solution.py:58
  25.8 0.9 %collective-permute-done.12 = f32[256,128]{1,0:T(8,128)S(1)} collective-permute-done((f32[256,128]{1,0:T(8,128)S(1)}, f32[256,128]{1,0:T(8,128)S(1)}, u32[]{:S(2)}, u32[]{:S(2)}) %collective-permute-start.12) | collective-permute-done | bytes 131104 | tf_op jit(solution)/shard_map/ppermute | solution.py:58
  26.6 0.0 collective-permute-done.13
  26.7 2.0 %shard_map.133 = (f32[256,128]{1,0:T(8,128)S(1)}, f32[256,128]{1,0:T(8,128)S(1)}, f32[256,128]{1,0:T(8,128)S(1)}, f32[256,128]{1,0:T(8,128)S(1)}, f32[8,128]{1,0:T(8,128)S(1)}) custom-call(s32[3]{0:T(128)S(1)} %pad_add_fusion.ids, s32[1]{0:T(128)} %get-tuple-element.49.deepest, f32[8,32,128]{2,1,0:T(8,128)S(1)} %bitcast.38, f32[8,32,128]{2,1,0:T(8,128)S(1)} %bitcast.42, ...), custom_call_target="tpu_custom_call" | custom-call | flops 268435456 | bytes 2097152 | tf_op jit(solution)/shard_map/pallas_call | solution.py:421
  28.6 0.6 %collective-permute-start.15 = (f32[256,128]{1,0:T(8,128)S(1)}, f32[256,128]{1,0:T(8,128)S(1)}, u32[]{:S(2)}, u32[]{:S(2)}) collective-permute-start(f32[256,128]{1,0:T(8,128)S(1)} %get-tuple-element.64), channel_id=1, source_target_pairs={{0,8},{8,0},{16,24},{24,16},{1,9},{9,1},{17,25},{25,17},{2,10},{10... | collective-permute-start | bytes 393224 | tf_op jit(solution)/shard_map/ppermute | solution.py:58
  29.3 0.7 %collective-permute-start.16 = (f32[256,128]{1,0:T(8,128)S(1)}, f32[256,128]{1,0:T(8,128)S(1)}, u32[]{:S(2)}, u32[]{:S(2)}) collective-permute-start(f32[256,128]{1,0:T(8,128)S(1)} %get-tuple-element.65), channel_id=1, source_target_pairs={{0,16},{8,24},{16,0},{24,8},{1,17},{9,25},{17,1},{25,9},{2,18},{10... | collective-permute-start | bytes 393224 | tf_op jit(solution)/shard_map/ppermute | solution.py:58
  29.9 0.0 collective-permute-done.6
  29.9 2.3 %collective-permute-start.17 = (f32[256,128]{1,0:T(8,128)S(1)}, f32[256,128]{1,0:T(8,128)S(1)}, u32[]{:S(2)}, u32[]{:S(2)}) collective-permute-start(f32[256,128]{1,0:T(8,128)S(1)} %get-tuple-element.66), channel_id=1, source_target_pairs={{0,24},{8,16},{16,8},{24,0},{1,25},{9,17},{17,9},{25,1},{2,26},{10... | collective-permute-start | bytes 393224 | tf_op jit(solution)/shard_map/ppermute | solution.py:58
  32.2 0.0 collective-permute-done.7
  32.2 0.0 collective-permute-done.8
  32.2 0.0 copy-start.2
  32.2 0.0 copy-start.4
  32.2 2.0 %shard_map.132 = (f32[256,128]{1,0:T(8,128)S(1)}, f32[256,128]{1,0:T(8,128)S(1)}, f32[256,128]{1,0:T(8,128)S(1)}, f32[256,128]{1,0:T(8,128)S(1)}, f32[8,128]{1,0:T(8,128)S(1)}) custom-call(s32[3]{0:T(128)S(1)} %pad_add_fusion.ids, s32[1]{0:T(128)} %get-tuple-element.49.deepest, f32[8,32,128]{2,1,0:T(8,128)S(1)} %bitcast.36, f32[8,32,128]{2,1,0:T(8,128)S(1)} %bitcast.37, ...), custom_call_target="tpu_custom_call" | custom-call | flops 268435456 | bytes 2097152 | tf_op jit(solution)/shard_map/pallas_call | solution.py:421
  34.2 0.0 copy-start
  34.3 0.6 %collective-permute-start.9 = (f32[256,128]{1,0:T(8,128)S(1)}, f32[256,128]{1,0:T(8,128)S(1)}, u32[]{:S(2)}, u32[]{:S(2)}) collective-permute-start(f32[256,128]{1,0:T(8,128)S(1)} %get-tuple-element.56), channel_id=1, source_target_pairs={{0,8},{8,0},{16,24},{24,16},{1,9},{9,1},{17,25},{25,17},{2,10},{10... | collective-permute-start | bytes 393224 | tf_op jit(solution)/shard_map/ppermute | solution.py:58
  34.9 1.6 %collective-permute-start.10 = (f32[256,128]{1,0:T(8,128)S(1)}, f32[256,128]{1,0:T(8,128)S(1)}, u32[]{:S(2)}, u32[]{:S(2)}) collective-permute-start(f32[256,128]{1,0:T(8,128)S(1)} %get-tuple-element.57), channel_id=1, source_target_pairs={{0,16},{8,24},{16,0},{24,8},{1,17},{9,25},{17,1},{25,9},{2,18},{10... | collective-permute-start | bytes 393224 | tf_op jit(solution)/shard_map/ppermute | solution.py:58
  36.5 1.3 %collective-permute-start.11 = (f32[256,128]{1,0:T(8,128)S(1)}, f32[256,128]{1,0:T(8,128)S(1)}, u32[]{:S(2)}, u32[]{:S(2)}) collective-permute-start(f32[256,128]{1,0:T(8,128)S(1)} %get-tuple-element.58), channel_id=1, source_target_pairs={{0,24},{8,16},{16,8},{24,0},{1,25},{9,17},{17,9},{25,1},{2,26},{10... | collective-permute-start | bytes 393224 | tf_op jit(solution)/shard_map/ppermute | solution.py:58
  37.8 1.2 %shard_map.136 = (f32[1,16,128]{2,1,0:T(8,128)}, f32[1,16,128]{2,1,0:T(8,128)}, f32[1,16,128]{2,1,0:T(8,128)}) custom-call(s32[3]{0:T(128)S(1)} %pad_add_fusion.ids, f32[1,16,128]{2,1,0:T(8,128)S(1)} %copy-done.2, f32[1,16,128]{2,1,0:T(8,128)S(1)} %copy-done.1, f32[1,16,128]{2,1,0:T(8,128)S(1)} %copy-done, f32[1,16,128]{2,1,0:T(8,128)S(1)} %copy-done.4, ...), custom_call_target="tpu_custom_call" | custom-call | tf_op jit(solution)/shard_map/pallas_call | solution.py:468
  39.1 0.0 collective-permute-done.17
  39.1 1.4 %shard_map.134.refs_4_ = f32[32,4,16,128]{3,2,1,0:T(8,128)} custom-call(s32[3]{0:T(128)S(1)} %pad_add_fusion.ids, f32[32,8,128]{2,1,0:T(8,128)S(1)} %bitcast.24, f32[32,8,128]{2,1,0:T(8,128)S(1)} %bitcast.25, f32[32,8,128]{2,1,0:T(8,128)S(1)} %bitcast.26, f32[32,8,128]{2,1,0:T(8,128)S(1)} %bitcast.28), custom_call_target="tpu_custom_call" | custom-call | bytes 1048576 | tf_op jit(solution)/shard_map/pallas_call | solution.py:446
  40.5 0.2 collective-permute-done.9
  40.7 0.7 %collective-permute-done.10 = f32[256,128]{1,0:T(8,128)S(1)} collective-permute-done((f32[256,128]{1,0:T(8,128)S(1)}, f32[256,128]{1,0:T(8,128)S(1)}, u32[]{:S(2)}, u32[]{:S(2)}) %collective-permute-start.10) | collective-permute-done | bytes 131104 | tf_op jit(solution)/shard_map/ppermute | solution.py:58
  41.4 0.9 %collective-permute-done.11 = f32[256,128]{1,0:T(8,128)S(1)} collective-permute-done((f32[256,128]{1,0:T(8,128)S(1)}, f32[256,128]{1,0:T(8,128)S(1)}, u32[]{:S(2)}, u32[]{:S(2)}) %collective-permute-start.11) | collective-permute-done | bytes 131104 | tf_op jit(solution)/shard_map/ppermute | solution.py:58
  42.3 1.4 %shard_map.135 = f32[32,4,16,128]{3,2,1,0:T(8,128)} custom-call(s32[3]{0:T(128)S(1)} %pad_add_fusion.ids, f32[32,8,128]{2,1,0:T(8,128)S(1)} %bitcast.27, f32[32,8,128]{2,1,0:T(8,128)S(1)} %bitcast.29, f32[32,8,128]{2,1,0:T(8,128)S(1)} %bitcast.30, f32[32,8,128]{2,1,0:T(8,128)S(1)} %bitcast.31, ...), custom_call_target="tpu_custom_call", output_to_operand_aliasing={{}: (5, {})} | custom-call | bytes 1048576 | tf_op jit(solution)/shard_map/pallas_call | solution.py:446
  (28 shorter events, 0.1 us)
Async XLA Ops:
  1.4 6.9 %collective-permute-start.2 = (f32[64,128]{1,0:T(8,128)S(1)}, f32[64,128]{1,0:T(8,128)S(1)}, u32[]{:S(2)}, u32[]{:S(2)}) collective-permute-start(f32[64,128]{1,0:T(8,128)S(1)} %pad_maximum_fusion.refs_0_), channel_id=1, source_target_pairs={{0,24},{8,16},{16,8},{24,0},{1,25},{9,17},{17,9},{25,1},{2,26},{10... | collective-permute-start | bytes 98312 | tf_op jit(solution)/shard_map/ppermute | solution.py:58
  3.8 4.4 %collective-permute-start.1 = (f32[64,128]{1,0:T(8,128)S(1)}, f32[64,128]{1,0:T(8,128)S(1)}, u32[]{:S(2)}, u32[]{:S(2)}) collective-permute-start(f32[64,128]{1,0:T(8,128)S(1)} %pad_maximum_fusion.refs_0_), channel_id=1, source_target_pairs={{0,16},{8,24},{16,0},{24,8},{1,17},{9,25},{17,1},{25,9},{2,18},{10... | collective-permute-start | bytes 98312 | tf_op jit(solution)/shard_map/ppermute | solution.py:58
  4.3 3.9 %collective-permute-start = (f32[64,128]{1,0:T(8,128)S(1)}, f32[64,128]{1,0:T(8,128)S(1)}, u32[]{:S(2)}, u32[]{:S(2)}) collective-permute-start(f32[64,128]{1,0:T(8,128)S(1)} %pad_maximum_fusion.refs_0_), channel_id=1, source_target_pairs={{0,8},{8,0},{16,24},{24,16},{1,9},{9,1},{17,25},{25,17},{2,10},{10... | collective-permute-start | bytes 98312 | tf_op jit(solution)/shard_map/ppermute | solution.py:58
  8.3 1.3 %collective-permute-start.3 = (f32[112,128]{1,0:T(8,128)S(1)}, f32[112,128]{1,0:T(8,128)S(1)}, u32[]{:S(2)}, u32[]{:S(2)}) collective-permute-start(f32[112,128]{1,0:T(8,128)S(1)} %get-tuple-element.73), channel_id=1, source_target_pairs={{0,1},{1,0},{2,3},{3,2},{4,5},{5,4},{6,7},{7,6},{8,9},{9,8},{10,11... | collective-permute-start | bytes 172040 | tf_op jit(solution)/shard_map/ppermute | solution.py:52
  9.6 8.4 %collective-permute-start.4 = (f32[136,128]{1,0:T(8,128)S(1)}, f32[136,128]{1,0:T(8,128)S(1)}, u32[]{:S(2)}, u32[]{:S(2)}) collective-permute-start(f32[136,128]{1,0:T(8,128)S(1)} %get-tuple-element.45), channel_id=1, source_target_pairs={{0,2},{2,0},{4,6},{6,4},{1,3},{3,1},{5,7},{7,5},{8,10},{10,8},{12,... | collective-permute-start | bytes 208904 | tf_op jit(solution)/shard_map/ppermute | solution.py:52
  10.1 7.9 %collective-permute-start.5 = (f32[136,128]{1,0:T(8,128)S(1)}, f32[136,128]{1,0:T(8,128)S(1)}, u32[]{:S(2)}, u32[]{:S(2)}) collective-permute-start(f32[136,128]{1,0:T(8,128)S(1)} %get-tuple-element.46), channel_id=1, source_target_pairs={{2,4},{4,2},{3,5},{5,3},{10,12},{12,10},{11,13},{13,11},{18,20},{2... | collective-permute-start | bytes 208904 | tf_op jit(solution)/shard_map/ppermute | solution.py:52
  14.7 5.4 %copy-start.3 = (s32[16,128]{1,0:T(8,128)S(1)}, s32[16,128]{1,0:T(8,128)}, u32[]{:S(2)}) copy-start(s32[16,128]{1,0:T(8,128)} %refs_5_.3) | copy-start | bytes 24580
  16.4 7.9 %collective-permute-start.14 = (f32[256,128]{1,0:T(8,128)S(1)}, f32[256,128]{1,0:T(8,128)S(1)}, u32[]{:S(2)}, u32[]{:S(2)}) collective-permute-start(f32[256,128]{1,0:T(8,128)S(1)} %get-tuple-element.62), channel_id=1, source_target_pairs={{0,24},{8,16},{16,8},{24,0},{1,25},{9,17},{17,9},{25,1},{2,26},{10... | collective-permute-start | bytes 393224 | tf_op jit(solution)/shard_map/ppermute | solution.py:58
  18.0 2.1 %copy-start.5 = (f32[128]{0:T(128)S(1)}, f32[128]{0:T(128)}, u32[]{:S(2)}) copy-start(f32[128]{0:T(128)} %param.19) | copy-start | bytes 1540
  18.0 8.7 %collective-permute-start.12 = (f32[256,128]{1,0:T(8,128)S(1)}, f32[256,128]{1,0:T(8,128)S(1)}, u32[]{:S(2)}, u32[]{:S(2)}) collective-permute-start(f32[256,128]{1,0:T(8,128)S(1)} %get-tuple-element.60), channel_id=1, source_target_pairs={{0,8},{8,0},{16,24},{24,16},{1,9},{9,1},{17,25},{25,17},{2,10},{10... | collective-permute-start | bytes 393224 | tf_op jit(solution)/shard_map/ppermute | solution.py:58
  19.5 7.1 %collective-permute-start.13 = (f32[256,128]{1,0:T(8,128)S(1)}, f32[256,128]{1,0:T(8,128)S(1)}, u32[]{:S(2)}, u32[]{:S(2)}) collective-permute-start(f32[256,128]{1,0:T(8,128)S(1)} %get-tuple-element.61), channel_id=1, source_target_pairs={{0,16},{8,24},{16,0},{24,8},{1,17},{9,25},{17,1},{25,9},{2,18},{10... | collective-permute-start | bytes 393224 | tf_op jit(solution)/shard_map/ppermute | solution.py:58
  20.0 6.6 %copy-start.6 = (bf16[512,128]{1,0:T(8,128)(2,1)S(1)}, bf16[512,128]{1,0:T(8,128)(2,1)}, u32[]{:S(2)}) copy-start(bf16[512,128]{1,0:T(8,128)(2,1)} %refs_6_.3) | copy-start | bytes 393220
  20.0 6.6 %copy-start.7 = (bf16[128,512]{1,0:T(8,128)(2,1)S(1)}, bf16[128,512]{1,0:T(8,128)(2,1)}, u32[]{:S(2)}) copy-start(bf16[128,512]{1,0:T(8,128)(2,1)} %refs_7_.5) | copy-start | bytes 393220
  22.2 7.7 %collective-permute-start.6 = (f32[256,128]{1,0:T(8,128)S(1)}, f32[256,128]{1,0:T(8,128)S(1)}, u32[]{:S(2)}, u32[]{:S(2)}) collective-permute-start(f32[256,128]{1,0:T(8,128)S(1)} %get-tuple-element.51), channel_id=1, source_target_pairs={{0,8},{8,0},{16,24},{24,16},{1,9},{9,1},{17,25},{25,17},{2,10},{10... | collective-permute-start | bytes 393224 | tf_op jit(solution)/shard_map/ppermute | solution.py:58
  22.8 9.4 %collective-permute-start.7 = (f32[256,128]{1,0:T(8,128)S(1)}, f32[256,128]{1,0:T(8,128)S(1)}, u32[]{:S(2)}, u32[]{:S(2)}) collective-permute-start(f32[256,128]{1,0:T(8,128)S(1)} %get-tuple-element.52), channel_id=1, source_target_pairs={{0,16},{8,24},{16,0},{24,8},{1,17},{9,25},{17,1},{25,9},{2,18},{10... | collective-permute-start | bytes 393224 | tf_op jit(solution)/shard_map/ppermute | solution.py:58
  24.3 7.9 %collective-permute-start.8 = (f32[256,128]{1,0:T(8,128)S(1)}, f32[256,128]{1,0:T(8,128)S(1)}, u32[]{:S(2)}, u32[]{:S(2)}) collective-permute-start(f32[256,128]{1,0:T(8,128)S(1)} %get-tuple-element.53), channel_id=1, source_target_pairs={{0,24},{8,16},{16,8},{24,0},{1,25},{9,17},{17,9},{25,1},{2,26},{10... | collective-permute-start | bytes 393224 | tf_op jit(solution)/shard_map/ppermute | solution.py:58
  28.6 7.8 %collective-permute-start.15 = (f32[256,128]{1,0:T(8,128)S(1)}, f32[256,128]{1,0:T(8,128)S(1)}, u32[]{:S(2)}, u32[]{:S(2)}) collective-permute-start(f32[256,128]{1,0:T(8,128)S(1)} %get-tuple-element.64), channel_id=1, source_target_pairs={{0,8},{8,0},{16,24},{24,16},{1,9},{9,1},{17,25},{25,17},{2,10},{10... | collective-permute-start | bytes 393224 | tf_op jit(solution)/shard_map/ppermute | solution.py:58
  29.3 9.8 %collective-permute-start.16 = (f32[256,128]{1,0:T(8,128)S(1)}, f32[256,128]{1,0:T(8,128)S(1)}, u32[]{:S(2)}, u32[]{:S(2)}) collective-permute-start(f32[256,128]{1,0:T(8,128)S(1)} %get-tuple-element.65), channel_id=1, source_target_pairs={{0,16},{8,24},{16,0},{24,8},{1,17},{9,25},{17,1},{25,9},{2,18},{10... | collective-permute-start | bytes 393224 | tf_op jit(solution)/shard_map/ppermute | solution.py:58
  29.9 9.2 %collective-permute-start.17 = (f32[256,128]{1,0:T(8,128)S(1)}, f32[256,128]{1,0:T(8,128)S(1)}, u32[]{:S(2)}, u32[]{:S(2)}) collective-permute-start(f32[256,128]{1,0:T(8,128)S(1)} %get-tuple-element.66), channel_id=1, source_target_pairs={{0,24},{8,16},{16,8},{24,0},{1,25},{9,17},{17,9},{25,1},{2,26},{10... | collective-permute-start | bytes 393224 | tf_op jit(solution)/shard_map/ppermute | solution.py:58
  32.2 5.6 %copy-start.1 = (f32[1,16,128]{2,1,0:T(8,128)S(1)}, f32[1,16,128]{2,1,0:T(8,128)}, u32[]{:S(2)}) copy-start(f32[1,16,128]{2,1,0:T(8,128)} %north.1) | copy-start | bytes 24580
  32.2 5.6 %copy-start.2 = (f32[1,16,128]{2,1,0:T(8,128)S(1)}, f32[1,16,128]{2,1,0:T(8,128)}, u32[]{:S(2)}) copy-start(f32[1,16,128]{2,1,0:T(8,128)} %east.1) | copy-start | bytes 24580
  32.2 5.6 %copy-start.4 = (f32[1,16,128]{2,1,0:T(8,128)S(1)}, f32[1,16,128]{2,1,0:T(8,128)}, u32[]{:S(2)}) copy-start(f32[1,16,128]{2,1,0:T(8,128)} %density.1) | copy-start | bytes 24580
  34.2 3.6 %copy-start = (f32[1,16,128]{2,1,0:T(8,128)S(1)}, f32[1,16,128]{2,1,0:T(8,128)}, u32[]{:S(2)}) copy-start(f32[1,16,128]{2,1,0:T(8,128)} %warmth.1) | copy-start | bytes 24580
  34.3 6.4 %collective-permute-start.9 = (f32[256,128]{1,0:T(8,128)S(1)}, f32[256,128]{1,0:T(8,128)S(1)}, u32[]{:S(2)}, u32[]{:S(2)}) collective-permute-start(f32[256,128]{1,0:T(8,128)S(1)} %get-tuple-element.56), channel_id=1, source_target_pairs={{0,8},{8,0},{16,24},{24,16},{1,9},{9,1},{17,25},{25,17},{2,10},{10... | collective-permute-start | bytes 393224 | tf_op jit(solution)/shard_map/ppermute | solution.py:58
  34.9 6.5 %collective-permute-start.10 = (f32[256,128]{1,0:T(8,128)S(1)}, f32[256,128]{1,0:T(8,128)S(1)}, u32[]{:S(2)}, u32[]{:S(2)}) collective-permute-start(f32[256,128]{1,0:T(8,128)S(1)} %get-tuple-element.57), channel_id=1, source_target_pairs={{0,16},{8,24},{16,0},{24,8},{1,17},{9,25},{17,1},{25,9},{2,18},{10... | collective-permute-start | bytes 393224 | tf_op jit(solution)/shard_map/ppermute | solution.py:58
  36.5 5.9 %collective-permute-start.11 = (f32[256,128]{1,0:T(8,128)S(1)}, f32[256,128]{1,0:T(8,128)S(1)}, u32[]{:S(2)}, u32[]{:S(2)}) collective-permute-start(f32[256,128]{1,0:T(8,128)S(1)} %get-tuple-element.58), channel_id=1, source_target_pairs={{0,24},{8,16},{16,8},{24,0},{1,25},{9,17},{17,9},{25,1},{2,26},{10... | collective-permute-start | bytes 393224 | tf_op jit(solution)/shard_map/ppermute | solution.py:58

commit v3 on v2

v3 whole, which is shorter than its diff:
```python
import functools

import jax
import jax.numpy as jnp
from jax import lax
from jax.experimental import pallas as pl
from jax.experimental.pallas import tpu as pltpu
from jax.sharding import PartitionSpec as P

diffusion = 0.1
pressure = 0.05
chem_step = 0.2

VMEM = pl.BlockSpec(memory_space=pltpu.VMEM)
ANY = pl.BlockSpec(memory_space=pl.ANY)
HBM = pl.BlockSpec(memory_space=pltpu.HBM)
LIMIT = 40 * 1024 * 1024
F32 = jnp.float32


def struct(*shape, dtype=F32):
    return jax.ShapeDtypeStruct(shape, dtype)


def call(kernel, out_shape, in_specs, out_specs=None, scratch=(), aliases=None, flops=1, touched=1, limit=LIMIT):
    return pl.pallas_call(
        kernel,
        out_shape=out_shape,
        in_specs=in_specs,
        out_specs=jax.tree.map(lambda _: VMEM, out_shape) if out_specs is None else out_specs,
        scratch_shapes=list(scratch),
        input_output_aliases=aliases or {},
        compiler_params=pltpu.CompilerParams(vmem_limit_bytes=limit),
        cost_estimate=pl.CostEstimate(flops=flops, bytes_accessed=touched, transcendentals=0),
    )


def parity(axis):
    return lax.rem(lax.axis_index(axis), 2)


def even_pairs(count):
    return [(i, i ^ 1) for i in range(count) if (i ^ 1) < count]


def odd_pairs(count):
    pairs = []
    for i in range(1, count - 1, 2):
        pairs += [(i, i + 1), (i + 1, i)]
    return pairs


def neighbours(messages, axis):
    count = lax.axis_size(axis)
    return [
        lax.ppermute(m, axis, pairs)
        for m, pairs in zip(messages, (even_pairs(count), odd_pairs(count)))
    ]


def lat_neighbours(messages):
    rows, columns = lax.axis_size("lat"), lax.axis_size("lon")
    if len(messages) < 2 or rows % 2 or columns % 2:
        return neighbours(messages, "lat")
    partner = dict(odd_pairs(rows))
    pairs = [
        (i * columns + j, partner[i] * columns + j if i in partner else i * columns + (j ^ 1))
        for i in range(rows)
        for j in range(columns)
    ]
    first = lax.ppermute(messages[0], "lat", even_pairs(rows))
    return [first, lax.ppermute(messages[1], ("lat", "lon"), pairs)]


def partner_swap(block, hop):
    return lax.ppermute(block, "group", [(i, i ^ hop) for i in range(lax.axis_size("group"))])


def lane_ids(shape):
    return lax.broadcasted_iota(jnp.int32, shape, len(shape) - 1)


def row_ids(shape):
    return lax.broadcasted_iota(jnp.int32, shape, len(shape) - 2)


def pack_kernel(n_lon, n_lat, parts, species_hbm, *refs):
    *outs, species, sems = refs
    tracers, strata, rows, width = species.shape
    share = tracers // parts
    copies = [
        pltpu.make_async_copy(
            species_hbm.at[pl.ds(part * share, share)],
            species.at[pl.ds(part * share, share)],
            sems.at[part],
        )
        for part in range(parts)
    ]
    for copy in copies:
        copy.start()
    lane = lane_ids((rows, width))
    flat = species.reshape(tracers * strata * rows, width)
    held = share * strata
    columns = [jnp.zeros((rows, width), F32) for _ in range(n_lon)]
    for part, copy in enumerate(copies):
        copy.wait()
        for at, message in enumerate(outs[n_lon:n_lon + n_lat]):
            edge = jnp.where(parity("lat") == at, rows - 1, 0)
            message[part * held:(part + 1) * held] = flat[
                pl.ds(part * held * rows + edge, held, stride=rows), :
            ]
        for at in range(n_lon):
            edge = jnp.where(parity("lon") == at, width - 1, 0)
            for place in range(part * held, (part + 1) * held):
                block = species[place // strata, place % strata]
                turned = pltpu.roll(block, lax.rem(place - edge + width, width), 1)
                columns[at] = jnp.where(lane == place, turned, columns[at])
    for message, block in zip(outs[:n_lon], columns):
        message[...] = block


def both_sides(axis, got):
    even = parity(axis) == 0
    if len(got) == 1:
        got = [got[0], got[0]]
    at = lax.axis_index(axis)
    low = jnp.where(even, got[1], got[0])
    high = jnp.where(even, got[0], got[1])
    return jnp.where(at > 0, low, 0.0), jnp.where(at < lax.axis_size(axis) - 1, high, 0.0)


def beside(value, axis, got):
    width = value.shape[1]
    lane = lane_ids(value.shape)
    low, high = both_sides(axis, got)
    west = pltpu.roll(jnp.where(lane == width - 1, low, value), 1, 1)
    east = pltpu.roll(jnp.where(lane == 0, high, value), width - 1, 1)
    return west, east


def beyond(value, axis, got):
    rows = value.shape[0]
    row = row_ids(value.shape)
    low, high = both_sides(axis, got)
    south = jnp.where(row == 0, low, pltpu.roll(value, 1, 0))
    north = jnp.where(row == rows - 1, high, pltpu.roll(value, rows - 1, 0))
    return south, north


def middle(value):
    quarter = value.shape[0] // 4
    return value[quarter:3 * quarter]


def ends(value):
    quarter = value.shape[0] // 4
    return jnp.concatenate([value[:quarter], value[3 * quarter:]], axis=0)


def faces(low, high):
    wind = 0.5 * (low + high)
    return jnp.maximum(wind, 0.0), jnp.minimum(wind, 0.0)


def transport_kernel(chunk, n_lon, n_lat, slots, species, *refs):
    refs = list(refs)
    winds = [refs.pop(0) for _ in range(slots)]
    lon_in = [refs.pop(0) for _ in range(n_lon)]
    lat_in = [refs.pop(0) for _ in range(n_lat)] if chunk else []
    if chunk:
        yields = refs.pop(0)
    outs = [refs.pop(0) for _ in range(slots)]
    if chunk:
        weight = refs.pop(0)
        weight[...] = jnp.broadcast_to(yields[...], weight.shape[::-1]).T
    upward = refs.pop(0)
    tracers, strata, rows, width = species.shape
    half = rows // 2
    quarter = rows // 4
    base = tracers * strata
    me, lon_even = lax.axis_index("group"), parity("lon") == 0
    pick = ends if chunk else middle
    lane = lane_ids((half, width))
    row = row_ids((half, width))
    for slot in range(slots):
        upward[me ^ slot] = winds[slot][2 * rows:3 * rows]

    coefficients = []
    for slot in range(slots):
        level = me ^ slot
        east = winds[slot][0:rows]
        east_last, east_next = beside(
            east, "lon", [winds[slot][at:at + rows] for at in range(4 * rows, (4 + n_lon) * rows, rows)]
        )
        north = winds[slot][rows:2 * rows]
        rim = [m[base + slot:base + slot + 1] for m in lat_in] or [jnp.zeros((1, width), F32)]
        north_last, north_next = beyond(north, "lat", rim)
        up = upward[level]
        above = upward[jnp.minimum(level + 1, strata - 1)]
        below = upward[jnp.maximum(level - 1, 0)]
        has_above = jnp.where(level < strata - 1, 1.0, 0.0)
        has_below = jnp.where(level > 0, 1.0, 0.0)
        east_out, east_in = faces(east, east_next)
        west_in, west_out = faces(east_last, east)
        north_out, north_in = faces(north, north_next)
        south_in, south_out = faces(north_last, north)
        up_out, up_in = [has_above * f for f in faces(up, above)]
        down_in, down_out = [has_below * f for f in faces(below, up)]
        stay = 1.0 - (
            (east_out - west_out) + (north_out - south_out) + (up_out - down_out)
        )
        stay, east_in, west_in, north_in, south_in, up_in, down_in = [
            pick(f) for f in (stay, -east_in, west_in, -north_in, south_in, -up_in, down_in)
        ]
        if n_lon < 2:
            east_in = jnp.where((lane == width - 1) & ~lon_even, 0.0, east_in)
            west_in = jnp.where((lane == 0) & lon_even, 0.0, west_in)
        coefficients.append((stay, east_in, west_in, north_in, south_in, up_in, down_in))

    columns = [pick(m[0:rows]) for m in lon_in]
    if n_lon == 2:
        columns = both_sides("lon", columns)
    edge = jnp.where(lon_even, width - 1, 0)

    def one(t, carry):
        for slot in range(slots):
            level = me ^ slot
            stay, east_in, west_in, north_in, south_in, up_in, down_in = coefficients[slot]
            place = t * strata + level
            if n_lon == 2:
                low = pltpu.roll(columns[0], lax.rem(width - place, width), 1)
                high = pltpu.roll(columns[1], width - 1 - place, 1)
            else:
                low = high = pltpu.roll(columns[0], lax.rem(width + edge - place, width), 1)
            above = jnp.minimum(level + 1, strata - 1)
            below = jnp.maximum(level - 1, 0)
            if chunk:
                first, last = species[t, level, 0:half], species[t, level, half:rows]
                here = jnp.where(row < quarter, first, last)
                low_row, high_row = both_sides("lat", [m[pl.ds(place, 1), :] for m in lat_in])
                south = pltpu.roll(jnp.where(row < quarter - 1, first, last), 1, 0)
                south = jnp.where(row == 0, low_row, south)
                north = pltpu.roll(jnp.where(row < quarter + 1, first, last), half - 1, 0)
                north = jnp.where(row == half - 1, high_row, north)
                up = jnp.where(
                    row < quarter, species[t, above, 0:half], species[t, above, half:rows]
                )
                down = jnp.where(
                    row < quarter, species[t, below, 0:half], species[t, below, half:rows]
                )
            else:
                here = species[t, level, quarter:3 * quarter]
                south = species[t, level, quarter - 1:3 * quarter - 1]
                north = species[t, level, quarter + 1:3 * quarter + 1]
                up = species[t, above, quarter:3 * quarter]
                down = species[t, below, quarter:3 * quarter]
            east = jnp.where(lane == width - 1, high, pltpu.roll(here, width - 1, 1))
            west = jnp.where(lane == 0, low, pltpu.roll(here, 1, 1))
            value = (
                (stay * here + east_in * east)
                + (west_in * west + north_in * north)
                + (south_in * south + up_in * up)
                + down_in * down
            )
            outs[slot][pl.ds(t, half, stride=tracers), :] = value
        return carry

    lax.fori_loop(0, tracers, one, 0, unroll=8)


def chemistry_kernel(chunk, slots, *refs):
    refs = list(refs)
    advected = [refs.pop(0) for _ in range(slots)]
    warmth, counts, companion, stoichiometry, weight = [refs.pop(0) for _ in range(5)]
    outs = [refs.pop(0) for _ in range(slots)]
    heat, current = refs
    half, owned, width = advected[0].shape
    species = slots * owned
    repeats = companion.shape[0] // species
    pick = ends if chunk else middle
    place = [pl.ds(pl.multiple_of((lax.axis_index("group") ^ slot) * owned, owned), owned) for slot in range(slots)]
    for slot in range(slots):
        current[:, place[slot], :] = advected[slot][...]
    line = lambda field: jnp.concatenate([field[r:r + 1] for r in range(half)], axis=1)
    rate = line(jax.nn.sigmoid(2.0 * pick(warmth[...])))
    many = line(pick(counts[...]))

    def substep(s, carry):
        now = jnp.concatenate([current[r] for r in range(half)], axis=1)
        pairs = jnp.dot(companion[...], now.astype(jnp.bfloat16), preferred_element_type=F32)
        quad = (pairs.reshape(repeats, species, half * width) * now[None]).astype(jnp.bfloat16)
        made = jnp.dot(
            stoichiometry[...],
            quad.reshape(repeats * species, half * width),
            preferred_element_type=F32,
        )
        after = now + chem_step * (rate * made - now)
        after = jnp.where(s < many, after, now)
        for r in range(half):
            current[r] = after[:, r * width:(r + 1) * width]
        return carry

    deepest = jnp.max(many)
    substep(0, 0)
    lax.fori_loop(1, deepest, substep, 0)
    total = None
    for slot in range(slots):
        final = current[:, place[slot], :]
        for r in range(half):
            outs[slot][pl.ds(r, owned, stride=half), :] = final[r]
        part = jnp.sum(weight[place[slot], :][None] * (final - advected[slot][...]), axis=1)
        total = part if total is None else total + part
    heat[...] = total


def dynamics_kernel(n_lon, n_lat, base, slots, east, north, warmth, density, *refs):
    refs = list(refs)
    lon_in = [refs.pop(0) for _ in range(n_lon)]
    lat_in = [refs.pop(0) for _ in range(n_lat)]
    heat_middle, heat_ends, east_out, north_out, temp_out = refs
    rows = temp_out.shape[1]
    quarter = rows // 4

    def around(value, tile, line):
        west, east = beside(value, "lon", [m[tile * rows:(tile + 1) * rows] for m in lon_in])
        south, north = beyond(value, "lat", [m[base + line:base + line + 1] for m in lat_in])
        laplace = east + west + north + south - 4.0 * value
        return value + diffusion * laplace, east - west, north - south

    new_east, _, _ = around(east[0], 0, slots)
    new_north, _, _ = around(north[0], 1, 0)
    warmed, zonal, meridional = around(warmth[0], 3, slots + 1)
    heating = jnp.concatenate(
        [heat_ends[:quarter], heat_middle[...], heat_ends[quarter:]], axis=0
    )
    east_out[0] = new_east - pressure * zonal
    north_out[0] = new_north - pressure * meridional
    temp_out[0] = warmed + heating / density[0]


def place_kernel(chunk, slots, *refs):
    got, out, sems = refs[:slots], refs[-2], refs[-1]
    rows = out.shape[2]
    quarter = rows // 4
    starts = (0, 3 * quarter) if chunk else (quarter, 2 * quarter)
    copies = [
        pltpu.make_async_copy(
            got[slot].at[:, part * quarter:(part + 1) * quarter, :],
            out.at[:, lax.axis_index("group") ^ slot, start:start + quarter, :],
            sems.at[slot, part],
        )
        for slot in range(slots)
        for part, start in enumerate(starts)
    ]
    for copy in copies:
        copy.start()
    for copy in copies:
        copy.wait()


def local(
    species_amounts,
    zonal_cell_fraction,
    meridional_cell_fraction,
    updraft_cell_fraction,
    warmth_anomaly,
    mass_per_volume,
    chemistry_iterations,
    companion_species,
    stoichiometric_rate,
    heat_yield,
):
    slots = lax.axis_size("group")
    n_lat = min(2, lax.axis_size("lat") - 1)
    n_lon = min(2, lax.axis_size("lon") - 1)
    tracers, strata, rows, width = species_amounts.shape
    half = rows // 2
    base = tracers * strata

    payload = jnp.concatenate(
        [
            zonal_cell_fraction[0],
            meridional_cell_fraction[0],
            updraft_cell_fraction[0],
            warmth_anomaly[0],
        ],
        axis=0,
    )
    payload = lax.optimization_barrier(payload)
    east, north, warmth = payload[:rows], payload[rows:2 * rows], payload[3 * rows:]
    lon_fields = neighbours([payload] * n_lon, "lon")
    payload = jnp.concatenate([payload] + [m[:rows] for m in lon_fields], axis=0)
    gathered = {hop: partner_swap(payload, hop) for hop in range(slots - 1, 0, -1)}
    winds = [payload] + [gathered[hop] for hop in range(1, slots)]

    packed = call(
        functools.partial(pack_kernel, n_lon, n_lat, 4),
        [struct(rows, width)] * n_lon
        + [struct(base, width)] * n_lat
        + [struct(tracers, strata, rows, width)],
        [HBM],
        scratch=[pltpu.SemaphoreType.DMA((4,))],
        limit=52 * 1024 * 1024,
    )(lax.optimization_barrier((species_amounts, payload))[0])
    species = packed[n_lon + n_lat]
    lon_in = neighbours(packed[:n_lon], "lon")
    lat_out = []
    for at, m in enumerate(packed[n_lon:n_lon + n_lat]):
        top = parity("lat") == at
        lines = [w[rows:2 * rows] for w in winds] + [east, warmth]
        lines = jnp.concatenate([jnp.where(top, f[rows - 1:], f[:1]) for f in lines], axis=0)
        lines = jnp.pad(lines, ((0, -lines.shape[0] % 8), (0, 0)))
        lat_out.append(jnp.concatenate([m, lines], axis=0))
    lat_out, lon_in = lax.optimization_barrier((lat_out, lon_in))
    lat_in = lat_neighbours(lat_out)

    def transport(chunk, lat_in=()):
        more = [*lat_in, heat_yield[None]] if chunk else []
        return call(
            functools.partial(transport_kernel, chunk, n_lon, n_lat, slots),
            [struct(half * tracers, width)] * slots + [struct(slots * tracers, width)] * chunk,
            [VMEM] * (1 + slots + n_lon + len(more)),
            scratch=[pltpu.VMEM((strata, rows, width), F32)],
            touched=256 * species_amounts.size if chunk else 1,
        )(species, *winds, *lon_in, *more)

    def swap_slots(blocks):
        swapped = {hop: partner_swap(blocks[hop], hop) for hop in range(slots - 1, 0, -1)}
        return [blocks[0]] + [swapped[hop] for hop in range(1, slots)]

    def chemistry(chunk, advected):
        got = call(
            functools.partial(chemistry_kernel, chunk, slots),
            [struct(tracers * half, width)] * slots + [struct(half, width)],
            [VMEM] * (slots + 5),
            scratch=[pltpu.VMEM((half, slots * tracers, width), F32)],
            flops=4 * half * width * companion_species.size,
            touched=8 * species_amounts.size,
        )(
            *[a.reshape(half, tracers, width) for a in advected],
            warmth,
            chemistry_iterations,
            companion_species,
            stoichiometric_rate,
            weight,
        )
        return got[:slots], got[slots]

    def put(chunk, blocks, partial):
        return call(
            functools.partial(place_kernel, chunk, slots),
            struct(tracers, strata, rows, width),
            [VMEM] * slots + [ANY] * len(partial),
            out_specs=ANY,
            scratch=[pltpu.SemaphoreType.DMA((slots, 2))],
            aliases={slots: 0} if partial else {},
            touched=4 * species_amounts.size,
        )(*[b.reshape(tracers, half, width) for b in blocks], *partial)

    mid = list(transport(0))
    mid[1], mid[2], lat_in = lax.optimization_barrier((mid[1], mid[2], lat_in))
    mid = swap_slots(mid)
    *end, weight = transport(1, lat_in)
    end = swap_slots(end)
    mid, heat_mid = chemistry(0, mid)
    mid = swap_slots(mid)
    end, heat_end = chemistry(1, end)
    end = swap_slots(end)
    east_out, north_out, temp_out = call(
        functools.partial(dynamics_kernel, n_lon, n_lat, base, slots),
        [struct(1, rows, width)] * 3,
        [VMEM] * (6 + n_lon + n_lat),
    )(
        zonal_cell_fraction,
        meridional_cell_fraction,
        warmth_anomaly,
        mass_per_volume,
        *lon_fields,
        *lat_in,
        heat_mid,
        heat_end,
    )
    tracers_out = put(1, end, [put(0, mid, [])])
    return (tracers_out, east_out, north_out, temp_out)


def solution(mesh):
    return jax.shard_map(
        local,
        mesh=mesh,
        in_specs=(
            P("group", None, "lat", "lon"),
            P("group", "lat", "lon"),
            P("group", "lat", "lon"),
            P("group", "lat", "lon"),
            P("group", "lat", "lon"),
            P("group", "lat", "lon"),
            P("lat", "lon"),
            P(),
            P(),
            P(),
        ),
        out_specs=(
            P("group", None, "lat", "lon"),
            P("group", "lat", "lon"),
            P("group", "lat", "lon"),
            P("group", "lat", "lon"),
        ),
        check_vma=False,
    )
```

time: 44 us -> 41.6 us (0.945)
  the two profiles are of different devices: /device:TPU:8 before, /device:TPU:0 now
where the time goes in v3:
time: 41.6 us; the launch traced here: 41.4 us
  starting transfers between devices  20.9 us (50%)
  waiting for transfers between devices  10.2 us (25%)
  Pallas kernels  7.97 us (19%)
  other arithmetic  0.79 us (2%)
  between operations  0.77 us (2%)
  local copies, waits for them, and re-layouts  0.74 us (2%)
    ppermute x15, starting transfers between devices, partner_swap(): lax.ppermute(block, 'group', [(i, i ^ hop) for i in range(lax.axis_size('...  18.8 us
    ppermute x15, waiting for transfers between devices, partner_swap(): lax.ppermute(block, 'group', [(i, i ^ hop) for i in range(lax.axis_size('...  9.29 us
    pallas_call x2, Pallas kernels, transport(): call(functools.partial(transport_kernel, chunk, n_lon, n_lat, slots), [st...  2.35 us
    pallas_call x2, Pallas kernels, put(): call(functools.partial(place_kernel, chunk, slots), struct(tracers, strat...  1.69 us
    ppermute x1, starting transfers between devices, lat_neighbours(): first = lax.ppermute(messages[0], 'lat', even_pairs(rows))  1.64 us
    pallas_call x2, Pallas kernels, chemistry(): call(functools.partial(chemistry_kernel, chunk, slots), [struct(tracers *...  1.61 us
    pallas_call x1, Pallas kernels, local(): call(functools.partial(pack_kernel, n_lon, n_lat, 4), [struct(rows, width...  1.61 us
    ppermute x2, waiting for transfers between devices, neighbours(): lax.ppermute(m, axis, pairs)  0.86 us
  transfers between devices with their start and end apart: 19, of which 9 were waited for; matrix products, arithmetic and copies ran while one was open for 0% of the time, Pallas kernels for 17%

profile of v3, /device:TPU:0, one launch (start us, length us, event | category | flops | bytes accessed | tf_op | source)
XLA Modules:
  0.0 41.4 jit_solution(8727575783690605689)
XLA Ops:
  0.6 0.8 %pad_maximum_fusion.1 = f32[64,128]{1,0:T(8,128)S(1)} fusion(f32[16,128]{1,0:T(8,128)} %bitcast.29, f32[16,128]{1,0:T(8,128)} %bitcast.41, f32[16,128]{1,0:T(8,128)} %bitcast.30, f32[16,128]{1,0:T(8,128)} %bitcast.31), kind=kLoop, calls=%fused_computation.4 | loop fusion | flops 24576 | bytes 65536 | tf_op jit(solution)/shard_map/concatenate | solution.py:380
  1.4 0.5 %collective-permute-start = (f32[64,128]{1,0:T(8,128)S(1)}, f32[64,128]{1,0:T(8,128)S(1)}, u32[]{:S(2)}, u32[]{:S(2)}) collective-permute-start(f32[64,128]{1,0:T(8,128)S(1)} %pad_maximum_fusion.1), channel_id=1, source_target_pairs={{0,1},{1,0},{2,3},{3,2},{4,5},{5,4},{6,7},{7,6},{8,9},{9,8},{10,11... | collective-permute-start | bytes 98312 | tf_op jit(solution)/shard_map/ppermute | solution.py:56
  1.8 0.9 %collective-permute-done.refs_0_ = f32[64,128]{1,0:T(8,128)S(1)} collective-permute-done((f32[64,128]{1,0:T(8,128)S(1)}, f32[64,128]{1,0:T(8,128)S(1)}, u32[]{:S(2)}, u32[]{:S(2)}) %collective-permute-start) | collective-permute-done | bytes 32800 | tf_op jit(solution)/shard_map/ppermute | solution.py:56
  2.7 3.8 %collective-permute-start.3 = (f32[80,128]{1,0:T(8,128)S(1)}, f32[80,128]{1,0:T(8,128)S(1)}, u32[]{:S(2)}, u32[]{:S(2)}) collective-permute-start(f32[80,128]{1,0:T(8,128)S(1)} %pad_maximum_fusion.refs_0_), channel_id=1, source_target_pairs={{0,24},{8,16},{16,8},{24,0},{1,25},{9,17},{17,9},{25,1},{2,26},{10... | collective-permute-start | bytes 122888 | tf_op jit(solution)/shard_map/ppermute | solution.py:76
  6.5 0.5 %collective-permute-start.2 = (f32[80,128]{1,0:T(8,128)S(1)}, f32[80,128]{1,0:T(8,128)S(1)}, u32[]{:S(2)}, u32[]{:S(2)}) collective-permute-start(f32[80,128]{1,0:T(8,128)S(1)} %pad_maximum_fusion.refs_0_), channel_id=1, source_target_pairs={{0,16},{8,24},{16,0},{24,8},{1,17},{9,25},{17,1},{25,9},{2,18},{10... | collective-permute-start | bytes 122888 | tf_op jit(solution)/shard_map/ppermute | solution.py:76
  7.0 0.1 collective-permute-start.1
  7.1 1.6 %shard_map.129 = (f32[16,128]{1,0:T(8,128)S(1)}, f32[128,128]{1,0:T(8,128)S(1)}, f32[128,128]{1,0:T(8,128)S(1)}, f32[32,4,16,128]{3,2,1,0:T(8,128)S(1)}) custom-call(f32[32,4,16,128]{3,2,1,0:T(8,128)} %species_hbm), custom_call_target="tpu_custom_call" | custom-call | flops 1 | bytes 1 | tf_op jit(solution)/shard_map/pallas_call | solution.py:396
  8.8 0.1 collective-permute-start.4
  8.8 0.0 collective-permute-done.3.refs_3_
  8.9 1.6 %collective-permute-done.2.refs_2_ = f32[80,128]{1,0:T(8,128)S(1)} collective-permute-done((f32[80,128]{1,0:T(8,128)S(1)}, f32[80,128]{1,0:T(8,128)S(1)}, u32[]{:S(2)}, u32[]{:S(2)}) %collective-permute-start.2) | collective-permute-done | bytes 40992 | tf_op jit(solution)/shard_map/ppermute | solution.py:76
  10.5 0.5 %collective-permute-done.1.refs_1_ = f32[80,128]{1,0:T(8,128)S(1)} collective-permute-done((f32[80,128]{1,0:T(8,128)S(1)}, f32[80,128]{1,0:T(8,128)S(1)}, u32[]{:S(2)}, u32[]{:S(2)}) %collective-permute-start.1) | collective-permute-done | bytes 40992 | tf_op jit(solution)/shard_map/ppermute | solution.py:76
  11.1 0.0 collective-permute-done.4.refs_4_
  11.1 1.6 %collective-permute-start.5 = (f32[136,128]{1,0:T(8,128)S(1)}, f32[136,128]{1,0:T(8,128)S(1)}, u32[]{:S(2)}, u32[]{:S(2)}) collective-permute-start(f32[136,128]{1,0:T(8,128)S(1)} %get-tuple-element.46), channel_id=1, source_target_pairs={{0,2},{2,0},{4,6},{6,4},{1,3},{3,1},{5,7},{7,5},{8,10},{10,8},{12,... | collective-permute-start | bytes 208904 | tf_op jit(solution)/shard_map/ppermute | solution.py:71
  12.7 0.0 collective-permute-start.6
  12.7 1.2 %shard_map.130 = (f32[256,128]{1,0:T(8,128)S(1)}, f32[256,128]{1,0:T(8,128)S(1)}, f32[256,128]{1,0:T(8,128)S(1)}, f32[256,128]{1,0:T(8,128)S(1)}) custom-call(f32[32,4,16,128]{3,2,1,0:T(8,128)S(1)} %get-tuple-element.39.species, f32[80,128]{1,0:T(8,128)S(1)} %pad_maximum_fusion.refs_0_, f32[80,128]{1,0:T(8,128)S(1)} %collective-permute-done.1.refs_1_, ...), custom_call_target="tpu_custom_call" | custom-call | flops 1 | bytes 1 | tf_op jit(solution)/shard_map/pallas_call | solution.py:419
  14.0 1.7 %collective-permute-start.15 = (f32[256,128]{1,0:T(8,128)S(1)}, f32[256,128]{1,0:T(8,128)S(1)}, u32[]{:S(2)}, u32[]{:S(2)}) collective-permute-start(f32[256,128]{1,0:T(8,128)S(1)} %get-tuple-element.62), channel_id=1, source_target_pairs={{0,24},{8,16},{16,8},{24,0},{1,25},{9,17},{17,9},{25,1},{2,26},{10... | collective-permute-start | bytes 393224 | tf_op jit(solution)/shard_map/ppermute | solution.py:76
  15.7 0.0 collective-permute-done.5.refs_5_.refs_1_
  15.7 0.0 collective-permute-done.6.refs_6_.refs_2_
  15.7 1.3 %collective-permute-start.13 = (f32[256,128]{1,0:T(8,128)S(1)}, f32[256,128]{1,0:T(8,128)S(1)}, u32[]{:S(2)}, u32[]{:S(2)}) collective-permute-start(f32[256,128]{1,0:T(8,128)S(1)} %get-tuple-element.60), channel_id=1, source_target_pairs={{0,8},{8,0},{16,24},{24,16},{1,9},{9,1},{17,25},{25,17},{2,10},{10... | collective-permute-start | bytes 393224 | tf_op jit(solution)/shard_map/ppermute | solution.py:76
  17.0 0.7 %collective-permute-start.14 = (f32[256,128]{1,0:T(8,128)S(1)}, f32[256,128]{1,0:T(8,128)S(1)}, u32[]{:S(2)}, u32[]{:S(2)}) collective-permute-start(f32[256,128]{1,0:T(8,128)S(1)} %get-tuple-element.61), channel_id=1, source_target_pairs={{0,16},{8,24},{16,0},{24,8},{1,17},{9,25},{17,1},{25,9},{2,18},{10... | collective-permute-start | bytes 393224 | tf_op jit(solution)/shard_map/ppermute | solution.py:76
  17.7 0.7 %copy-done.4 = f32[128]{0:T(128)S(1)} copy-done((f32[128]{0:T(128)S(1)}, f32[128]{0:T(128)}, u32[]{:S(2)}) %copy-start.4) | copy-done | bytes 536
  18.4 1.1 %shard_map.131 = (f32[256,128]{1,0:T(8,128)S(1)}, f32[256,128]{1,0:T(8,128)S(1)}, f32[256,128]{1,0:T(8,128)S(1)}, f32[256,128]{1,0:T(8,128)S(1)}, f32[128,128]{1,0:T(8,128)S(1)}) custom-call(f32[32,4,16,128]{3,2,1,0:T(8,128)S(1)} %get-tuple-element.39.species, f32[80,128]{1,0:T(8,128)S(1)} %pad_maximum_fusion.refs_0_, ...), custom_call_target="tpu_custom_call" | custom-call | flops 1 | bytes 67108864 | tf_op jit(solution)/shard_map/pallas_call | solution.py:419
  19.5 0.0 copy-start.7
  19.5 1.4 %collective-permute-start.7 = (f32[256,128]{1,0:T(8,128)S(1)}, f32[256,128]{1,0:T(8,128)S(1)}, u32[]{:S(2)}, u32[]{:S(2)}) collective-permute-start(f32[256,128]{1,0:T(8,128)S(1)} %get-tuple-element.51), channel_id=1, source_target_pairs={{0,8},{8,0},{16,24},{24,16},{1,9},{9,1},{17,25},{25,17},{2,10},{10... | collective-permute-start | bytes 393224 | tf_op jit(solution)/shard_map/ppermute | solution.py:76
  20.9 0.7 %collective-permute-start.8 = (f32[256,128]{1,0:T(8,128)S(1)}, f32[256,128]{1,0:T(8,128)S(1)}, u32[]{:S(2)}, u32[]{:S(2)}) collective-permute-start(f32[256,128]{1,0:T(8,128)S(1)} %get-tuple-element.52), channel_id=1, source_target_pairs={{0,16},{8,24},{16,0},{24,8},{1,17},{9,25},{17,1},{25,9},{2,18},{10... | collective-permute-start | bytes 393224 | tf_op jit(solution)/shard_map/ppermute | solution.py:76
  21.7 0.0 collective-permute-done.15
  21.7 1.4 %collective-permute-start.9 = (f32[256,128]{1,0:T(8,128)S(1)}, f32[256,128]{1,0:T(8,128)S(1)}, u32[]{:S(2)}, u32[]{:S(2)}) collective-permute-start(f32[256,128]{1,0:T(8,128)S(1)} %get-tuple-element.53), channel_id=1, source_target_pairs={{0,24},{8,16},{16,8},{24,0},{1,25},{9,17},{17,9},{25,1},{2,26},{10... | collective-permute-start | bytes 393224 | tf_op jit(solution)/shard_map/ppermute | solution.py:76
  23.1 1.1 %collective-permute-done.13 = f32[256,128]{1,0:T(8,128)S(1)} collective-permute-done((f32[256,128]{1,0:T(8,128)S(1)}, f32[256,128]{1,0:T(8,128)S(1)}, u32[]{:S(2)}, u32[]{:S(2)}) %collective-permute-start.13) | collective-permute-done | bytes 131104 | tf_op jit(solution)/shard_map/ppermute | solution.py:76
  24.1 0.0 collective-permute-done.14
  24.2 0.8 %shard_map.133 = (f32[256,128]{1,0:T(8,128)S(1)}, f32[256,128]{1,0:T(8,128)S(1)}, f32[256,128]{1,0:T(8,128)S(1)}, f32[256,128]{1,0:T(8,128)S(1)}, f32[8,128]{1,0:T(8,128)S(1)}) custom-call(f32[8,32,128]{2,1,0:T(8,128)S(1)} %bitcast.34, f32[8,32,128]{2,1,0:T(8,128)S(1)} %bitcast.39, f32[8,32,128]{2,1,0:T(8,128)S(1)} %bitcast.40, f32[8,32,128]{2,1,0:T(8,128)S(1)} %bitcast.36, ...), custom_call_target="tpu_custom_call" | custom-call | flops 268435456 | bytes 2097152 | tf_op jit(solution)/shard_map/pallas_call | solution.py:432
  25.0 0.8 %collective-permute-start.16 = (f32[256,128]{1,0:T(8,128)S(1)}, f32[256,128]{1,0:T(8,128)S(1)}, u32[]{:S(2)}, u32[]{:S(2)}) collective-permute-start(f32[256,128]{1,0:T(8,128)S(1)} %get-tuple-element.64), channel_id=1, source_target_pairs={{0,8},{8,0},{16,24},{24,16},{1,9},{9,1},{17,25},{25,17},{2,10},{10... | collective-permute-start | bytes 393224 | tf_op jit(solution)/shard_map/ppermute | solution.py:76
  25.8 1.1 %collective-permute-start.17 = (f32[256,128]{1,0:T(8,128)S(1)}, f32[256,128]{1,0:T(8,128)S(1)}, u32[]{:S(2)}, u32[]{:S(2)}) collective-permute-start(f32[256,128]{1,0:T(8,128)S(1)} %get-tuple-element.65), channel_id=1, source_target_pairs={{0,16},{8,24},{16,0},{24,8},{1,17},{9,25},{17,1},{25,9},{2,18},{10... | collective-permute-start | bytes 393224 | tf_op jit(solution)/shard_map/ppermute | solution.py:76
  26.9 0.1 collective-permute-done.7
  26.9 1.6 %collective-permute-start.18 = (f32[256,128]{1,0:T(8,128)S(1)}, f32[256,128]{1,0:T(8,128)S(1)}, u32[]{:S(2)}, u32[]{:S(2)}) collective-permute-start(f32[256,128]{1,0:T(8,128)S(1)} %get-tuple-element.66), channel_id=1, source_target_pairs={{0,24},{8,16},{16,8},{24,0},{1,25},{9,17},{17,9},{25,1},{2,26},{10... | collective-permute-start | bytes 393224 | tf_op jit(solution)/shard_map/ppermute | solution.py:76
  28.5 1.1 %collective-permute-done.9 = f32[256,128]{1,0:T(8,128)S(1)} collective-permute-done((f32[256,128]{1,0:T(8,128)S(1)}, f32[256,128]{1,0:T(8,128)S(1)}, u32[]{:S(2)}, u32[]{:S(2)}) %collective-permute-start.9) | collective-permute-done | bytes 131104 | tf_op jit(solution)/shard_map/ppermute | solution.py:76
  29.7 0.8 %shard_map.132 = (f32[256,128]{1,0:T(8,128)S(1)}, f32[256,128]{1,0:T(8,128)S(1)}, f32[256,128]{1,0:T(8,128)S(1)}, f32[256,128]{1,0:T(8,128)S(1)}, f32[8,128]{1,0:T(8,128)S(1)}) custom-call(f32[8,32,128]{2,1,0:T(8,128)S(1)} %bitcast.33, f32[8,32,128]{2,1,0:T(8,128)S(1)} %bitcast.35, f32[8,32,128]{2,1,0:T(8,128)S(1)} %bitcast.37, f32[8,32,128]{2,1,0:T(8,128)S(1)} %bitcast.38, ...), custom_call_target="tpu_custom_call" | custom-call | flops 268435456 | bytes 2097152 | tf_op jit(solution)/shard_map/pallas_call | solution.py:432
  30.5 0.0 copy-start
  30.5 0.8 %collective-permute-start.10 = (f32[256,128]{1,0:T(8,128)S(1)}, f32[256,128]{1,0:T(8,128)S(1)}, u32[]{:S(2)}, u32[]{:S(2)}) collective-permute-start(f32[256,128]{1,0:T(8,128)S(1)} %get-tuple-element.56), channel_id=1, source_target_pairs={{0,8},{8,0},{16,24},{24,16},{1,9},{9,1},{17,25},{25,17},{2,10},{10... | collective-permute-start | bytes 393224 | tf_op jit(solution)/shard_map/ppermute | solution.py:76
  31.3 1.6 %collective-permute-start.11 = (f32[256,128]{1,0:T(8,128)S(1)}, f32[256,128]{1,0:T(8,128)S(1)}, u32[]{:S(2)}, u32[]{:S(2)}) collective-permute-start(f32[256,128]{1,0:T(8,128)S(1)} %get-tuple-element.57), channel_id=1, source_target_pairs={{0,16},{8,24},{16,0},{24,8},{1,17},{9,25},{17,1},{25,9},{2,18},{10... | collective-permute-start | bytes 393224 | tf_op jit(solution)/shard_map/ppermute | solution.py:76
  32.8 0.0 collective-permute-done.16
  32.8 1.2 %collective-permute-start.12 = (f32[256,128]{1,0:T(8,128)S(1)}, f32[256,128]{1,0:T(8,128)S(1)}, u32[]{:S(2)}, u32[]{:S(2)}) collective-permute-start(f32[256,128]{1,0:T(8,128)S(1)} %get-tuple-element.58), channel_id=1, source_target_pairs={{0,24},{8,16},{16,8},{24,0},{1,25},{9,17},{17,9},{25,1},{2,26},{10... | collective-permute-start | bytes 393224 | tf_op jit(solution)/shard_map/ppermute | solution.py:76
  34.1 0.7 %shard_map.136 = (f32[1,16,128]{2,1,0:T(8,128)}, f32[1,16,128]{2,1,0:T(8,128)}, f32[1,16,128]{2,1,0:T(8,128)}) custom-call(f32[1,16,128]{2,1,0:T(8,128)S(1)} %copy-done.2, f32[1,16,128]{2,1,0:T(8,128)S(1)} %copy-done.1, f32[1,16,128]{2,1,0:T(8,128)S(1)} %copy-done, f32[1,16,128]{2,1,0:T(8,128)S(1)} %copy-done.3, f32[64,128]{1,0:T(8,128)S(1)} %collective-permute-done.refs_0_, ...), custom_call_target="tpu_custom_call" | custom-call | flops 1 | bytes 1 | tf_op jit(solution)/shard_map/pallas_call | solution.py:469
  34.8 0.0 collective-permute-done.17
  34.8 0.5 %collective-permute-done.18 = f32[256,128]{1,0:T(8,128)S(1)} collective-permute-done((f32[256,128]{1,0:T(8,128)S(1)}, f32[256,128]{1,0:T(8,128)S(1)}, u32[]{:S(2)}, u32[]{:S(2)}) %collective-permute-start.18) | collective-permute-done | bytes 131104 | tf_op jit(solution)/shard_map/ppermute | solution.py:76
  35.3 0.8 %shard_map.134.refs_4_ = f32[32,4,16,128]{3,2,1,0:T(8,128)} custom-call(f32[32,8,128]{2,1,0:T(8,128)S(1)} %bitcast.21, f32[32,8,128]{2,1,0:T(8,128)S(1)} %bitcast.22, f32[32,8,128]{2,1,0:T(8,128)S(1)} %bitcast.23, f32[32,8,128]{2,1,0:T(8,128)S(1)} %bitcast.24), custom_call_target="tpu_custom_call" | custom-call | flops 1 | bytes 1048576 | tf_op jit(solution)/shard_map/pallas_call | solution.py:450
  36.1 2.0 %collective-permute-done.10 = f32[256,128]{1,0:T(8,128)S(1)} collective-permute-done((f32[256,128]{1,0:T(8,128)S(1)}, f32[256,128]{1,0:T(8,128)S(1)}, u32[]{:S(2)}, u32[]{:S(2)}) %collective-permute-start.10) | collective-permute-done | bytes 131104 | tf_op jit(solution)/shard_map/ppermute | solution.py:76
  38.2 2.3 %collective-permute-done.12 = f32[256,128]{1,0:T(8,128)S(1)} collective-permute-done((f32[256,128]{1,0:T(8,128)S(1)}, f32[256,128]{1,0:T(8,128)S(1)}, u32[]{:S(2)}, u32[]{:S(2)}) %collective-permute-start.12) | collective-permute-done | bytes 131104 | tf_op jit(solution)/shard_map/ppermute | solution.py:76
  40.5 0.8 %shard_map.135 = f32[32,4,16,128]{3,2,1,0:T(8,128)} custom-call(f32[32,8,128]{2,1,0:T(8,128)S(1)} %bitcast.25, f32[32,8,128]{2,1,0:T(8,128)S(1)} %bitcast.26, f32[32,8,128]{2,1,0:T(8,128)S(1)} %bitcast.27, f32[32,8,128]{2,1,0:T(8,128)S(1)} %bitcast.28, f32[32,4,16,128]{3,2,1,0:T(8,128)} %shard_map.134.refs_4_), custom_call_target="tpu_custom_call", output_to_operand_aliasing={{}: (4, {})} | custom-call | flops 1 | bytes 1048576 | tf_op jit(solution)/shard_map/pallas_call | solution.py:450
  (25 shorter events, 0.1 us)
Async XLA Ops:
  1.4 1.3 %collective-permute-start = (f32[64,128]{1,0:T(8,128)S(1)}, f32[64,128]{1,0:T(8,128)S(1)}, u32[]{:S(2)}, u32[]{:S(2)}) collective-permute-start(f32[64,128]{1,0:T(8,128)S(1)} %pad_maximum_fusion.1), channel_id=1, source_target_pairs={{0,1},{1,0},{2,3},{3,2},{4,5},{5,4},{6,7},{7,6},{8,9},{9,8},{10,11... | collective-permute-start | bytes 98312 | tf_op jit(solution)/shard_map/ppermute | solution.py:56
  2.7 6.1 %collective-permute-start.3 = (f32[80,128]{1,0:T(8,128)S(1)}, f32[80,128]{1,0:T(8,128)S(1)}, u32[]{:S(2)}, u32[]{:S(2)}) collective-permute-start(f32[80,128]{1,0:T(8,128)S(1)} %pad_maximum_fusion.refs_0_), channel_id=1, source_target_pairs={{0,24},{8,16},{16,8},{24,0},{1,25},{9,17},{17,9},{25,1},{2,26},{10... | collective-permute-start | bytes 122888 | tf_op jit(solution)/shard_map/ppermute | solution.py:76
  6.5 4.0 %collective-permute-start.2 = (f32[80,128]{1,0:T(8,128)S(1)}, f32[80,128]{1,0:T(8,128)S(1)}, u32[]{:S(2)}, u32[]{:S(2)}) collective-permute-start(f32[80,128]{1,0:T(8,128)S(1)} %pad_maximum_fusion.refs_0_), channel_id=1, source_target_pairs={{0,16},{8,24},{16,0},{24,8},{1,17},{9,25},{17,1},{25,9},{2,18},{10... | collective-permute-start | bytes 122888 | tf_op jit(solution)/shard_map/ppermute | solution.py:76
  7.0 4.0 %collective-permute-start.1 = (f32[80,128]{1,0:T(8,128)S(1)}, f32[80,128]{1,0:T(8,128)S(1)}, u32[]{:S(2)}, u32[]{:S(2)}) collective-permute-start(f32[80,128]{1,0:T(8,128)S(1)} %pad_maximum_fusion.refs_0_), channel_id=1, source_target_pairs={{0,8},{8,0},{16,24},{24,16},{1,9},{9,1},{17,25},{25,17},{2,10},{10... | collective-permute-start | bytes 122888 | tf_op jit(solution)/shard_map/ppermute | solution.py:76
  8.8 2.3 %collective-permute-start.4 = (f32[16,128]{1,0:T(8,128)S(1)}, f32[16,128]{1,0:T(8,128)S(1)}, u32[]{:S(2)}, u32[]{:S(2)}) collective-permute-start(f32[16,128]{1,0:T(8,128)S(1)} %get-tuple-element.42), channel_id=1, source_target_pairs={{0,1},{1,0},{2,3},{3,2},{4,5},{5,4},{6,7},{7,6},{8,9},{9,8},{10,11... | collective-permute-start | bytes 24584 | tf_op jit(solution)/shard_map/ppermute | solution.py:56
  11.1 4.6 %collective-permute-start.5 = (f32[136,128]{1,0:T(8,128)S(1)}, f32[136,128]{1,0:T(8,128)S(1)}, u32[]{:S(2)}, u32[]{:S(2)}) collective-permute-start(f32[136,128]{1,0:T(8,128)S(1)} %get-tuple-element.46), channel_id=1, source_target_pairs={{0,2},{2,0},{4,6},{6,4},{1,3},{3,1},{5,7},{7,5},{8,10},{10,8},{12,... | collective-permute-start | bytes 208904 | tf_op jit(solution)/shard_map/ppermute | solution.py:71
  12.7 3.0 %collective-permute-start.6 = (f32[136,128]{1,0:T(8,128)S(1)}, f32[136,128]{1,0:T(8,128)S(1)}, u32[]{:S(2)}, u32[]{:S(2)}) collective-permute-start(f32[136,128]{1,0:T(8,128)S(1)} %get-tuple-element.47), channel_id=1, source_target_pairs={{0,1},{1,0},{2,4},{3,5},{4,2},{5,3},{6,7},{7,6},{8,9},{9,8},{10,12... | collective-permute-start | bytes 208904 | tf_op jit(solution)/shard_map/ppermute | solution.py:72
  14.0 7.7 %collective-permute-start.15 = (f32[256,128]{1,0:T(8,128)S(1)}, f32[256,128]{1,0:T(8,128)S(1)}, u32[]{:S(2)}, u32[]{:S(2)}) collective-permute-start(f32[256,128]{1,0:T(8,128)S(1)} %get-tuple-element.62), channel_id=1, source_target_pairs={{0,24},{8,16},{16,8},{24,0},{1,25},{9,17},{17,9},{25,1},{2,26},{10... | collective-permute-start | bytes 393224 | tf_op jit(solution)/shard_map/ppermute | solution.py:76
  15.7 8.4 %collective-permute-start.13 = (f32[256,128]{1,0:T(8,128)S(1)}, f32[256,128]{1,0:T(8,128)S(1)}, u32[]{:S(2)}, u32[]{:S(2)}) collective-permute-start(f32[256,128]{1,0:T(8,128)S(1)} %get-tuple-element.60), channel_id=1, source_target_pairs={{0,8},{8,0},{16,24},{24,16},{1,9},{9,1},{17,25},{25,17},{2,10},{10... | collective-permute-start | bytes 393224 | tf_op jit(solution)/shard_map/ppermute | solution.py:76
  17.0 7.1 %collective-permute-start.14 = (f32[256,128]{1,0:T(8,128)S(1)}, f32[256,128]{1,0:T(8,128)S(1)}, u32[]{:S(2)}, u32[]{:S(2)}) collective-permute-start(f32[256,128]{1,0:T(8,128)S(1)} %get-tuple-element.61), channel_id=1, source_target_pairs={{0,16},{8,24},{16,0},{24,8},{1,17},{9,25},{17,1},{25,9},{2,18},{10... | collective-permute-start | bytes 393224 | tf_op jit(solution)/shard_map/ppermute | solution.py:76
  17.7 0.7 %copy-start.4 = (f32[128]{0:T(128)S(1)}, f32[128]{0:T(128)}, u32[]{:S(2)}) copy-start(f32[128]{0:T(128)} %param.19) | copy-start | bytes 1540
  18.4 5.8 %copy-start.5 = (bf16[512,128]{1,0:T(8,128)(2,1)S(1)}, bf16[512,128]{1,0:T(8,128)(2,1)}, u32[]{:S(2)}) copy-start(bf16[512,128]{1,0:T(8,128)(2,1)} %refs_6_.3) | copy-start | bytes 393220
  18.4 5.8 %copy-start.6 = (bf16[128,512]{1,0:T(8,128)(2,1)S(1)}, bf16[128,512]{1,0:T(8,128)(2,1)}, u32[]{:S(2)}) copy-start(bf16[128,512]{1,0:T(8,128)(2,1)} %refs_7_.3) | copy-start | bytes 393220
  19.5 4.6 %copy-start.7 = (s32[16,128]{1,0:T(8,128)S(1)}, s32[16,128]{1,0:T(8,128)}, u32[]{:S(2)}) copy-start(s32[16,128]{1,0:T(8,128)} %refs_5_.3) | copy-start | bytes 24580
  19.5 7.4 %collective-permute-start.7 = (f32[256,128]{1,0:T(8,128)S(1)}, f32[256,128]{1,0:T(8,128)S(1)}, u32[]{:S(2)}, u32[]{:S(2)}) collective-permute-start(f32[256,128]{1,0:T(8,128)S(1)} %get-tuple-element.51), channel_id=1, source_target_pairs={{0,8},{8,0},{16,24},{24,16},{1,9},{9,1},{17,25},{25,17},{2,10},{10... | collective-permute-start | bytes 393224 | tf_op jit(solution)/shard_map/ppermute | solution.py:76
  20.9 7.6 %collective-permute-start.8 = (f32[256,128]{1,0:T(8,128)S(1)}, f32[256,128]{1,0:T(8,128)S(1)}, u32[]{:S(2)}, u32[]{:S(2)}) collective-permute-start(f32[256,128]{1,0:T(8,128)S(1)} %get-tuple-element.52), channel_id=1, source_target_pairs={{0,16},{8,24},{16,0},{24,8},{1,17},{9,25},{17,1},{25,9},{2,18},{10... | collective-permute-start | bytes 393224 | tf_op jit(solution)/shard_map/ppermute | solution.py:76
  21.7 8.0 %collective-permute-start.9 = (f32[256,128]{1,0:T(8,128)S(1)}, f32[256,128]{1,0:T(8,128)S(1)}, u32[]{:S(2)}, u32[]{:S(2)}) collective-permute-start(f32[256,128]{1,0:T(8,128)S(1)} %get-tuple-element.53), channel_id=1, source_target_pairs={{0,24},{8,16},{16,8},{24,0},{1,25},{9,17},{17,9},{25,1},{2,26},{10... | collective-permute-start | bytes 393224 | tf_op jit(solution)/shard_map/ppermute | solution.py:76
  25.0 7.9 %collective-permute-start.16 = (f32[256,128]{1,0:T(8,128)S(1)}, f32[256,128]{1,0:T(8,128)S(1)}, u32[]{:S(2)}, u32[]{:S(2)}) collective-permute-start(f32[256,128]{1,0:T(8,128)S(1)} %get-tuple-element.64), channel_id=1, source_target_pairs={{0,8},{8,0},{16,24},{24,16},{1,9},{9,1},{17,25},{25,17},{2,10},{10... | collective-permute-start | bytes 393224 | tf_op jit(solution)/shard_map/ppermute | solution.py:76
  25.8 9.0 %collective-permute-start.17 = (f32[256,128]{1,0:T(8,128)S(1)}, f32[256,128]{1,0:T(8,128)S(1)}, u32[]{:S(2)}, u32[]{:S(2)}) collective-permute-start(f32[256,128]{1,0:T(8,128)S(1)} %get-tuple-element.65), channel_id=1, source_target_pairs={{0,16},{8,24},{16,0},{24,8},{1,17},{9,25},{17,1},{25,9},{2,18},{10... | collective-permute-start | bytes 393224 | tf_op jit(solution)/shard_map/ppermute | solution.py:76
  26.9 8.3 %collective-permute-start.18 = (f32[256,128]{1,0:T(8,128)S(1)}, f32[256,128]{1,0:T(8,128)S(1)}, u32[]{:S(2)}, u32[]{:S(2)}) collective-permute-start(f32[256,128]{1,0:T(8,128)S(1)} %get-tuple-element.66), channel_id=1, source_target_pairs={{0,24},{8,16},{16,8},{24,0},{1,25},{9,17},{17,9},{25,1},{2,26},{10... | collective-permute-start | bytes 393224 | tf_op jit(solution)/shard_map/ppermute | solution.py:76
  29.7 4.4 %copy-start.1 = (f32[1,16,128]{2,1,0:T(8,128)S(1)}, f32[1,16,128]{2,1,0:T(8,128)}, u32[]{:S(2)}) copy-start(f32[1,16,128]{2,1,0:T(8,128)} %north.1) | copy-start | bytes 24580
  29.7 4.4 %copy-start.2 = (f32[1,16,128]{2,1,0:T(8,128)S(1)}, f32[1,16,128]{2,1,0:T(8,128)}, u32[]{:S(2)}) copy-start(f32[1,16,128]{2,1,0:T(8,128)} %east.1) | copy-start | bytes 24580
  29.7 4.4 %copy-start.3 = (f32[1,16,128]{2,1,0:T(8,128)S(1)}, f32[1,16,128]{2,1,0:T(8,128)}, u32[]{:S(2)}) copy-start(f32[1,16,128]{2,1,0:T(8,128)} %density.1) | copy-start | bytes 24580
  30.5 3.6 %copy-start = (f32[1,16,128]{2,1,0:T(8,128)S(1)}, f32[1,16,128]{2,1,0:T(8,128)}, u32[]{:S(2)}) copy-start(f32[1,16,128]{2,1,0:T(8,128)} %warmth.1) | copy-start | bytes 24580
  30.5 7.7 %collective-permute-start.10 = (f32[256,128]{1,0:T(8,128)S(1)}, f32[256,128]{1,0:T(8,128)S(1)}, u32[]{:S(2)}, u32[]{:S(2)}) collective-permute-start(f32[256,128]{1,0:T(8,128)S(1)} %get-tuple-element.56), channel_id=1, source_target_pairs={{0,8},{8,0},{16,24},{24,16},{1,9},{9,1},{17,25},{25,17},{2,10},{10... | collective-permute-start | bytes 393224 | tf_op jit(solution)/shard_map/ppermute | solution.py:76
  31.3 6.9 %collective-permute-start.11 = (f32[256,128]{1,0:T(8,128)S(1)}, f32[256,128]{1,0:T(8,128)S(1)}, u32[]{:S(2)}, u32[]{:S(2)}) collective-permute-start(f32[256,128]{1,0:T(8,128)S(1)} %get-tuple-element.57), channel_id=1, source_target_pairs={{0,16},{8,24},{16,0},{24,8},{1,17},{9,25},{17,1},{25,9},{2,18},{10... | collective-permute-start | bytes 393224 | tf_op jit(solution)/shard_map/ppermute | solution.py:76
  32.8 7.7 %collective-permute-start.12 = (f32[256,128]{1,0:T(8,128)S(1)}, f32[256,128]{1,0:T(8,128)S(1)}, u32[]{:S(2)}, u32[]{:S(2)}) collective-permute-start(f32[256,128]{1,0:T(8,128)S(1)} %get-tuple-element.58), channel_id=1, source_target_pairs={{0,24},{8,16},{16,8},{24,0},{1,25},{9,17},{17,9},{25,1},{2,26},{10... | collective-permute-start | bytes 393224 | tf_op jit(solution)/shard_map/ppermute | solution.py:76

commit v4 on v3

--- a/solution.py
+++ b/solution.py
@@ -111,10 +111,11 @@
             ]
         for at in range(n_lon):
             edge = jnp.where(parity("lon") == at, width - 1, 0)
-            for place in range(part * held, (part + 1) * held):
-                block = species[place // strata, place % strata]
-                turned = pltpu.roll(block, lax.rem(place - edge + width, width), 1)
-                columns[at] = jnp.where(lane == place, turned, columns[at])
+            for t in range(part * share, (part + 1) * share):
+                for level in range(strata):
+                    place = level * tracers + t
+                    turned = pltpu.roll(species[t, level], lax.rem(place - edge + width, width), 1)
+                    columns[at] = jnp.where(lane == place, turned, columns[at])
     for message, block in zip(outs[:n_lon], columns):
         message[...] = block
 
@@ -162,35 +163,18 @@
     return jnp.maximum(wind, 0.0), jnp.minimum(wind, 0.0)
 
 
-def transport_kernel(chunk, n_lon, n_lat, slots, species, *refs):
-    refs = list(refs)
-    winds = [refs.pop(0) for _ in range(slots)]
-    lon_in = [refs.pop(0) for _ in range(n_lon)]
-    lat_in = [refs.pop(0) for _ in range(n_lat)] if chunk else []
-    if chunk:
-        yields = refs.pop(0)
-    outs = [refs.pop(0) for _ in range(slots)]
-    if chunk:
-        weight = refs.pop(0)
-        weight[...] = jnp.broadcast_to(yields[...], weight.shape[::-1]).T
-    upward = refs.pop(0)
-    tracers, strata, rows, width = species.shape
-    half = rows // 2
-    quarter = rows // 4
-    base = tracers * strata
-    me, lon_even = lax.axis_index("group"), parity("lon") == 0
-    pick = ends if chunk else middle
-    lane = lane_ids((half, width))
-    row = row_ids((half, width))
+def coefficients(winds, lon_fields, upward, lat_in, base, pick):
+    slots, n_lon = len(winds), len(lon_fields)
+    strata, rows, width = upward.shape
+    me = lax.axis_index("group")
     for slot in range(slots):
         upward[me ^ slot] = winds[slot][2 * rows:3 * rows]
-
-    coefficients = []
+    found = []
     for slot in range(slots):
         level = me ^ slot
         east = winds[slot][0:rows]
         east_last, east_next = beside(
-            east, "lon", [winds[slot][at:at + rows] for at in range(4 * rows, (4 + n_lon) * rows, rows)]
+            east, "lon", [m[slot * rows:(slot + 1) * rows] for m in lon_fields]
         )
         north = winds[slot][rows:2 * rows]
         rim = [m[base + slot:base + slot + 1] for m in lat_in] or [jnp.zeros((1, width), F32)]
@@ -209,24 +193,54 @@
         stay = 1.0 - (
             (east_out - west_out) + (north_out - south_out) + (up_out - down_out)
         )
-        stay, east_in, west_in, north_in, south_in, up_in, down_in = [
-            pick(f) for f in (stay, -east_in, west_in, -north_in, south_in, -up_in, down_in)
-        ]
         if n_lon < 2:
-            east_in = jnp.where((lane == width - 1) & ~lon_even, 0.0, east_in)
-            west_in = jnp.where((lane == 0) & lon_even, 0.0, west_in)
-        coefficients.append((stay, east_in, west_in, north_in, south_in, up_in, down_in))
-
-    columns = [pick(m[0:rows]) for m in lon_in]
+            lane, even = lane_ids((rows, width)), parity("lon") == 0
+            east_in = jnp.where((lane == width - 1) & ~even, 0.0, east_in)
+            west_in = jnp.where((lane == 0) & even, 0.0, west_in)
+        found.append(
+            [pick(f) for f in (stay, -east_in, west_in, -north_in, south_in, -up_in, down_in)]
+        )
+    return found
+
+
+def combine(coefficient, here, east, west, north, south, up, down):
+    stay, east_in, west_in, north_in, south_in, up_in, down_in = coefficient
+    return (
+        (stay * here + east_in * east)
+        + (west_in * west + north_in * north)
+        + (south_in * south + up_in * up)
+        + down_in * down
+    )
+
+
+def weight_kernel(yields, weight):
+    weight[...] = jnp.broadcast_to(yields[...], weight.shape[::-1]).T
+
+
+def ends_kernel(n_lon, n_lat, slots, species, *refs):
+    refs = list(refs)
+    winds = [refs.pop(0) for _ in range(slots)]
+    lon_fields = [refs.pop(0) for _ in range(n_lon)]
+    lon_in = [refs.pop(0) for _ in range(n_lon)]
+    lat_in = [refs.pop(0) for _ in range(n_lat)]
+    outs = [refs.pop(0) for _ in range(slots)]
+    upward = refs.pop(0)
+    tracers, strata, rows, width = species.shape
+    half = rows // 2
+    quarter = rows // 4
+    me = lax.axis_index("group")
+    lane = lane_ids((half, width))
+    row = row_ids((half, width))
+    found = coefficients(winds, lon_fields, upward, lat_in, tracers * strata, ends)
+    columns = [ends(m[0:rows]) for m in lon_in]
     if n_lon == 2:
         columns = both_sides("lon", columns)
-    edge = jnp.where(lon_even, width - 1, 0)
+    edge = jnp.where(parity("lon") == 0, width - 1, 0)
 
     def one(t, carry):
         for slot in range(slots):
             level = me ^ slot
-            stay, east_in, west_in, north_in, south_in, up_in, down_in = coefficients[slot]
-            place = t * strata + level
+            place = level * tracers + t
             if n_lon == 2:
                 low = pltpu.roll(columns[0], lax.rem(width - place, width), 1)
                 high = pltpu.roll(columns[1], width - 1 - place, 1)
@@ -234,56 +248,258 @@
                 low = high = pltpu.roll(columns[0], lax.rem(width + edge - place, width), 1)
             above = jnp.minimum(level + 1, strata - 1)
             below = jnp.maximum(level - 1, 0)
-            if chunk:
-                first, last = species[t, level, 0:half], species[t, level, half:rows]
-                here = jnp.where(row < quarter, first, last)
-                low_row, high_row = both_sides("lat", [m[pl.ds(place, 1), :] for m in lat_in])
-                south = pltpu.roll(jnp.where(row < quarter - 1, first, last), 1, 0)
-                south = jnp.where(row == 0, low_row, south)
-                north = pltpu.roll(jnp.where(row < quarter + 1, first, last), half - 1, 0)
-                north = jnp.where(row == half - 1, high_row, north)
-                up = jnp.where(
-                    row < quarter, species[t, above, 0:half], species[t, above, half:rows]
-                )
-                down = jnp.where(
-                    row < quarter, species[t, below, 0:half], species[t, below, half:rows]
-                )
-            else:
-                here = species[t, level, quarter:3 * quarter]
-                south = species[t, level, quarter - 1:3 * quarter - 1]
-                north = species[t, level, quarter + 1:3 * quarter + 1]
-                up = species[t, above, quarter:3 * quarter]
-                down = species[t, below, quarter:3 * quarter]
+            first, last = species[t, level, 0:half], species[t, level, half:rows]
+            here = jnp.where(row < quarter, first, last)
+            place = t * strata + level
+            low_row, high_row = both_sides("lat", [m[pl.ds(place, 1), :] for m in lat_in])
+            south = pltpu.roll(jnp.where(row < quarter - 1, first, last), 1, 0)
+            south = jnp.where(row == 0, low_row, south)
+            north = pltpu.roll(jnp.where(row < quarter + 1, first, last), half - 1, 0)
+            north = jnp.where(row == half - 1, high_row, north)
+            up = jnp.where(row < quarter, species[t, above, 0:half], species[t, above, half:rows])
+            down = jnp.where(row < quarter, species[t, below, 0:half], species[t, below, half:rows])
             east = jnp.where(lane == width - 1, high, pltpu.roll(here, width - 1, 1))
             west = jnp.where(lane == 0, low, pltpu.roll(here, 1, 1))
-            value = (
-                (stay * here + east_in * east)
-                + (west_in * west + north_in * north)
-                + (south_in * south + up_in * up)
-                + down_in * down
+            outs[slot][pl.ds(t, half, stride=tracers), :] = combine(
+                found[slot], here, east, west, north, south, up, down
             )
-            outs[slot][pl.ds(t, half, stride=tracers), :] = value
         return carry
 
-    lax.fori_loop(0, tracers, one, 0, unroll=8)
-
-
-def chemistry_kernel(chunk, slots, *refs):
+    lax.fori_loop(0, tracers, one, 0, unroll=tracers)
+
+
+def strip_lanes(value, shift):
+    width = value.shape[-1]
+    return pltpu.roll(value, lax.rem(shift + 2 * width, width), 1)
+
+
+def strip_of(turned, owner, strip, around=0):
+    lane = lane_ids(turned[0].shape)
+    block = lane // strip
+    if around:
+        block = jnp.where(lax.rem(lane, strip) == 0, block + len(turned) - 1, block + 1)
+        block = lax.rem(block, len(turned))
+    packed = turned[0]
+    for level in range(1, len(turned)):
+        packed = jnp.where(block == lax.rem(owner + level, len(turned)), turned[level], packed)
+    return packed
+
+
+def strip_kernel(slots, species, *outs):
+    tracers, strata, rows, width = species.shape
+    half, quarter = rows // 2, rows // 4
+    strip = width // slots
+    me = lax.axis_index("group")
+    flat = species.reshape(tracers * strata * rows, width)
+
+    def one(t, carry):
+        turned = [
+            strip_lanes(species[t, level, quarter:3 * quarter], strip * level)
+            for level in range(strata)
+        ]
+        for slot in range(slots):
+            outs[slot][pl.ds(pl.multiple_of(t * half, half), half), :] = strip_of(
+                turned, me ^ slot, strip
+            )
+        return carry
+
+    lax.fori_loop(0, tracers, one, 0, unroll=tracers)
+    for at, line in enumerate((quarter - 1, 3 * quarter)):
+        for group in range(tracers // half):
+            turned = [
+                strip_lanes(
+                    flat[pl.ds((group * half * strata + level) * rows + line, half, stride=strata * rows), :],
+                    strip * level,
+                )
+                for level in range(strata)
+            ]
+            base = tracers * (half + at) + group * half
+            for slot in range(slots):
+                outs[slot][base:base + half] = strip_of(turned, me ^ slot, strip)
+
+
+def strip_rim_kernel(slots, species, *refs):
+    strips, outs = refs[:slots], refs[slots:]
+    tracers, strata, rows, width = species.shape
+    half, quarter = rows // 2, rows // 4
+    strip = width // slots
+    share = strip // 2
+    me = lax.axis_index("group")
+    lane = lane_ids((half, width))
+    done = tracers * (half + 2)
+    for slot in range(slots):
+        outs[slot][0:done] = strips[slot][...]
+    for part in range(tracers // share):
+
+        def one(i, rims):
+            t = part * share + i
+            turned = [
+                strip_lanes(species[t, level, quarter:3 * quarter], strip * level)
+                for level in range(strata)
+            ]
+            new = []
+            for slot in range(slots):
+                owner = me ^ slot
+                rim = strip_of(turned, owner, strip, 1)
+                rim = pltpu.roll(rim, 2 * i, 1)
+                mine = lax.rem(lane - 2 * i + 1 + width, strip) < 2
+                new.append(jnp.where(mine, rim, rims[slot]))
+            return tuple(new)
+
+        rims = lax.fori_loop(
+            0, share, one, tuple(jnp.zeros((half, width), F32) for _ in range(slots)), unroll=8
+        )
+        for slot in range(slots):
+            outs[slot][done + part * half:done + (part + 1) * half] = rims[slot]
+
+
+def strip_edge_kernel(n_lon, slots, *refs):
     refs = list(refs)
-    advected = [refs.pop(0) for _ in range(slots)]
-    warmth, counts, companion, stoichiometry, weight = [refs.pop(0) for _ in range(5)]
+    lon_in = [refs.pop(0) for _ in range(n_lon)]
+    strips, outs = refs[:slots], refs[slots:]
+    rows, width = lon_in[0].shape
+    half = rows // 2
+    strip = width // slots
+    share = strip // 2
+    me = lax.axis_index("group")
+    lane = lane_ids((half, width))
+    columns = [middle(m[...]) for m in lon_in]
+    if n_lon == 2:
+        sides = list(zip(both_sides("lon", columns), (False, True)))
+    else:
+        sides = [(columns[0], parity("lon") == 0)]
+    parts = strip // share
+    done = outs[0].shape[0] - parts * half
+    for slot in range(slots):
+        outs[slot][0:done] = strips[slot][0:done]
+    for part in range(parts):
+        place = slice(done + part * half, done + (part + 1) * half)
+        rims = [strips[slot][place] for slot in range(slots)]
+        for column, high in sides:
+            beyond_edge = jnp.zeros((half, width), F32)
+            for i in range(share):
+                turned = strip_lanes(column, jnp.where(high, 0, -1) - (part * share + i) + 2 * i)
+                mine = lax.rem(lane - 2 * i + width, strip) == jnp.where(high, 0, strip - 1)
+                beyond_edge = jnp.where(mine, turned, beyond_edge)
+            lanes = lax.rem(lane, 2) == jnp.where(high, 0, 1)
+            for slot in range(slots):
+                at_edge = (me ^ slot) == jnp.where(high, slots - 1, 0)
+                rims[slot] = jnp.where(lanes & at_edge, beyond_edge, rims[slot])
+        for slot in range(slots):
+            outs[slot][place] = rims[slot]
+
+
+def by_level(values, me, strip):
+    block = lane_ids(values[0].shape) // strip
+    packed = strip_lanes(values[0], strip * me)
+    for slot in range(1, len(values)):
+        level = me ^ slot
+        turned = strip_lanes(values[slot], strip * level)
+        packed = jnp.where(block == lax.rem(me + level, len(values)), turned, packed)
+    return packed
+
+
+def strip_react_kernel(n_lon, slots, *refs):
+    refs = list(refs)
+    raw = [refs.pop(0) for _ in range(slots)]
+    winds = [refs.pop(0) for _ in range(slots)]
+    lon_fields = [refs.pop(0) for _ in range(n_lon)]
+    counts, companion, stoichiometry, weight = [refs.pop(0) for _ in range(4)]
     outs = [refs.pop(0) for _ in range(slots)]
-    heat, current = refs
-    half, owned, width = advected[0].shape
-    species = slots * owned
+    current, start, upward = refs
+    strata, rows, width = upward.shape
+    half, species = current.shape[:2]
+    owned = species // slots
+    strip = width // slots
+    share = strip // 2
+    me = lax.axis_index("group")
+    lane = lane_ids((half, width))
+    row = row_ids((half, width))
+    found = coefficients(winds, lon_fields, upward, [], 0, middle)
+    coefficient = [by_level(list(f), me, strip) for f in zip(*found)]
+    first = [(me ^ slot) * owned for slot in range(slots)]
+    flat = current.reshape(half * species, width)
+
+    def one(t, carry):
+        for slot in range(slots):
+            block = raw[slot]
+            here = block[pl.ds(pl.multiple_of(t * half, half), half), :]
+            part = owned * (half + 2) + t // share * half
+            rim = block[pl.ds(pl.multiple_of(part, half), half), :]
+            rim = pltpu.roll(rim, lax.rem(width - 2 * lax.rem(t, share), width), 1)
+            west = pltpu.roll(jnp.where(lax.rem(lane, strip) == strip - 1, rim, here), 1, 1)
+            east = pltpu.roll(jnp.where(lax.rem(lane, strip) == 0, rim, here), width - 1, 1)
+            south = jnp.where(row == 0, block[pl.ds(owned * half + t, 1), :], pltpu.roll(here, 1, 0))
+            north = jnp.where(
+                row == half - 1, block[pl.ds(owned * (half + 1) + t, 1), :], pltpu.roll(here, half - 1, 0)
+            )
+            up = pltpu.roll(here, width - strip, 1)
+            down = pltpu.roll(here, strip, 1)
+            value = combine(coefficient, here, east, west, north, south, up, down)
+            flat[pl.ds(first[slot] + t, half, stride=species), :] = value
+        return carry
+
+    lax.fori_loop(0, owned, one, 0, unroll=owned)
+    start[...] = current[...]
+    warmth = by_level([middle(w[3 * rows:4 * rows]) for w in winds], me, strip)
+    many = by_level([middle(counts[...])] * slots, me, strip)
+    react(current, warmth, many, companion, stoichiometry)
+    total = None
+    for slot in range(slots):
+        place = pl.ds(pl.multiple_of(first[slot], owned), owned)
+        final = current[:, place, :]
+        for r in range(half):
+            outs[slot][r * owned:(r + 1) * owned] = final[r]
+        part = jnp.sum(weight[place, :][None] * (final - start[:, place, :]), axis=1)
+        total = part if total is None else total + part
+    for slot in range(slots):
+        outs[slot][owned * half:owned * half + half] = total
+
+
+def strip_place_kernel(slots, *refs):
+    got = refs[:slots]
+    out, heat, stage, sems = refs[slots:]
+    tracers, strata, rows, width = out.shape
+    half, quarter = rows // 2, rows // 4
+    strip = width // slots
+    me = lax.axis_index("group")
+    lane = lane_ids((half, width))
+
+    def side_by_side(blocks, level):
+        whole = blocks[0]
+        for slot in range(1, slots):
+            at = lax.rem((me ^ slot) + level, slots)
+            whole = jnp.where(lane // strip == at, blocks[slot], whole)
+        return strip_lanes(whole, -strip * level)
+
+    def one(t, carry):
+        blocks = [g[pl.ds(t, half, stride=tracers), :] for g in got]
+        for level in range(strata):
+            stage[t, level] = side_by_side(blocks, level)
+        return carry
+
+    lax.fori_loop(0, tracers, one, 0, unroll=tracers)
+    copies = [
+        pltpu.make_async_copy(
+            stage.at[:, :, part * quarter:(part + 1) * quarter, :],
+            out.at[:, :, (1 + part) * quarter:(2 + part) * quarter, :],
+            sems.at[part],
+        )
+        for part in range(2)
+    ]
+    for copy in copies:
+        copy.start()
+    heat[...] = side_by_side([g[tracers * half:tracers * half + half] for g in got], me)
+    for copy in copies:
+        copy.wait()
+
+
+def react(current, warmth, counts, companion, stoichiometry):
+    half, species, width = current.shape
     repeats = companion.shape[0] // species
-    pick = ends if chunk else middle
-    place = [pl.ds(pl.multiple_of((lax.axis_index("group") ^ slot) * owned, owned), owned) for slot in range(slots)]
-    for slot in range(slots):
-        current[:, place[slot], :] = advected[slot][...]
     line = lambda field: jnp.concatenate([field[r:r + 1] for r in range(half)], axis=1)
-    rate = line(jax.nn.sigmoid(2.0 * pick(warmth[...])))
-    many = line(pick(counts[...]))
+    rate = line(jax.nn.sigmoid(2.0 * warmth))
+    many = line(counts)
 
     def substep(s, carry):
         now = jnp.concatenate([current[r] for r in range(half)], axis=1)
@@ -303,6 +519,22 @@
     deepest = jnp.max(many)
     substep(0, 0)
     lax.fori_loop(1, deepest, substep, 0)
+
+
+def chemistry_kernel(slots, *refs):
+    refs = list(refs)
+    advected = [refs.pop(0) for _ in range(slots)]
+    warmth, counts, companion, stoichiometry, weight = [refs.pop(0) for _ in range(5)]
+    outs = [refs.pop(0) for _ in range(slots)]
+    heat, current = refs
+    half, owned, width = advected[0].shape
+    place = [
+        pl.ds(pl.multiple_of((lax.axis_index("group") ^ slot) * owned, owned), owned)
+        for slot in range(slots)
+    ]
+    for slot in range(slots):
+        current[:, place[slot], :] = advected[slot][...]
+    react(current, ends(warmth[...]), ends(counts[...]), companion, stoichiometry)
     total = None
     for slot in range(slots):
         final = current[:, place[slot], :]
@@ -328,8 +560,8 @@
         return value + diffusion * laplace, east - west, north - south
 
     new_east, _, _ = around(east[0], 0, slots)
-    new_north, _, _ = around(north[0], 1, 0)
-    warmed, zonal, meridional = around(warmth[0], 3, slots + 1)
+    new_north, _, _ = around(north[0], slots, 0)
+    warmed, zonal, meridional = around(warmth[0], slots + 1, slots + 1)
     heating = jnp.concatenate(
         [heat_ends[:quarter], heat_middle[...], heat_ends[quarter:]], axis=0
     )
@@ -338,11 +570,10 @@
     temp_out[0] = warmed + heating / density[0]
 
 
-def place_kernel(chunk, slots, *refs):
+def place_kernel(slots, *refs):
     got, out, sems = refs[:slots], refs[-2], refs[-1]
     rows = out.shape[2]
     quarter = rows // 4
-    starts = (0, 3 * quarter) if chunk else (quarter, 2 * quarter)
     copies = [
         pltpu.make_async_copy(
             got[slot].at[:, part * quarter:(part + 1) * quarter, :],
@@ -350,7 +581,7 @@
             sems.at[slot, part],
         )
         for slot in range(slots)
-        for part, start in enumerate(starts)
+        for part, start in enumerate((0, 3 * quarter))
     ]
     for copy in copies:
         copy.start()
@@ -388,8 +619,6 @@
     )
     payload = lax.optimization_barrier(payload)
     east, north, warmth = payload[:rows], payload[rows:2 * rows], payload[3 * rows:]
-    lon_fields = neighbours([payload] * n_lon, "lon")
-    payload = jnp.concatenate([payload] + [m[:rows] for m in lon_fields], axis=0)
     gathered = {hop: partner_swap(payload, hop) for hop in range(slots - 1, 0, -1)}
     winds = [payload] + [gathered[hop] for hop in range(1, slots)]
 
@@ -401,9 +630,30 @@
         [HBM],
         scratch=[pltpu.SemaphoreType.DMA((4,))],
         limit=52 * 1024 * 1024,
-    )(lax.optimization_barrier((species_amounts, payload))[0])
+    )(species_amounts)
     species = packed[n_lon + n_lat]
     lon_in = neighbours(packed[:n_lon], "lon")
+    strip = width // slots
+    strips = call(
+        functools.partial(strip_kernel, slots),
+        [struct(tracers * (half + 2), width)] * slots,
+        [VMEM],
+        touched=64 * species_amounts.size,
+    )(species)
+    strips = call(
+        functools.partial(strip_rim_kernel, slots),
+        [struct(tracers * (half + 2) + tracers // (strip // 2) * half, width)] * slots,
+        [VMEM] * (1 + slots),
+        touched=64 * species_amounts.size,
+    )(species, *strips)
+    strips = call(
+        functools.partial(strip_edge_kernel, n_lon, slots),
+        [struct(*strips[0].shape)] * slots,
+        [VMEM] * (n_lon + slots),
+    )(*lon_in, *strips)
+    strips, winds[1] = lax.optimization_barrier((strips, winds[1]))
+    lon_fields = jnp.concatenate([w[:rows] for w in winds] + [north, warmth], axis=0)
+    lon_fields = neighbours([lon_fields] * n_lon, "lon")
     lat_out = []
     for at, m in enumerate(packed[n_lon:n_lon + n_lat]):
         top = parity("lat") == at
@@ -411,61 +661,63 @@
         lines = jnp.concatenate([jnp.where(top, f[rows - 1:], f[:1]) for f in lines], axis=0)
         lines = jnp.pad(lines, ((0, -lines.shape[0] % 8), (0, 0)))
         lat_out.append(jnp.concatenate([m, lines], axis=0))
-    lat_out, lon_in = lax.optimization_barrier((lat_out, lon_in))
+    lat_out, lon_fields = lax.optimization_barrier((lat_out, lon_fields))
     lat_in = lat_neighbours(lat_out)
-
-    def transport(chunk, lat_in=()):
-        more = [*lat_in, heat_yield[None]] if chunk else []
-        return call(
-            functools.partial(transport_kernel, chunk, n_lon, n_lat, slots),
-            [struct(half * tracers, width)] * slots + [struct(slots * tracers, width)] * chunk,
-            [VMEM] * (1 + slots + n_lon + len(more)),
-            scratch=[pltpu.VMEM((strata, rows, width), F32)],
-            touched=256 * species_amounts.size if chunk else 1,
-        )(species, *winds, *lon_in, *more)
 
     def swap_slots(blocks):
         swapped = {hop: partner_swap(blocks[hop], hop) for hop in range(slots - 1, 0, -1)}
         return [blocks[0]] + [swapped[hop] for hop in range(1, slots)]
 
-    def chemistry(chunk, advected):
-        got = call(
-            functools.partial(chemistry_kernel, chunk, slots),
-            [struct(tracers * half, width)] * slots + [struct(half, width)],
-            [VMEM] * (slots + 5),
-            scratch=[pltpu.VMEM((half, slots * tracers, width), F32)],
-            flops=4 * half * width * companion_species.size,
-            touched=8 * species_amounts.size,
-        )(
-            *[a.reshape(half, tracers, width) for a in advected],
-            warmth,
-            chemistry_iterations,
-            companion_species,
-            stoichiometric_rate,
-            weight,
-        )
-        return got[:slots], got[slots]
-
-    def put(chunk, blocks, partial):
-        return call(
-            functools.partial(place_kernel, chunk, slots),
-            struct(tracers, strata, rows, width),
-            [VMEM] * slots + [ANY] * len(partial),
-            out_specs=ANY,
-            scratch=[pltpu.SemaphoreType.DMA((slots, 2))],
-            aliases={slots: 0} if partial else {},
-            touched=4 * species_amounts.size,
-        )(*[b.reshape(tracers, half, width) for b in blocks], *partial)
-
-    mid = list(transport(0))
-    mid[1], mid[2], lat_in = lax.optimization_barrier((mid[1], mid[2], lat_in))
-    mid = swap_slots(mid)
-    *end, weight = transport(1, lat_in)
+    strips = swap_slots(strips)
+    weight = call(
+        weight_kernel, struct(slots * tracers, width), [VMEM], touched=256 * species_amounts.size
+    )(heat_yield[None])
+    weight, lat_in = lax.optimization_barrier((weight, lat_in))
+    adv = call(
+        functools.partial(ends_kernel, n_lon, n_lat, slots),
+        [struct(half * tracers, width)] * slots,
+        [VMEM] * (1 + slots + 2 * n_lon + n_lat),
+        scratch=[pltpu.VMEM((strata, rows, width), F32)],
+        touched=256 * species_amounts.size,
+    )(species, *winds, *lon_fields, *lon_in, *lat_in)
+    adv = swap_slots(adv)
+    reacted = call(
+        functools.partial(strip_react_kernel, n_lon, slots),
+        [struct(tracers * half + half, width)] * slots,
+        [VMEM] * (2 * slots + n_lon + 4),
+        scratch=[
+            pltpu.VMEM((half, slots * tracers, width), F32),
+            pltpu.VMEM((half, slots * tracers, width), F32),
+            pltpu.VMEM((strata, rows, width), F32),
+        ],
+        flops=4 * half * width * companion_species.size,
+        touched=8 * species_amounts.size,
+    )(*strips, *winds, *lon_fields, chemistry_iterations, companion_species, stoichiometric_rate, weight)
+    reacted = swap_slots(reacted)
+    *end, heat_end = call(
+        functools.partial(chemistry_kernel, slots),
+        [struct(tracers * half, width)] * slots + [struct(half, width)],
+        [VMEM] * (slots + 5),
+        scratch=[pltpu.VMEM((half, slots * tracers, width), F32)],
+        flops=4 * half * width * companion_species.size,
+        touched=8 * species_amounts.size,
+    )(
+        *[a.reshape(half, tracers, width) for a in adv],
+        warmth,
+        chemistry_iterations,
+        companion_species,
+        stoichiometric_rate,
+        weight,
+    )
     end = swap_slots(end)
-    mid, heat_mid = chemistry(0, mid)
-    mid = swap_slots(mid)
-    end, heat_end = chemistry(1, end)
-    end = swap_slots(end)
+    partial, heat_mid = call(
+        functools.partial(strip_place_kernel, slots),
+        [struct(tracers, strata, rows, width), struct(half, width)],
+        [VMEM] * slots,
+        out_specs=[ANY, VMEM],
+        scratch=[pltpu.VMEM((tracers, strata, half, width), F32), pltpu.SemaphoreType.DMA((2,))],
+        touched=4 * species_amounts.size,
+    )(*reacted)
     east_out, north_out, temp_out = call(
         functools.partial(dynamics_kernel, n_lon, n_lat, base, slots),
         [struct(1, rows, width)] * 3,
@@ -480,7 +732,15 @@
         heat_mid,
         heat_end,
     )
-    tracers_out = put(1, end, [put(0, mid, [])])
+    tracers_out = call(
+        functools.partial(place_kernel, slots),
+        struct(tracers, strata, rows, width),
+        [VMEM] * slots + [ANY],
+        out_specs=ANY,
+        scratch=[pltpu.SemaphoreType.DMA((slots, 2))],
+        aliases={slots: 0},
+        touched=4 * species_amounts.size,
+    )(*[b.reshape(tracers, half, width) for b in end], partial)
     return (tracers_out, east_out, north_out, temp_out)
 
 

time: 41.6 us -> 40.4 us (0.971)
  waiting for transfers between devices: 10.2 us -> 8.88 us
  Pallas kernels: 7.97 us -> 8.96 us
  local copies, waits for them, and re-layouts: 0.74 us -> 0.1 us
    ppermute x15, waiting for transfers between devices: 9.29 us -> 6.09 us  [partner_swap(): lax.ppermute(block, 'group', [(i, i ^ hop) for i in range(lax.axis_size('...]
    ppermute x1, waiting for transfers between devices: 0.01 us -> 2.61 us  [lat_neighbours(): first = lax.ppermute(messages[0], 'lat', even_pairs(rows))]
    pallas_call x6 -> x9, Pallas kernels: 5.66 us -> 6.65 us  [the longest x1 1.67 us: local(): call(functools.partial(strip_react_kernel, n_lon, slots), [struct(tracers...]
    ppermute x2, waiting for transfers between devices: 0.86 us -> 0.18 us  [neighbours(): lax.ppermute(m, axis, pairs)]
    unnamed x16 -> x21, local copies, waits for them, and re-layouts: 0.69 us -> 0.05 us
  transfers between devices with their start and end apart: 19 -> 19, of which waited for: 9 -> 6; matrix products, arithmetic and copies ran while one was open for 0% -> 0% of each run, Pallas kernels for 17% -> 20%
where the time goes in v4:
time: 40.4 us; the launch traced here: 40.1 us
  starting transfers between devices  20.5 us (51%)
  Pallas kernels  8.96 us (22%)
  waiting for transfers between devices  8.88 us (22%)
  between operations  0.89 us (2%)
  other arithmetic  0.79 us (2%)
    ppermute x15, starting transfers between devices, partner_swap(): lax.ppermute(block, 'group', [(i, i ^ hop) for i in range(lax.axis_size('...  18.7 us
    ppermute x15, waiting for transfers between devices, partner_swap(): lax.ppermute(block, 'group', [(i, i ^ hop) for i in range(lax.axis_size('...  6.09 us
    ppermute x1, waiting for transfers between devices, lat_neighbours(): first = lax.ppermute(messages[0], 'lat', even_pairs(rows))  2.61 us
    pallas_call x1, Pallas kernels, local(): call(functools.partial(strip_react_kernel, n_lon, slots), [struct(tracers...  1.67 us
    ppermute x1, starting transfers between devices, lat_neighbours(): first = lax.ppermute(messages[0], 'lat', even_pairs(rows))  1.64 us
    pallas_call x1, Pallas kernels, local(): call(functools.partial(pack_kernel, n_lon, n_lat, 4), [struct(rows, width...  1.61 us
    pallas_call x1, Pallas kernels, local(): call(functools.partial(strip_place_kernel, slots), [struct(tracers, strat...  1.18 us
    pallas_call x1, Pallas kernels, local(): call(functools.partial(ends_kernel, n_lon, n_lat, slots), [struct(half *...  1.02 us
  transfers between devices with their start and end apart: 19, of which 6 were waited for; matrix products, arithmetic and copies ran while one was open for 0% of the time, Pallas kernels for 20%

profile of v4, /device:TPU:0, one launch (start us, length us, event | category | flops | bytes accessed | tf_op | source)
XLA Modules:
  0.0 40.1 jit_solution(6975257160381328006)
XLA Ops:
  0.6 0.8 %pad_maximum_fusion.refs_0_.refs_4_ = f32[64,128]{1,0:T(8,128)S(1)} fusion(f32[16,128]{1,0:T(8,128)} %bitcast.17, f32[16,128]{1,0:T(8,128)} %bitcast.25, f32[16,128]{1,0:T(8,128)} %bitcast.18, f32[16,128]{1,0:T(8,128)} %bitcast.19), kind=kLoop, calls=%fused_computation.3 | loop fusion | flops 24576 | bytes 65536 | tf_op jit(solution)/shard_map/concatenate | solution.py:611
  1.4 3.9 %collective-permute-start.3 = (f32[64,128]{1,0:T(8,128)S(1)}, f32[64,128]{1,0:T(8,128)S(1)}, u32[]{:S(2)}, u32[]{:S(2)}) collective-permute-start(f32[64,128]{1,0:T(8,128)S(1)} %pad_maximum_fusion.refs_0_.refs_4_), channel_id=1, source_target_pairs={{0,24},{8,16},{16,8},{24,0},{1,25},{9,17},{17,9},{25,1},{2,26},{10... | collective-permute-start | bytes 98312 | tf_op jit(solution)/shard_map/ppermute | solution.py:76
  5.3 0.5 %collective-permute-start.2 = (f32[64,128]{1,0:T(8,128)S(1)}, f32[64,128]{1,0:T(8,128)S(1)}, u32[]{:S(2)}, u32[]{:S(2)}) collective-permute-start(f32[64,128]{1,0:T(8,128)S(1)} %pad_maximum_fusion.refs_0_.refs_4_), channel_id=1, source_target_pairs={{0,16},{8,24},{16,0},{24,8},{1,17},{9,25},{17,1},{25,9},{2,18},{10... | collective-permute-start | bytes 98312 | tf_op jit(solution)/shard_map/ppermute | solution.py:76
  5.8 0.1 collective-permute-start.1
  5.9 1.6 %shard_map.129 = (f32[16,128]{1,0:T(8,128)S(1)}, f32[128,128]{1,0:T(8,128)S(1)}, f32[128,128]{1,0:T(8,128)S(1)}, f32[32,4,16,128]{3,2,1,0:T(8,128)S(1)}) custom-call(f32[32,4,16,128]{3,2,1,0:T(8,128)} %species_hbm.1), custom_call_target="tpu_custom_call" | custom-call | flops 1 | bytes 1 | tf_op jit(solution)/shard_map/pallas_call | solution.py:625
  7.5 0.1 collective-permute-start
  7.6 0.2 shard_map.130
  7.8 0.7 %shard_map.131 = (f32[336,128]{1,0:T(8,128)S(1)}, f32[336,128]{1,0:T(8,128)S(1)}, f32[336,128]{1,0:T(8,128)S(1)}, f32[336,128]{1,0:T(8,128)S(1)}) custom-call(f32[32,4,16,128]{3,2,1,0:T(8,128)S(1)} %get-tuple-element.49.species, f32[320,128]{1,0:T(8,128)S(1)} %get-tuple-element.51.refs_0_, f32[320,128]{1,0:T(8,128)S(1)} %get-tuple-element.52.refs_1_, ...), custom_call_target="tpu_custom_call" | custom-call | flops 1 | bytes 16777216 | tf_op jit(solution)/shard_map/pallas_call | solution.py:643
  8.6 0.2 collective-permute-done.refs_0_.refs_5_
  8.7 0.1 shard_map.132
  8.9 0.8 %collective-permute-done.1.refs_1_.refs_5_ = f32[64,128]{1,0:T(8,128)S(1)} collective-permute-done((f32[64,128]{1,0:T(8,128)S(1)}, f32[64,128]{1,0:T(8,128)S(1)}, u32[]{:S(2)}, u32[]{:S(2)}) %collective-permute-start.1) | collective-permute-done | bytes 32800 | tf_op jit(solution)/shard_map/ppermute | solution.py:76
  9.7 0.0 collective-permute-done.2.refs_2_.refs_6_
  9.7 0.0 collective-permute-done.3.refs_3_.refs_7_
  9.8 0.1 collective-permute-start.4
  9.8 1.4 %collective-permute-start.13 = (f32[336,128]{1,0:T(8,128)S(1)}, f32[336,128]{1,0:T(8,128)S(1)}, u32[]{:S(2)}, u32[]{:S(2)}) collective-permute-start(f32[336,128]{1,0:T(8,128)S(1)} %get-tuple-element.81), channel_id=1, source_target_pairs={{0,8},{8,0},{16,24},{24,16},{1,9},{9,1},{17,25},{25,17},{2,10},{10... | collective-permute-start | bytes 516104 | tf_op jit(solution)/shard_map/ppermute | solution.py:76
  11.3 1.5 %collective-permute-start.14 = (f32[336,128]{1,0:T(8,128)S(1)}, f32[336,128]{1,0:T(8,128)S(1)}, u32[]{:S(2)}, u32[]{:S(2)}) collective-permute-start(f32[336,128]{1,0:T(8,128)S(1)} %get-tuple-element.82), channel_id=1, source_target_pairs={{0,16},{8,24},{16,0},{24,8},{1,17},{9,25},{17,1},{25,9},{2,18},{10... | collective-permute-start | bytes 516104 | tf_op jit(solution)/shard_map/ppermute | solution.py:76
  12.8 0.6 %collective-permute-start.15 = (f32[336,128]{1,0:T(8,128)S(1)}, f32[336,128]{1,0:T(8,128)S(1)}, u32[]{:S(2)}, u32[]{:S(2)}) collective-permute-start(f32[336,128]{1,0:T(8,128)S(1)} %get-tuple-element.83), channel_id=1, source_target_pairs={{0,24},{8,16},{16,8},{24,0},{1,25},{9,17},{17,9},{25,1},{2,26},{10... | collective-permute-start | bytes 516104 | tf_op jit(solution)/shard_map/ppermute | solution.py:76
  13.5 0.0 copy-start.7
  13.5 1.6 %collective-permute-start.5 = (f32[136,128]{1,0:T(8,128)S(1)}, f32[136,128]{1,0:T(8,128)S(1)}, u32[]{:S(2)}, u32[]{:S(2)}) collective-permute-start(f32[136,128]{1,0:T(8,128)S(1)} %get-tuple-element.67), channel_id=1, source_target_pairs={{0,2},{2,0},{4,6},{6,4},{1,3},{3,1},{5,7},{7,5},{8,10},{10,8},{12,... | collective-permute-start | bytes 208904 | tf_op jit(solution)/shard_map/ppermute | solution.py:71
  15.1 0.1 shard_map.133.refs_8_.refs_12_
  15.2 0.0 copy-start
  15.3 0.0 copy-start.1
  15.3 2.6 %collective-permute-done.5.refs_6_.refs_1_ = f32[136,128]{1,0:T(8,128)S(1)} collective-permute-done((f32[136,128]{1,0:T(8,128)S(1)}, f32[136,128]{1,0:T(8,128)S(1)}, u32[]{:S(2)}, u32[]{:S(2)}) %collective-permute-start.5) | collective-permute-done | bytes 69664 | tf_op jit(solution)/shard_map/ppermute | solution.py:71
  17.9 0.0 collective-permute-done.6.refs_7_.refs_2_
  17.9 1.0 %shard_map.134 = (f32[256,128]{1,0:T(8,128)S(1)}, f32[256,128]{1,0:T(8,128)S(1)}, f32[256,128]{1,0:T(8,128)S(1)}, f32[256,128]{1,0:T(8,128)S(1)}) custom-call(f32[32,4,16,128]{3,2,1,0:T(8,128)S(1)} %get-tuple-element.49.species, f32[64,128]{1,0:T(8,128)S(1)} %pad_maximum_fusion.refs_0_.refs_4_, f32[64,128]{1,0:T(8,128)S(1)} %collective-permute-done.1.refs_1_.refs_5_, ...), custom_call_target="tpu_custom_call" | custom-call | flops 1 | bytes 67108864 | tf_op jit(solution)/shard_map/pallas_call | solution.py:676
  18.9 1.4 %collective-permute-start.7 = (f32[256,128]{1,0:T(8,128)S(1)}, f32[256,128]{1,0:T(8,128)S(1)}, u32[]{:S(2)}, u32[]{:S(2)}) collective-permute-start(f32[256,128]{1,0:T(8,128)S(1)} %get-tuple-element.72), channel_id=1, source_target_pairs={{0,8},{8,0},{16,24},{24,16},{1,9},{9,1},{17,25},{25,17},{2,10},{10... | collective-permute-start | bytes 393224 | tf_op jit(solution)/shard_map/ppermute | solution.py:76
  20.3 1.5 %collective-permute-start.8 = (f32[256,128]{1,0:T(8,128)S(1)}, f32[256,128]{1,0:T(8,128)S(1)}, u32[]{:S(2)}, u32[]{:S(2)}) collective-permute-start(f32[256,128]{1,0:T(8,128)S(1)} %get-tuple-element.73), channel_id=1, source_target_pairs={{0,16},{8,24},{16,0},{24,8},{1,17},{9,25},{17,1},{25,9},{2,18},{10... | collective-permute-start | bytes 393224 | tf_op jit(solution)/shard_map/ppermute | solution.py:76
  21.8 0.0 collective-permute-done.13.refs_1_
  21.8 0.6 %collective-permute-start.9 = (f32[256,128]{1,0:T(8,128)S(1)}, f32[256,128]{1,0:T(8,128)S(1)}, u32[]{:S(2)}, u32[]{:S(2)}) collective-permute-start(f32[256,128]{1,0:T(8,128)S(1)} %get-tuple-element.74), channel_id=1, source_target_pairs={{0,24},{8,16},{16,8},{24,0},{1,25},{9,17},{17,9},{25,1},{2,26},{10... | collective-permute-start | bytes 393224 | tf_op jit(solution)/shard_map/ppermute | solution.py:76
  22.5 0.0 collective-permute-done.14.refs_2_
  22.5 0.0 collective-permute-done.15.refs_3_
  22.5 1.7 %shard_map.136 = (f32[264,128]{1,0:T(8,128)S(1)}, f32[264,128]{1,0:T(8,128)S(1)}, f32[264,128]{1,0:T(8,128)S(1)}, f32[264,128]{1,0:T(8,128)S(1)}) custom-call(f32[336,128]{1,0:T(8,128)S(1)} %get-tuple-element.80.refs_0_, f32[336,128]{1,0:T(8,128)S(1)} %collective-permute-done.13.refs_1_, f32[336,128]{1,0:T(8,128)S(1)} %collective-permute-done.14.refs_2_, ...), custom_call_target="tpu_custom_call" | custom-call | flops 268435456 | bytes 2097152 | tf_op jit(solution)/shard_map/pallas_call | solution.py:684
  24.2 1.4 %collective-permute-start.16 = (f32[264,128]{1,0:T(8,128)S(1)}, f32[264,128]{1,0:T(8,128)S(1)}, u32[]{:S(2)}, u32[]{:S(2)}) collective-permute-start(f32[264,128]{1,0:T(8,128)S(1)} %get-tuple-element.85), channel_id=1, source_target_pairs={{0,8},{8,0},{16,24},{24,16},{1,9},{9,1},{17,25},{25,17},{2,10},{10... | collective-permute-start | bytes 405512 | tf_op jit(solution)/shard_map/ppermute | solution.py:76
  25.6 1.5 %collective-permute-start.17 = (f32[264,128]{1,0:T(8,128)S(1)}, f32[264,128]{1,0:T(8,128)S(1)}, u32[]{:S(2)}, u32[]{:S(2)}) collective-permute-start(f32[264,128]{1,0:T(8,128)S(1)} %get-tuple-element.86), channel_id=1, source_target_pairs={{0,16},{8,24},{16,0},{24,8},{1,17},{9,25},{17,1},{25,9},{2,18},{10... | collective-permute-start | bytes 405512 | tf_op jit(solution)/shard_map/ppermute | solution.py:76
  27.1 0.0 collective-permute-done.7
  27.1 0.6 %collective-permute-start.18 = (f32[264,128]{1,0:T(8,128)S(1)}, f32[264,128]{1,0:T(8,128)S(1)}, u32[]{:S(2)}, u32[]{:S(2)}) collective-permute-start(f32[264,128]{1,0:T(8,128)S(1)} %get-tuple-element.87), channel_id=1, source_target_pairs={{0,24},{8,16},{16,8},{24,0},{1,25},{9,17},{17,9},{25,1},{2,26},{10... | collective-permute-start | bytes 405512 | tf_op jit(solution)/shard_map/ppermute | solution.py:76
  27.7 1.5 %collective-permute-done.9 = f32[256,128]{1,0:T(8,128)S(1)} collective-permute-done((f32[256,128]{1,0:T(8,128)S(1)}, f32[256,128]{1,0:T(8,128)S(1)}, u32[]{:S(2)}, u32[]{:S(2)}) %collective-permute-start.9) | collective-permute-done | bytes 131104 | tf_op jit(solution)/shard_map/ppermute | solution.py:76
  29.3 0.8 %shard_map.135 = (f32[256,128]{1,0:T(8,128)S(1)}, f32[256,128]{1,0:T(8,128)S(1)}, f32[256,128]{1,0:T(8,128)S(1)}, f32[256,128]{1,0:T(8,128)S(1)}, f32[8,128]{1,0:T(8,128)S(1)}) custom-call(f32[8,32,128]{2,1,0:T(8,128)S(1)} %bitcast.21, f32[8,32,128]{2,1,0:T(8,128)S(1)} %bitcast.22, f32[8,32,128]{2,1,0:T(8,128)S(1)} %bitcast.23, f32[8,32,128]{2,1,0:T(8,128)S(1)} %bitcast.24, ...), custom_call_target="tpu_custom_call" | custom-call | flops 268435456 | bytes 2097152 | tf_op jit(solution)/shard_map/pallas_call | solution.py:697
  30.1 0.6 %collective-permute-start.10 = (f32[256,128]{1,0:T(8,128)S(1)}, f32[256,128]{1,0:T(8,128)S(1)}, u32[]{:S(2)}, u32[]{:S(2)}) collective-permute-start(f32[256,128]{1,0:T(8,128)S(1)} %get-tuple-element.77), channel_id=1, source_target_pairs={{0,8},{8,0},{16,24},{24,16},{1,9},{9,1},{17,25},{25,17},{2,10},{10... | collective-permute-start | bytes 393224 | tf_op jit(solution)/shard_map/ppermute | solution.py:76
  30.7 0.8 %collective-permute-start.11 = (f32[256,128]{1,0:T(8,128)S(1)}, f32[256,128]{1,0:T(8,128)S(1)}, u32[]{:S(2)}, u32[]{:S(2)}) collective-permute-start(f32[256,128]{1,0:T(8,128)S(1)} %get-tuple-element.78), channel_id=1, source_target_pairs={{0,16},{8,24},{16,0},{24,8},{1,17},{9,25},{17,1},{25,9},{2,18},{10... | collective-permute-start | bytes 393224 | tf_op jit(solution)/shard_map/ppermute | solution.py:76
  31.5 2.2 %collective-permute-start.12 = (f32[256,128]{1,0:T(8,128)S(1)}, f32[256,128]{1,0:T(8,128)S(1)}, u32[]{:S(2)}, u32[]{:S(2)}) collective-permute-start(f32[256,128]{1,0:T(8,128)S(1)} %get-tuple-element.79), channel_id=1, source_target_pairs={{0,24},{8,16},{16,8},{24,0},{1,25},{9,17},{17,9},{25,1},{2,26},{10... | collective-permute-start | bytes 393224 | tf_op jit(solution)/shard_map/ppermute | solution.py:76
  33.6 1.7 %collective-permute-done.17.refs_2_ = f32[264,128]{1,0:T(8,128)S(1)} collective-permute-done((f32[264,128]{1,0:T(8,128)S(1)}, f32[264,128]{1,0:T(8,128)S(1)}, u32[]{:S(2)}, u32[]{:S(2)}) %collective-permute-start.17) | collective-permute-done | bytes 135200 | tf_op jit(solution)/shard_map/ppermute | solution.py:76
  35.4 0.0 collective-permute-done.18.refs_3_
  35.4 0.0 copy-start.6
  35.4 1.2 %shard_map.137 = (f32[32,4,16,128]{3,2,1,0:T(8,128)}, f32[8,128]{1,0:T(8,128)S(1)}) custom-call(f32[264,128]{1,0:T(8,128)S(1)} %get-tuple-element.84.refs_0_, f32[264,128]{1,0:T(8,128)S(1)} %collective-permute-done.16.refs_1_, f32[264,128]{1,0:T(8,128)S(1)} %collective-permute-done.17.refs_2_, f32[264,128]{1,0:T(8,128)S(1)} %collective-permute-done.18.refs_3_), custom_call_target="tpu_custom_call" | custom-call | flops 1 | bytes 1048576 | tf_op jit(solution)/shard_map/pallas_call | solution.py:713
  36.6 0.7 %shard_map.139 = (f32[1,16,128]{2,1,0:T(8,128)}, f32[1,16,128]{2,1,0:T(8,128)}, f32[1,16,128]{2,1,0:T(8,128)}) custom-call(f32[1,16,128]{2,1,0:T(8,128)S(1)} %copy-done.4, f32[1,16,128]{2,1,0:T(8,128)S(1)} %copy-done.3, f32[1,16,128]{2,1,0:T(8,128)S(1)} %copy-done.2, f32[1,16,128]{2,1,0:T(8,128)S(1)} %copy-done.6, ...), custom_call_target="tpu_custom_call" | custom-call | flops 1 | bytes 1 | tf_op jit(solution)/shard_map/pallas_call | solution.py:721
  37.3 1.9 %collective-permute-done.11 = f32[256,128]{1,0:T(8,128)S(1)} collective-permute-done((f32[256,128]{1,0:T(8,128)S(1)}, f32[256,128]{1,0:T(8,128)S(1)}, u32[]{:S(2)}, u32[]{:S(2)}) %collective-permute-start.11) | collective-permute-done | bytes 131104 | tf_op jit(solution)/shard_map/ppermute | solution.py:76
  39.3 0.8 %shard_map.138 = f32[32,4,16,128]{3,2,1,0:T(8,128)} custom-call(f32[32,8,128]{2,1,0:T(8,128)S(1)} %bitcast.13, f32[32,8,128]{2,1,0:T(8,128)S(1)} %bitcast.14, f32[32,8,128]{2,1,0:T(8,128)S(1)} %bitcast.15, f32[32,8,128]{2,1,0:T(8,128)S(1)} %bitcast.16, f32[32,4,16,128]{3,2,1,0:T(8,128)} %get-tuple-element.88.refs_4_), custom_call_target="tpu_custom_call", output_to_operand_aliasing={{}: (4, {})} | custom-call | flops 1 | bytes 1048576 | tf_op jit(solution)/shard_map/pallas_call | solution.py:735
  (31 shorter events, 0.1 us)
Async XLA Ops:
  1.4 8.3 %collective-permute-start.3 = (f32[64,128]{1,0:T(8,128)S(1)}, f32[64,128]{1,0:T(8,128)S(1)}, u32[]{:S(2)}, u32[]{:S(2)}) collective-permute-start(f32[64,128]{1,0:T(8,128)S(1)} %pad_maximum_fusion.refs_0_.refs_4_), channel_id=1, source_target_pairs={{0,24},{8,16},{16,8},{24,0},{1,25},{9,17},{17,9},{25,1},{2,26},{10... | collective-permute-start | bytes 98312 | tf_op jit(solution)/shard_map/ppermute | solution.py:76
  5.3 4.4 %collective-permute-start.2 = (f32[64,128]{1,0:T(8,128)S(1)}, f32[64,128]{1,0:T(8,128)S(1)}, u32[]{:S(2)}, u32[]{:S(2)}) collective-permute-start(f32[64,128]{1,0:T(8,128)S(1)} %pad_maximum_fusion.refs_0_.refs_4_), channel_id=1, source_target_pairs={{0,16},{8,24},{16,0},{24,8},{1,17},{9,25},{17,1},{25,9},{2,18},{10... | collective-permute-start | bytes 98312 | tf_op jit(solution)/shard_map/ppermute | solution.py:76
  5.8 3.9 %collective-permute-start.1 = (f32[64,128]{1,0:T(8,128)S(1)}, f32[64,128]{1,0:T(8,128)S(1)}, u32[]{:S(2)}, u32[]{:S(2)}) collective-permute-start(f32[64,128]{1,0:T(8,128)S(1)} %pad_maximum_fusion.refs_0_.refs_4_), channel_id=1, source_target_pairs={{0,8},{8,0},{16,24},{24,16},{1,9},{9,1},{17,25},{25,17},{2,10},{10... | collective-permute-start | bytes 98312 | tf_op jit(solution)/shard_map/ppermute | solution.py:76
  7.5 1.2 %collective-permute-start = (f32[16,128]{1,0:T(8,128)S(1)}, f32[16,128]{1,0:T(8,128)S(1)}, u32[]{:S(2)}, u32[]{:S(2)}) collective-permute-start(f32[16,128]{1,0:T(8,128)S(1)} %get-tuple-element.50), channel_id=1, source_target_pairs={{0,1},{1,0},{2,3},{3,2},{4,5},{5,4},{6,7},{7,6},{8,9},{9,8},{10,11... | collective-permute-start | bytes 24584 | tf_op jit(solution)/shard_map/ppermute | solution.py:56
  9.8 3.7 %collective-permute-start.4 = (f32[96,128]{1,0:T(8,128)S(1)}, f32[96,128]{1,0:T(8,128)S(1)}, u32[]{:S(2)}, u32[]{:S(2)}) collective-permute-start(f32[96,128]{1,0:T(8,128)S(1)} %get-tuple-element.95), channel_id=1, source_target_pairs={{0,1},{1,0},{2,3},{3,2},{4,5},{5,4},{6,7},{7,6},{8,9},{9,8},{10,11... | collective-permute-start | bytes 147464 | tf_op jit(solution)/shard_map/ppermute | solution.py:56
  9.8 12.0 %collective-permute-start.13 = (f32[336,128]{1,0:T(8,128)S(1)}, f32[336,128]{1,0:T(8,128)S(1)}, u32[]{:S(2)}, u32[]{:S(2)}) collective-permute-start(f32[336,128]{1,0:T(8,128)S(1)} %get-tuple-element.81), channel_id=1, source_target_pairs={{0,8},{8,0},{16,24},{24,16},{1,9},{9,1},{17,25},{25,17},{2,10},{10... | collective-permute-start | bytes 516104 | tf_op jit(solution)/shard_map/ppermute | solution.py:76
  11.3 11.2 %collective-permute-start.14 = (f32[336,128]{1,0:T(8,128)S(1)}, f32[336,128]{1,0:T(8,128)S(1)}, u32[]{:S(2)}, u32[]{:S(2)}) collective-permute-start(f32[336,128]{1,0:T(8,128)S(1)} %get-tuple-element.82), channel_id=1, source_target_pairs={{0,16},{8,24},{16,0},{24,8},{1,17},{9,25},{17,1},{25,9},{2,18},{10... | collective-permute-start | bytes 516104 | tf_op jit(solution)/shard_map/ppermute | solution.py:76
  12.8 9.7 %collective-permute-start.15 = (f32[336,128]{1,0:T(8,128)S(1)}, f32[336,128]{1,0:T(8,128)S(1)}, u32[]{:S(2)}, u32[]{:S(2)}) collective-permute-start(f32[336,128]{1,0:T(8,128)S(1)} %get-tuple-element.83), channel_id=1, source_target_pairs={{0,24},{8,16},{16,8},{24,0},{1,25},{9,17},{17,9},{25,1},{2,26},{10... | collective-permute-start | bytes 516104 | tf_op jit(solution)/shard_map/ppermute | solution.py:76
  13.5 1.7 %copy-start.7 = (f32[128]{0:T(128)S(1)}, f32[128]{0:T(128)}, u32[]{:S(2)}) copy-start(f32[128]{0:T(128)} %param.19) | copy-start | bytes 1540
  13.5 4.4 %collective-permute-start.5 = (f32[136,128]{1,0:T(8,128)S(1)}, f32[136,128]{1,0:T(8,128)S(1)}, u32[]{:S(2)}, u32[]{:S(2)}) collective-permute-start(f32[136,128]{1,0:T(8,128)S(1)} %get-tuple-element.67), channel_id=1, source_target_pairs={{0,2},{2,0},{4,6},{6,4},{1,3},{3,1},{5,7},{7,5},{8,10},{10,8},{12,... | collective-permute-start | bytes 208904 | tf_op jit(solution)/shard_map/ppermute | solution.py:71
  15.1 2.7 %collective-permute-start.6 = (f32[136,128]{1,0:T(8,128)S(1)}, f32[136,128]{1,0:T(8,128)S(1)}, u32[]{:S(2)}, u32[]{:S(2)}) collective-permute-start(f32[136,128]{1,0:T(8,128)S(1)} %get-tuple-element.68), channel_id=1, source_target_pairs={{0,1},{1,0},{2,4},{3,5},{4,2},{5,3},{6,7},{7,6},{8,9},{9,8},{10,12... | collective-permute-start | bytes 208904 | tf_op jit(solution)/shard_map/ppermute | solution.py:72
  15.2 7.2 %copy-start = (bf16[512,128]{1,0:T(8,128)(2,1)S(1)}, bf16[512,128]{1,0:T(8,128)(2,1)}, u32[]{:S(2)}) copy-start(bf16[512,128]{1,0:T(8,128)(2,1)} %refs_10_.1) | copy-start | bytes 393220
  15.3 7.2 %copy-start.1 = (bf16[128,512]{1,0:T(8,128)(2,1)S(1)}, bf16[128,512]{1,0:T(8,128)(2,1)}, u32[]{:S(2)}) copy-start(bf16[128,512]{1,0:T(8,128)(2,1)} %refs_11_.1) | copy-start | bytes 393220
  17.9 4.6 %copy-start.5 = (s32[16,128]{1,0:T(8,128)S(1)}, s32[16,128]{1,0:T(8,128)}, u32[]{:S(2)}) copy-start(s32[16,128]{1,0:T(8,128)} %refs_9_.1) | copy-start | bytes 24580
  18.9 8.2 %collective-permute-start.7 = (f32[256,128]{1,0:T(8,128)S(1)}, f32[256,128]{1,0:T(8,128)S(1)}, u32[]{:S(2)}, u32[]{:S(2)}) collective-permute-start(f32[256,128]{1,0:T(8,128)S(1)} %get-tuple-element.72), channel_id=1, source_target_pairs={{0,8},{8,0},{16,24},{24,16},{1,9},{9,1},{17,25},{25,17},{2,10},{10... | collective-permute-start | bytes 393224 | tf_op jit(solution)/shard_map/ppermute | solution.py:76
  20.3 7.4 %collective-permute-start.8 = (f32[256,128]{1,0:T(8,128)S(1)}, f32[256,128]{1,0:T(8,128)S(1)}, u32[]{:S(2)}, u32[]{:S(2)}) collective-permute-start(f32[256,128]{1,0:T(8,128)S(1)} %get-tuple-element.73), channel_id=1, source_target_pairs={{0,16},{8,24},{16,0},{24,8},{1,17},{9,25},{17,1},{25,9},{2,18},{10... | collective-permute-start | bytes 393224 | tf_op jit(solution)/shard_map/ppermute | solution.py:76
  21.8 7.4 %collective-permute-start.9 = (f32[256,128]{1,0:T(8,128)S(1)}, f32[256,128]{1,0:T(8,128)S(1)}, u32[]{:S(2)}, u32[]{:S(2)}) collective-permute-start(f32[256,128]{1,0:T(8,128)S(1)} %get-tuple-element.74), channel_id=1, source_target_pairs={{0,24},{8,16},{16,8},{24,0},{1,25},{9,17},{17,9},{25,1},{2,26},{10... | collective-permute-start | bytes 393224 | tf_op jit(solution)/shard_map/ppermute | solution.py:76
  24.2 7.3 %collective-permute-start.16 = (f32[264,128]{1,0:T(8,128)S(1)}, f32[264,128]{1,0:T(8,128)S(1)}, u32[]{:S(2)}, u32[]{:S(2)}) collective-permute-start(f32[264,128]{1,0:T(8,128)S(1)} %get-tuple-element.85), channel_id=1, source_target_pairs={{0,8},{8,0},{16,24},{24,16},{1,9},{9,1},{17,25},{25,17},{2,10},{10... | collective-permute-start | bytes 405512 | tf_op jit(solution)/shard_map/ppermute | solution.py:76
  25.6 9.8 %collective-permute-start.17 = (f32[264,128]{1,0:T(8,128)S(1)}, f32[264,128]{1,0:T(8,128)S(1)}, u32[]{:S(2)}, u32[]{:S(2)}) collective-permute-start(f32[264,128]{1,0:T(8,128)S(1)} %get-tuple-element.86), channel_id=1, source_target_pairs={{0,16},{8,24},{16,0},{24,8},{1,17},{9,25},{17,1},{25,9},{2,18},{10... | collective-permute-start | bytes 405512 | tf_op jit(solution)/shard_map/ppermute | solution.py:76
  27.1 8.3 %collective-permute-start.18 = (f32[264,128]{1,0:T(8,128)S(1)}, f32[264,128]{1,0:T(8,128)S(1)}, u32[]{:S(2)}, u32[]{:S(2)}) collective-permute-start(f32[264,128]{1,0:T(8,128)S(1)} %get-tuple-element.87), channel_id=1, source_target_pairs={{0,24},{8,16},{16,8},{24,0},{1,25},{9,17},{17,9},{25,1},{2,26},{10... | collective-permute-start | bytes 405512 | tf_op jit(solution)/shard_map/ppermute | solution.py:76
  30.1 7.3 %collective-permute-start.10 = (f32[256,128]{1,0:T(8,128)S(1)}, f32[256,128]{1,0:T(8,128)S(1)}, u32[]{:S(2)}, u32[]{:S(2)}) collective-permute-start(f32[256,128]{1,0:T(8,128)S(1)} %get-tuple-element.77), channel_id=1, source_target_pairs={{0,8},{8,0},{16,24},{24,16},{1,9},{9,1},{17,25},{25,17},{2,10},{10... | collective-permute-start | bytes 393224 | tf_op jit(solution)/shard_map/ppermute | solution.py:76
  30.7 8.6 %collective-permute-start.11 = (f32[256,128]{1,0:T(8,128)S(1)}, f32[256,128]{1,0:T(8,128)S(1)}, u32[]{:S(2)}, u32[]{:S(2)}) collective-permute-start(f32[256,128]{1,0:T(8,128)S(1)} %get-tuple-element.78), channel_id=1, source_target_pairs={{0,16},{8,24},{16,0},{24,8},{1,17},{9,25},{17,1},{25,9},{2,18},{10... | collective-permute-start | bytes 393224 | tf_op jit(solution)/shard_map/ppermute | solution.py:76
  31.5 7.8 %collective-permute-start.12 = (f32[256,128]{1,0:T(8,128)S(1)}, f32[256,128]{1,0:T(8,128)S(1)}, u32[]{:S(2)}, u32[]{:S(2)}) collective-permute-start(f32[256,128]{1,0:T(8,128)S(1)} %get-tuple-element.79), channel_id=1, source_target_pairs={{0,24},{8,16},{16,8},{24,0},{1,25},{9,17},{17,9},{25,1},{2,26},{10... | collective-permute-start | bytes 393224 | tf_op jit(solution)/shard_map/ppermute | solution.py:76
  35.4 1.2 %copy-start.2 = (f32[1,16,128]{2,1,0:T(8,128)S(1)}, f32[1,16,128]{2,1,0:T(8,128)}, u32[]{:S(2)}) copy-start(f32[1,16,128]{2,1,0:T(8,128)} %warmth.1) | copy-start | bytes 24580
  35.4 1.2 %copy-start.3 = (f32[1,16,128]{2,1,0:T(8,128)S(1)}, f32[1,16,128]{2,1,0:T(8,128)}, u32[]{:S(2)}) copy-start(f32[1,16,128]{2,1,0:T(8,128)} %north.1) | copy-start | bytes 24580
  35.4 1.2 %copy-start.4 = (f32[1,16,128]{2,1,0:T(8,128)S(1)}, f32[1,16,128]{2,1,0:T(8,128)}, u32[]{:S(2)}) copy-start(f32[1,16,128]{2,1,0:T(8,128)} %east.1) | copy-start | bytes 24580
  35.4 1.2 %copy-start.6 = (f32[1,16,128]{2,1,0:T(8,128)S(1)}, f32[1,16,128]{2,1,0:T(8,128)}, u32[]{:S(2)}) copy-start(f32[1,16,128]{2,1,0:T(8,128)} %density.1) | copy-start | bytes 24580

commit v5 on v4

--- a/solution.py
+++ b/solution.py
@@ -217,12 +217,11 @@
     weight[...] = jnp.broadcast_to(yields[...], weight.shape[::-1]).T
 
 
-def ends_kernel(n_lon, n_lat, slots, species, *refs):
+def ends_kernel(n_lon, slots, species, *refs):
     refs = list(refs)
     winds = [refs.pop(0) for _ in range(slots)]
     lon_fields = [refs.pop(0) for _ in range(n_lon)]
     lon_in = [refs.pop(0) for _ in range(n_lon)]
-    lat_in = [refs.pop(0) for _ in range(n_lat)]
     outs = [refs.pop(0) for _ in range(slots)]
     upward = refs.pop(0)
     tracers, strata, rows, width = species.shape
@@ -231,7 +230,7 @@
     me = lax.axis_index("group")
     lane = lane_ids((half, width))
     row = row_ids((half, width))
-    found = coefficients(winds, lon_fields, upward, lat_in, tracers * strata, ends)
+    found = coefficients(winds, lon_fields, upward, [], 0, ends)
     columns = [ends(m[0:rows]) for m in lon_in]
     if n_lon == 2:
         columns = both_sides("lon", columns)
@@ -250,12 +249,10 @@
             below = jnp.maximum(level - 1, 0)
             first, last = species[t, level, 0:half], species[t, level, half:rows]
             here = jnp.where(row < quarter, first, last)
-            place = t * strata + level
-            low_row, high_row = both_sides("lat", [m[pl.ds(place, 1), :] for m in lat_in])
             south = pltpu.roll(jnp.where(row < quarter - 1, first, last), 1, 0)
-            south = jnp.where(row == 0, low_row, south)
+            south = jnp.where(row == 0, 0.0, south)
             north = pltpu.roll(jnp.where(row < quarter + 1, first, last), half - 1, 0)
-            north = jnp.where(row == half - 1, high_row, north)
+            north = jnp.where(row == half - 1, 0.0, north)
             up = jnp.where(row < quarter, species[t, above, 0:half], species[t, above, half:rows])
             down = jnp.where(row < quarter, species[t, below, 0:half], species[t, below, half:rows])
             east = jnp.where(lane == width - 1, high, pltpu.roll(here, width - 1, 1))
@@ -266,6 +263,36 @@
         return carry
 
     lax.fori_loop(0, tracers, one, 0, unroll=tracers)
+
+
+def ends_rim_kernel(n_lat, slots, species, *refs):
+    refs = list(refs)
+    winds = [refs.pop(0) for _ in range(slots)]
+    lat_in = [refs.pop(0) for _ in range(n_lat)]
+    before, outs = refs[:slots], refs[slots:]
+    tracers, strata, rows, width = species.shape
+    held = before[0].shape[0]
+    base = tracers * strata
+    me = lax.axis_index("group")
+    flat = species.reshape(base * rows, width)
+    for slot in range(slots):
+        level = me ^ slot
+        here = [
+            flat[pl.ds(level * rows + line, tracers, stride=strata * rows), :]
+            for line in (0, rows - 1)
+        ]
+        low, high = both_sides(
+            "lat", [m[pl.ds(level, tracers, stride=strata), :] for m in lat_in]
+        )
+        low_wind, high_wind = both_sides("lat", [m[base + slot:base + slot + 1] for m in lat_in])
+        first, last = winds[slot][rows:rows + 1], winds[slot][2 * rows - 1:2 * rows]
+        came, went = faces(low_wind, first)
+        south = (went - jnp.minimum(0.5 * first, 0.0)) * here[0] + came * low
+        went, came = faces(last, high_wind)
+        north = (went - jnp.maximum(0.5 * last, 0.0)) * here[1] + came * high
+        outs[slot][0:tracers] = before[slot][0:tracers] + south
+        outs[slot][tracers:held - tracers] = before[slot][tracers:held - tracers]
+        outs[slot][held - tracers:held] = before[slot][held - tracers:held] - north
 
 
 def strip_lanes(value, shift):
@@ -329,28 +356,31 @@
     done = tracers * (half + 2)
     for slot in range(slots):
         outs[slot][0:done] = strips[slot][...]
-    for part in range(tracers // share):
-
-        def one(i, rims):
-            t = part * share + i
+    parts = tracers // share
+
+    def one(i, rims):
+        new = []
+        for part in range(parts):
             turned = [
-                strip_lanes(species[t, level, quarter:3 * quarter], strip * level)
+                strip_lanes(species[part * share + i, level, quarter:3 * quarter], strip * level)
                 for level in range(strata)
             ]
-            new = []
             for slot in range(slots):
-                owner = me ^ slot
-                rim = strip_of(turned, owner, strip, 1)
-                rim = pltpu.roll(rim, 2 * i, 1)
+                rim = pltpu.roll(strip_of(turned, me ^ slot, strip, 1), 2 * i, 1)
                 mine = lax.rem(lane - 2 * i + 1 + width, strip) < 2
-                new.append(jnp.where(mine, rim, rims[slot]))
-            return tuple(new)
-
-        rims = lax.fori_loop(
-            0, share, one, tuple(jnp.zeros((half, width), F32) for _ in range(slots)), unroll=8
-        )
+                new.append(jnp.where(mine, rim, rims[part * slots + slot]))
+        return tuple(new)
+
+    rims = lax.fori_loop(
+        0,
+        share,
+        one,
+        tuple(jnp.zeros((half, width), F32) for _ in range(parts * slots)),
+        unroll=8,
+    )
+    for part in range(parts):
         for slot in range(slots):
-            outs[slot][done + part * half:done + (part + 1) * half] = rims[slot]
+            outs[slot][done + part * half:done + (part + 1) * half] = rims[part * slots + slot]
 
 
 def strip_edge_kernel(n_lon, slots, *refs):
@@ -672,14 +702,19 @@
     weight = call(
         weight_kernel, struct(slots * tracers, width), [VMEM], touched=256 * species_amounts.size
     )(heat_yield[None])
+    adv = call(
+        functools.partial(ends_kernel, n_lon, slots),
+        [struct(half * tracers, width)] * slots,
+        [VMEM] * (1 + slots + 2 * n_lon),
+        scratch=[pltpu.VMEM((strata, rows, width), F32)],
+        touched=256 * species_amounts.size,
+    )(species, *winds, *lon_fields, *lon_in)
     weight, lat_in = lax.optimization_barrier((weight, lat_in))
     adv = call(
-        functools.partial(ends_kernel, n_lon, n_lat, slots),
+        functools.partial(ends_rim_kernel, n_lat, slots),
         [struct(half * tracers, width)] * slots,
-        [VMEM] * (1 + slots + 2 * n_lon + n_lat),
-        scratch=[pltpu.VMEM((strata, rows, width), F32)],
-        touched=256 * species_amounts.size,
-    )(species, *winds, *lon_fields, *lon_in, *lat_in)
+        [VMEM] * (1 + 2 * slots + n_lat),
+    )(species, *winds, *lat_in, *adv)
     adv = swap_slots(adv)
     reacted = call(
         functools.partial(strip_react_kernel, n_lon, slots),

time: 40.4 us -> 39.6 us (0.980)
  waiting for transfers between devices: 8.88 us -> 8.43 us
    ppermute x1, waiting for transfers between devices: 2.61 us -> 1.76 us  [lat_neighbours(): first = lax.ppermute(messages[0], 'lat', even_pairs(rows))]
    pallas_call x1 -> x2, Pallas kernels: 1.02 us -> 1.01 us  [the longest x1 0.86 us: local(): call(functools.partial(ends_kernel, n_lon, slots), [struct(half * tracers...]
  transfers between devices with their start and end apart: 19 -> 19, of which waited for: 6 -> 7; matrix products, arithmetic and copies ran while one was open for 0% -> 0% of each run, Pallas kernels for 20% -> 20%
where the time goes in v5:
time: 39.6 us; the launch traced here: 39.3 us
  starting transfers between devices  20.4 us (52%)
  Pallas kernels  8.73 us (22%)
  waiting for transfers between devices  8.43 us (21%)
  between operations  0.88 us (2%)
  other arithmetic  0.79 us (2%)
    ppermute x15, starting transfers between devices, partner_swap(): lax.ppermute(block, 'group', [(i, i ^ hop) for i in range(lax.axis_size('...  18.7 us
    ppermute x15, waiting for transfers between devices, partner_swap(): lax.ppermute(block, 'group', [(i, i ^ hop) for i in range(lax.axis_size('...  6.28 us
    ppermute x1, waiting for transfers between devices, lat_neighbours(): first = lax.ppermute(messages[0], 'lat', even_pairs(rows))  1.76 us
    pallas_call x1, Pallas kernels, local(): call(functools.partial(strip_react_kernel, n_lon, slots), [struct(tracers...  1.67 us
    ppermute x1, starting transfers between devices, lat_neighbours(): first = lax.ppermute(messages[0], 'lat', even_pairs(rows))  1.64 us
    pallas_call x1, Pallas kernels, local(): call(functools.partial(pack_kernel, n_lon, n_lat, 4), [struct(rows, width...  1.61 us
    pallas_call x1, Pallas kernels, local(): call(functools.partial(strip_place_kernel, slots), [struct(tracers, strat...  1.18 us
    pallas_call x1, Pallas kernels, local(): call(functools.partial(ends_kernel, n_lon, slots), [struct(half * tracers...  0.86 us
  transfers between devices with their start and end apart: 19, of which 7 were waited for; matrix products, arithmetic and copies ran while one was open for 0% of the time, Pallas kernels for 20%

profile of v5, /device:TPU:0, one launch (start us, length us, event | category | flops | bytes accessed | tf_op | source)
XLA Modules:
  0.0 39.3 jit_solution(1013827514255080773)
XLA Ops:
  0.6 0.8 %pad_maximum_fusion.refs_0_.refs_4_ = f32[64,128]{1,0:T(8,128)S(1)} fusion(f32[16,128]{1,0:T(8,128)} %bitcast.17, f32[16,128]{1,0:T(8,128)} %bitcast.25, f32[16,128]{1,0:T(8,128)} %bitcast.18, f32[16,128]{1,0:T(8,128)} %bitcast.19), kind=kLoop, calls=%fused_computation.3 | loop fusion | flops 24576 | bytes 65536 | tf_op jit(solution)/shard_map/concatenate | solution.py:641
  1.4 2.9 %collective-permute-start.1 = (f32[64,128]{1,0:T(8,128)S(1)}, f32[64,128]{1,0:T(8,128)S(1)}, u32[]{:S(2)}, u32[]{:S(2)}) collective-permute-start(f32[64,128]{1,0:T(8,128)S(1)} %pad_maximum_fusion.refs_0_.refs_4_), channel_id=1, source_target_pairs={{0,8},{8,0},{16,24},{24,16},{1,9},{9,1},{17,25},{25,17},{2,10},{10... | collective-permute-start | bytes 98312 | tf_op jit(solution)/shard_map/ppermute | solution.py:76
  4.3 1.5 %collective-permute-start.2 = (f32[64,128]{1,0:T(8,128)S(1)}, f32[64,128]{1,0:T(8,128)S(1)}, u32[]{:S(2)}, u32[]{:S(2)}) collective-permute-start(f32[64,128]{1,0:T(8,128)S(1)} %pad_maximum_fusion.refs_0_.refs_4_), channel_id=1, source_target_pairs={{0,16},{8,24},{16,0},{24,8},{1,17},{9,25},{17,1},{25,9},{2,18},{10... | collective-permute-start | bytes 98312 | tf_op jit(solution)/shard_map/ppermute | solution.py:76
  5.8 0.0 collective-permute-start.3
  5.8 1.6 %shard_map.129 = (f32[16,128]{1,0:T(8,128)S(1)}, f32[128,128]{1,0:T(8,128)S(1)}, f32[128,128]{1,0:T(8,128)S(1)}, f32[32,4,16,128]{3,2,1,0:T(8,128)S(1)}) custom-call(f32[32,4,16,128]{3,2,1,0:T(8,128)} %species_hbm.1), custom_call_target="tpu_custom_call" | custom-call | flops 1 | bytes 1 | tf_op jit(solution)/shard_map/pallas_call | solution.py:655
  7.5 0.1 collective-permute-start
  7.6 0.2 shard_map.130
  7.8 0.5 %shard_map.131 = (f32[336,128]{1,0:T(8,128)S(1)}, f32[336,128]{1,0:T(8,128)S(1)}, f32[336,128]{1,0:T(8,128)S(1)}, f32[336,128]{1,0:T(8,128)S(1)}) custom-call(f32[32,4,16,128]{3,2,1,0:T(8,128)S(1)} %get-tuple-element.53.species, f32[320,128]{1,0:T(8,128)S(1)} %get-tuple-element.55.refs_0_, f32[320,128]{1,0:T(8,128)S(1)} %get-tuple-element.56.refs_1_, ...), custom_call_target="tpu_custom_call" | custom-call | flops 1 | bytes 16777216 | tf_op jit(solution)/shard_map/pallas_call | solution.py:673
  8.3 0.4 collective-permute-done.refs_0_.refs_5_
  8.7 0.1 shard_map.132
  8.9 1.8 %collective-permute-done.3.refs_3_.refs_7_ = f32[64,128]{1,0:T(8,128)S(1)} collective-permute-done((f32[64,128]{1,0:T(8,128)S(1)}, f32[64,128]{1,0:T(8,128)S(1)}, u32[]{:S(2)}, u32[]{:S(2)}) %collective-permute-start.3) | collective-permute-done | bytes 32800 | tf_op jit(solution)/shard_map/ppermute | solution.py:76
  10.7 0.0 collective-permute-start.4
  10.7 0.6 %collective-permute-start.13 = (f32[336,128]{1,0:T(8,128)S(1)}, f32[336,128]{1,0:T(8,128)S(1)}, u32[]{:S(2)}, u32[]{:S(2)}) collective-permute-start(f32[336,128]{1,0:T(8,128)S(1)} %get-tuple-element.89), channel_id=1, source_target_pairs={{0,8},{8,0},{16,24},{24,16},{1,9},{9,1},{17,25},{25,17},{2,10},{10... | collective-permute-start | bytes 516104 | tf_op jit(solution)/shard_map/ppermute | solution.py:76
  11.3 1.4 %collective-permute-start.14 = (f32[336,128]{1,0:T(8,128)S(1)}, f32[336,128]{1,0:T(8,128)S(1)}, u32[]{:S(2)}, u32[]{:S(2)}) collective-permute-start(f32[336,128]{1,0:T(8,128)S(1)} %get-tuple-element.90), channel_id=1, source_target_pairs={{0,16},{8,24},{16,0},{24,8},{1,17},{9,25},{17,1},{25,9},{2,18},{10... | collective-permute-start | bytes 516104 | tf_op jit(solution)/shard_map/ppermute | solution.py:76
  12.6 1.6 %collective-permute-start.15 = (f32[336,128]{1,0:T(8,128)S(1)}, f32[336,128]{1,0:T(8,128)S(1)}, u32[]{:S(2)}, u32[]{:S(2)}) collective-permute-start(f32[336,128]{1,0:T(8,128)S(1)} %get-tuple-element.91), channel_id=1, source_target_pairs={{0,24},{8,16},{16,8},{24,0},{1,25},{9,17},{17,9},{25,1},{2,26},{10... | collective-permute-start | bytes 516104 | tf_op jit(solution)/shard_map/ppermute | solution.py:76
  14.3 0.0 collective-permute-done.4.refs_4_.refs_8_.refs_0_
  14.3 0.0 copy-start.7
  14.3 1.6 %collective-permute-start.5 = (f32[136,128]{1,0:T(8,128)S(1)}, f32[136,128]{1,0:T(8,128)S(1)}, u32[]{:S(2)}, u32[]{:S(2)}) collective-permute-start(f32[136,128]{1,0:T(8,128)S(1)} %get-tuple-element.70), channel_id=1, source_target_pairs={{0,2},{2,0},{4,6},{6,4},{1,3},{3,1},{5,7},{7,5},{8,10},{10,8},{12,... | collective-permute-start | bytes 208904 | tf_op jit(solution)/shard_map/ppermute | solution.py:71
  16.0 0.0 collective-permute-start.6
  16.0 0.1 shard_map.133.refs_8_.refs_12_
  16.1 0.9 %shard_map.134 = (f32[256,128]{1,0:T(8,128)S(1)}, f32[256,128]{1,0:T(8,128)S(1)}, f32[256,128]{1,0:T(8,128)S(1)}, f32[256,128]{1,0:T(8,128)S(1)}) custom-call(f32[32,4,16,128]{3,2,1,0:T(8,128)S(1)} %get-tuple-element.53.species, f32[64,128]{1,0:T(8,128)S(1)} %pad_maximum_fusion.refs_0_.refs_4_, f32[64,128]{1,0:T(8,128)S(1)} %collective-permute-done.1.refs_1_.refs_5_, ...), custom_call_target="tpu_custom_call" | custom-call | flops 1 | bytes 67108864 | tf_op jit(solution)/shard_map/pallas_call | solution.py:705
  16.9 1.8 %collective-permute-done.5.refs_4_.refs_1_ = f32[136,128]{1,0:T(8,128)S(1)} collective-permute-done((f32[136,128]{1,0:T(8,128)S(1)}, f32[136,128]{1,0:T(8,128)S(1)}, u32[]{:S(2)}, u32[]{:S(2)}) %collective-permute-start.5) | collective-permute-done | bytes 69664 | tf_op jit(solution)/shard_map/ppermute | solution.py:71
  18.7 0.0 collective-permute-done.6.refs_5_.refs_2_
  18.7 0.1 shard_map.135
  18.9 0.6 %collective-permute-start.7 = (f32[256,128]{1,0:T(8,128)S(1)}, f32[256,128]{1,0:T(8,128)S(1)}, u32[]{:S(2)}, u32[]{:S(2)}) collective-permute-start(f32[256,128]{1,0:T(8,128)S(1)} %get-tuple-element.80), channel_id=1, source_target_pairs={{0,8},{8,0},{16,24},{24,16},{1,9},{9,1},{17,25},{25,17},{2,10},{10... | collective-permute-start | bytes 393224 | tf_op jit(solution)/shard_map/ppermute | solution.py:76
  19.5 1.4 %collective-permute-start.8 = (f32[256,128]{1,0:T(8,128)S(1)}, f32[256,128]{1,0:T(8,128)S(1)}, u32[]{:S(2)}, u32[]{:S(2)}) collective-permute-start(f32[256,128]{1,0:T(8,128)S(1)} %get-tuple-element.81), channel_id=1, source_target_pairs={{0,16},{8,24},{16,0},{24,8},{1,17},{9,25},{17,1},{25,9},{2,18},{10... | collective-permute-start | bytes 393224 | tf_op jit(solution)/shard_map/ppermute | solution.py:76
  20.8 0.0 collective-permute-done.13.refs_1_
  20.8 1.6 %collective-permute-start.9 = (f32[256,128]{1,0:T(8,128)S(1)}, f32[256,128]{1,0:T(8,128)S(1)}, u32[]{:S(2)}, u32[]{:S(2)}) collective-permute-start(f32[256,128]{1,0:T(8,128)S(1)} %get-tuple-element.82), channel_id=1, source_target_pairs={{0,24},{8,16},{16,8},{24,0},{1,25},{9,17},{17,9},{25,1},{2,26},{10... | collective-permute-start | bytes 393224 | tf_op jit(solution)/shard_map/ppermute | solution.py:76
  22.5 1.7 %shard_map.137 = (f32[264,128]{1,0:T(8,128)S(1)}, f32[264,128]{1,0:T(8,128)S(1)}, f32[264,128]{1,0:T(8,128)S(1)}, f32[264,128]{1,0:T(8,128)S(1)}) custom-call(f32[336,128]{1,0:T(8,128)S(1)} %get-tuple-element.88.refs_0_, f32[336,128]{1,0:T(8,128)S(1)} %collective-permute-done.13.refs_1_, f32[336,128]{1,0:T(8,128)S(1)} %collective-permute-done.14.refs_2_, ...), custom_call_target="tpu_custom_call" | custom-call | flops 268435456 | bytes 2097152 | tf_op jit(solution)/shard_map/pallas_call | solution.py:719
  24.1 0.8 %collective-permute-start.16 = (f32[264,128]{1,0:T(8,128)S(1)}, f32[264,128]{1,0:T(8,128)S(1)}, u32[]{:S(2)}, u32[]{:S(2)}) collective-permute-start(f32[264,128]{1,0:T(8,128)S(1)} %get-tuple-element.93), channel_id=1, source_target_pairs={{0,8},{8,0},{16,24},{24,16},{1,9},{9,1},{17,25},{25,17},{2,10},{10... | collective-permute-start | bytes 405512 | tf_op jit(solution)/shard_map/ppermute | solution.py:76
  24.9 1.2 %collective-permute-start.17 = (f32[264,128]{1,0:T(8,128)S(1)}, f32[264,128]{1,0:T(8,128)S(1)}, u32[]{:S(2)}, u32[]{:S(2)}) collective-permute-start(f32[264,128]{1,0:T(8,128)S(1)} %get-tuple-element.94), channel_id=1, source_target_pairs={{0,16},{8,24},{16,0},{24,8},{1,17},{9,25},{17,1},{25,9},{2,18},{10... | collective-permute-start | bytes 405512 | tf_op jit(solution)/shard_map/ppermute | solution.py:76
  26.1 0.0 collective-permute-done.7
  26.1 1.6 %collective-permute-start.18 = (f32[264,128]{1,0:T(8,128)S(1)}, f32[264,128]{1,0:T(8,128)S(1)}, u32[]{:S(2)}, u32[]{:S(2)}) collective-permute-start(f32[264,128]{1,0:T(8,128)S(1)} %get-tuple-element.95), channel_id=1, source_target_pairs={{0,24},{8,16},{16,8},{24,0},{1,25},{9,17},{17,9},{25,1},{2,26},{10... | collective-permute-start | bytes 405512 | tf_op jit(solution)/shard_map/ppermute | solution.py:76
  27.7 0.0 collective-permute-done.8
  27.7 0.0 collective-permute-done.9
  27.7 0.8 %shard_map.136 = (f32[256,128]{1,0:T(8,128)S(1)}, f32[256,128]{1,0:T(8,128)S(1)}, f32[256,128]{1,0:T(8,128)S(1)}, f32[256,128]{1,0:T(8,128)S(1)}, f32[8,128]{1,0:T(8,128)S(1)}) custom-call(f32[8,32,128]{2,1,0:T(8,128)S(1)} %bitcast.21, f32[8,32,128]{2,1,0:T(8,128)S(1)} %bitcast.22, f32[8,32,128]{2,1,0:T(8,128)S(1)} %bitcast.23, f32[8,32,128]{2,1,0:T(8,128)S(1)} %bitcast.24, ...), custom_call_target="tpu_custom_call" | custom-call | flops 268435456 | bytes 2097152 | tf_op jit(solution)/shard_map/pallas_call | solution.py:732
  28.5 1.8 %collective-permute-start.10 = (f32[256,128]{1,0:T(8,128)S(1)}, f32[256,128]{1,0:T(8,128)S(1)}, u32[]{:S(2)}, u32[]{:S(2)}) collective-permute-start(f32[256,128]{1,0:T(8,128)S(1)} %get-tuple-element.85), channel_id=1, source_target_pairs={{0,8},{8,0},{16,24},{24,16},{1,9},{9,1},{17,25},{25,17},{2,10},{10... | collective-permute-start | bytes 393224 | tf_op jit(solution)/shard_map/ppermute | solution.py:76
  30.3 0.5 %collective-permute-start.11 = (f32[256,128]{1,0:T(8,128)S(1)}, f32[256,128]{1,0:T(8,128)S(1)}, u32[]{:S(2)}, u32[]{:S(2)}) collective-permute-start(f32[256,128]{1,0:T(8,128)S(1)} %get-tuple-element.86), channel_id=1, source_target_pairs={{0,16},{8,24},{16,0},{24,8},{1,17},{9,25},{17,1},{25,9},{2,18},{10... | collective-permute-start | bytes 393224 | tf_op jit(solution)/shard_map/ppermute | solution.py:76
  30.8 0.3 collective-permute-done.16.refs_1_
  31.1 1.2 %collective-permute-start.12 = (f32[256,128]{1,0:T(8,128)S(1)}, f32[256,128]{1,0:T(8,128)S(1)}, u32[]{:S(2)}, u32[]{:S(2)}) collective-permute-start(f32[256,128]{1,0:T(8,128)S(1)} %get-tuple-element.87), channel_id=1, source_target_pairs={{0,24},{8,16},{16,8},{24,0},{1,25},{9,17},{17,9},{25,1},{2,26},{10... | collective-permute-start | bytes 393224 | tf_op jit(solution)/shard_map/ppermute | solution.py:76
  32.3 1.4 %collective-permute-done.17.refs_2_ = f32[264,128]{1,0:T(8,128)S(1)} collective-permute-done((f32[264,128]{1,0:T(8,128)S(1)}, f32[264,128]{1,0:T(8,128)S(1)}, u32[]{:S(2)}, u32[]{:S(2)}) %collective-permute-start.17) | collective-permute-done | bytes 135200 | tf_op jit(solution)/shard_map/ppermute | solution.py:76
  33.8 0.0 collective-permute-done.18.refs_3_
  33.8 0.0 copy-start.6
  33.8 1.2 %shard_map.138 = (f32[32,4,16,128]{3,2,1,0:T(8,128)}, f32[8,128]{1,0:T(8,128)S(1)}) custom-call(f32[264,128]{1,0:T(8,128)S(1)} %get-tuple-element.92.refs_0_, f32[264,128]{1,0:T(8,128)S(1)} %collective-permute-done.16.refs_1_, f32[264,128]{1,0:T(8,128)S(1)} %collective-permute-done.17.refs_2_, f32[264,128]{1,0:T(8,128)S(1)} %collective-permute-done.18.refs_3_), custom_call_target="tpu_custom_call" | custom-call | flops 1 | bytes 1048576 | tf_op jit(solution)/shard_map/pallas_call | solution.py:748
  35.0 0.7 %shard_map.140 = (f32[1,16,128]{2,1,0:T(8,128)}, f32[1,16,128]{2,1,0:T(8,128)}, f32[1,16,128]{2,1,0:T(8,128)}) custom-call(f32[1,16,128]{2,1,0:T(8,128)S(1)} %copy-done.4, f32[1,16,128]{2,1,0:T(8,128)S(1)} %copy-done.3, f32[1,16,128]{2,1,0:T(8,128)S(1)} %copy-done.2, f32[1,16,128]{2,1,0:T(8,128)S(1)} %copy-done.6, ...), custom_call_target="tpu_custom_call" | custom-call | flops 1 | bytes 1 | tf_op jit(solution)/shard_map/pallas_call | solution.py:756
  35.7 1.1 %collective-permute-done.10 = f32[256,128]{1,0:T(8,128)S(1)} collective-permute-done((f32[256,128]{1,0:T(8,128)S(1)}, f32[256,128]{1,0:T(8,128)S(1)}, u32[]{:S(2)}, u32[]{:S(2)}) %collective-permute-start.10) | collective-permute-done | bytes 131104 | tf_op jit(solution)/shard_map/ppermute | solution.py:76
  36.8 1.7 %collective-permute-done.11 = f32[256,128]{1,0:T(8,128)S(1)} collective-permute-done((f32[256,128]{1,0:T(8,128)S(1)}, f32[256,128]{1,0:T(8,128)S(1)}, u32[]{:S(2)}, u32[]{:S(2)}) %collective-permute-start.11) | collective-permute-done | bytes 131104 | tf_op jit(solution)/shard_map/ppermute | solution.py:76
  38.5 0.8 %shard_map.139 = f32[32,4,16,128]{3,2,1,0:T(8,128)} custom-call(f32[32,8,128]{2,1,0:T(8,128)S(1)} %bitcast.13, f32[32,8,128]{2,1,0:T(8,128)S(1)} %bitcast.14, f32[32,8,128]{2,1,0:T(8,128)S(1)} %bitcast.15, f32[32,8,128]{2,1,0:T(8,128)S(1)} %bitcast.16, f32[32,4,16,128]{3,2,1,0:T(8,128)} %get-tuple-element.96.refs_4_), custom_call_target="tpu_custom_call", output_to_operand_aliasing={{}: (4, {})} | custom-call | flops 1 | bytes 1048576 | tf_op jit(solution)/shard_map/pallas_call | solution.py:770
  (32 shorter events, 0.1 us)
Async XLA Ops:
  1.4 7.4 %collective-permute-start.1 = (f32[64,128]{1,0:T(8,128)S(1)}, f32[64,128]{1,0:T(8,128)S(1)}, u32[]{:S(2)}, u32[]{:S(2)}) collective-permute-start(f32[64,128]{1,0:T(8,128)S(1)} %pad_maximum_fusion.refs_0_.refs_4_), channel_id=1, source_target_pairs={{0,8},{8,0},{16,24},{24,16},{1,9},{9,1},{17,25},{25,17},{2,10},{10... | collective-permute-start | bytes 98312 | tf_op jit(solution)/shard_map/ppermute | solution.py:76
  4.3 4.5 %collective-permute-start.2 = (f32[64,128]{1,0:T(8,128)S(1)}, f32[64,128]{1,0:T(8,128)S(1)}, u32[]{:S(2)}, u32[]{:S(2)}) collective-permute-start(f32[64,128]{1,0:T(8,128)S(1)} %pad_maximum_fusion.refs_0_.refs_4_), channel_id=1, source_target_pairs={{0,16},{8,24},{16,0},{24,8},{1,17},{9,25},{17,1},{25,9},{2,18},{10... | collective-permute-start | bytes 98312 | tf_op jit(solution)/shard_map/ppermute | solution.py:76
  5.8 4.8 %collective-permute-start.3 = (f32[64,128]{1,0:T(8,128)S(1)}, f32[64,128]{1,0:T(8,128)S(1)}, u32[]{:S(2)}, u32[]{:S(2)}) collective-permute-start(f32[64,128]{1,0:T(8,128)S(1)} %pad_maximum_fusion.refs_0_.refs_4_), channel_id=1, source_target_pairs={{0,24},{8,16},{16,8},{24,0},{1,25},{9,17},{17,9},{25,1},{2,26},{10... | collective-permute-start | bytes 98312 | tf_op jit(solution)/shard_map/ppermute | solution.py:76
  7.5 1.2 %collective-permute-start = (f32[16,128]{1,0:T(8,128)S(1)}, f32[16,128]{1,0:T(8,128)S(1)}, u32[]{:S(2)}, u32[]{:S(2)}) collective-permute-start(f32[16,128]{1,0:T(8,128)S(1)} %get-tuple-element.54), channel_id=1, source_target_pairs={{0,1},{1,0},{2,3},{3,2},{4,5},{5,4},{6,7},{7,6},{8,9},{9,8},{10,11... | collective-permute-start | bytes 24584 | tf_op jit(solution)/shard_map/ppermute | solution.py:56
  10.7 3.6 %collective-permute-start.4 = (f32[96,128]{1,0:T(8,128)S(1)}, f32[96,128]{1,0:T(8,128)S(1)}, u32[]{:S(2)}, u32[]{:S(2)}) collective-permute-start(f32[96,128]{1,0:T(8,128)S(1)} %get-tuple-element.103), channel_id=1, source_target_pairs={{0,1},{1,0},{2,3},{3,2},{4,5},{5,4},{6,7},{7,6},{8,9},{9,8},{10,11... | collective-permute-start | bytes 147464 | tf_op jit(solution)/shard_map/ppermute | solution.py:56
  10.7 10.2 %collective-permute-start.13 = (f32[336,128]{1,0:T(8,128)S(1)}, f32[336,128]{1,0:T(8,128)S(1)}, u32[]{:S(2)}, u32[]{:S(2)}) collective-permute-start(f32[336,128]{1,0:T(8,128)S(1)} %get-tuple-element.89), channel_id=1, source_target_pairs={{0,8},{8,0},{16,24},{24,16},{1,9},{9,1},{17,25},{25,17},{2,10},{10... | collective-permute-start | bytes 516104 | tf_op jit(solution)/shard_map/ppermute | solution.py:76
  11.3 11.2 %collective-permute-start.14 = (f32[336,128]{1,0:T(8,128)S(1)}, f32[336,128]{1,0:T(8,128)S(1)}, u32[]{:S(2)}, u32[]{:S(2)}) collective-permute-start(f32[336,128]{1,0:T(8,128)S(1)} %get-tuple-element.90), channel_id=1, source_target_pairs={{0,16},{8,24},{16,0},{24,8},{1,17},{9,25},{17,1},{25,9},{2,18},{10... | collective-permute-start | bytes 516104 | tf_op jit(solution)/shard_map/ppermute | solution.py:76
  12.6 9.8 %collective-permute-start.15 = (f32[336,128]{1,0:T(8,128)S(1)}, f32[336,128]{1,0:T(8,128)S(1)}, u32[]{:S(2)}, u32[]{:S(2)}) collective-permute-start(f32[336,128]{1,0:T(8,128)S(1)} %get-tuple-element.91), channel_id=1, source_target_pairs={{0,24},{8,16},{16,8},{24,0},{1,25},{9,17},{17,9},{25,1},{2,26},{10... | collective-permute-start | bytes 516104 | tf_op jit(solution)/shard_map/ppermute | solution.py:76
  14.3 1.7 %copy-start.7 = (f32[128]{0:T(128)S(1)}, f32[128]{0:T(128)}, u32[]{:S(2)}) copy-start(f32[128]{0:T(128)} %param.19) | copy-start | bytes 1540
  14.3 4.4 %collective-permute-start.5 = (f32[136,128]{1,0:T(8,128)S(1)}, f32[136,128]{1,0:T(8,128)S(1)}, u32[]{:S(2)}, u32[]{:S(2)}) collective-permute-start(f32[136,128]{1,0:T(8,128)S(1)} %get-tuple-element.70), channel_id=1, source_target_pairs={{0,2},{2,0},{4,6},{6,4},{1,3},{3,1},{5,7},{7,5},{8,10},{10,8},{12,... | collective-permute-start | bytes 208904 | tf_op jit(solution)/shard_map/ppermute | solution.py:71
  16.0 2.7 %collective-permute-start.6 = (f32[136,128]{1,0:T(8,128)S(1)}, f32[136,128]{1,0:T(8,128)S(1)}, u32[]{:S(2)}, u32[]{:S(2)}) collective-permute-start(f32[136,128]{1,0:T(8,128)S(1)} %get-tuple-element.71), channel_id=1, source_target_pairs={{0,1},{1,0},{2,4},{3,5},{4,2},{5,3},{6,7},{7,6},{8,9},{9,8},{10,12... | collective-permute-start | bytes 208904 | tf_op jit(solution)/shard_map/ppermute | solution.py:72
  18.7 3.7 %copy-start = (bf16[512,128]{1,0:T(8,128)(2,1)S(1)}, bf16[512,128]{1,0:T(8,128)(2,1)}, u32[]{:S(2)}) copy-start(bf16[512,128]{1,0:T(8,128)(2,1)} %refs_10_.1) | copy-start | bytes 393220
  18.7 3.7 %copy-start.1 = (bf16[128,512]{1,0:T(8,128)(2,1)S(1)}, bf16[128,512]{1,0:T(8,128)(2,1)}, u32[]{:S(2)}) copy-start(bf16[128,512]{1,0:T(8,128)(2,1)} %refs_11_.1) | copy-start | bytes 393220
  18.7 3.7 %copy-start.5 = (s32[16,128]{1,0:T(8,128)S(1)}, s32[16,128]{1,0:T(8,128)}, u32[]{:S(2)}) copy-start(s32[16,128]{1,0:T(8,128)} %refs_9_.1) | copy-start | bytes 24580
  18.9 7.2 %collective-permute-start.7 = (f32[256,128]{1,0:T(8,128)S(1)}, f32[256,128]{1,0:T(8,128)S(1)}, u32[]{:S(2)}, u32[]{:S(2)}) collective-permute-start(f32[256,128]{1,0:T(8,128)S(1)} %get-tuple-element.80), channel_id=1, source_target_pairs={{0,8},{8,0},{16,24},{24,16},{1,9},{9,1},{17,25},{25,17},{2,10},{10... | collective-permute-start | bytes 393224 | tf_op jit(solution)/shard_map/ppermute | solution.py:76
  19.5 8.2 %collective-permute-start.8 = (f32[256,128]{1,0:T(8,128)S(1)}, f32[256,128]{1,0:T(8,128)S(1)}, u32[]{:S(2)}, u32[]{:S(2)}) collective-permute-start(f32[256,128]{1,0:T(8,128)S(1)} %get-tuple-element.81), channel_id=1, source_target_pairs={{0,16},{8,24},{16,0},{24,8},{1,17},{9,25},{17,1},{25,9},{2,18},{10... | collective-permute-start | bytes 393224 | tf_op jit(solution)/shard_map/ppermute | solution.py:76
  20.8 6.9 %collective-permute-start.9 = (f32[256,128]{1,0:T(8,128)S(1)}, f32[256,128]{1,0:T(8,128)S(1)}, u32[]{:S(2)}, u32[]{:S(2)}) collective-permute-start(f32[256,128]{1,0:T(8,128)S(1)} %get-tuple-element.82), channel_id=1, source_target_pairs={{0,24},{8,16},{16,8},{24,0},{1,25},{9,17},{17,9},{25,1},{2,26},{10... | collective-permute-start | bytes 393224 | tf_op jit(solution)/shard_map/ppermute | solution.py:76
  24.1 6.9 %collective-permute-start.16 = (f32[264,128]{1,0:T(8,128)S(1)}, f32[264,128]{1,0:T(8,128)S(1)}, u32[]{:S(2)}, u32[]{:S(2)}) collective-permute-start(f32[264,128]{1,0:T(8,128)S(1)} %get-tuple-element.93), channel_id=1, source_target_pairs={{0,8},{8,0},{16,24},{24,16},{1,9},{9,1},{17,25},{25,17},{2,10},{10... | collective-permute-start | bytes 405512 | tf_op jit(solution)/shard_map/ppermute | solution.py:76
  24.9 8.8 %collective-permute-start.17 = (f32[264,128]{1,0:T(8,128)S(1)}, f32[264,128]{1,0:T(8,128)S(1)}, u32[]{:S(2)}, u32[]{:S(2)}) collective-permute-start(f32[264,128]{1,0:T(8,128)S(1)} %get-tuple-element.94), channel_id=1, source_target_pairs={{0,16},{8,24},{16,0},{24,8},{1,17},{9,25},{17,1},{25,9},{2,18},{10... | collective-permute-start | bytes 405512 | tf_op jit(solution)/shard_map/ppermute | solution.py:76
  26.1 7.7 %collective-permute-start.18 = (f32[264,128]{1,0:T(8,128)S(1)}, f32[264,128]{1,0:T(8,128)S(1)}, u32[]{:S(2)}, u32[]{:S(2)}) collective-permute-start(f32[264,128]{1,0:T(8,128)S(1)} %get-tuple-element.95), channel_id=1, source_target_pairs={{0,24},{8,16},{16,8},{24,0},{1,25},{9,17},{17,9},{25,1},{2,26},{10... | collective-permute-start | bytes 405512 | tf_op jit(solution)/shard_map/ppermute | solution.py:76
  28.5 8.3 %collective-permute-start.10 = (f32[256,128]{1,0:T(8,128)S(1)}, f32[256,128]{1,0:T(8,128)S(1)}, u32[]{:S(2)}, u32[]{:S(2)}) collective-permute-start(f32[256,128]{1,0:T(8,128)S(1)} %get-tuple-element.85), channel_id=1, source_target_pairs={{0,8},{8,0},{16,24},{24,16},{1,9},{9,1},{17,25},{25,17},{2,10},{10... | collective-permute-start | bytes 393224 | tf_op jit(solution)/shard_map/ppermute | solution.py:76
  30.3 8.2 %collective-permute-start.11 = (f32[256,128]{1,0:T(8,128)S(1)}, f32[256,128]{1,0:T(8,128)S(1)}, u32[]{:S(2)}, u32[]{:S(2)}) collective-permute-start(f32[256,128]{1,0:T(8,128)S(1)} %get-tuple-element.86), channel_id=1, source_target_pairs={{0,16},{8,24},{16,0},{24,8},{1,17},{9,25},{17,1},{25,9},{2,18},{10... | collective-permute-start | bytes 393224 | tf_op jit(solution)/shard_map/ppermute | solution.py:76
  31.1 7.4 %collective-permute-start.12 = (f32[256,128]{1,0:T(8,128)S(1)}, f32[256,128]{1,0:T(8,128)S(1)}, u32[]{:S(2)}, u32[]{:S(2)}) collective-permute-start(f32[256,128]{1,0:T(8,128)S(1)} %get-tuple-element.87), channel_id=1, source_target_pairs={{0,24},{8,16},{16,8},{24,0},{1,25},{9,17},{17,9},{25,1},{2,26},{10... | collective-permute-start | bytes 393224 | tf_op jit(solution)/shard_map/ppermute | solution.py:76
  33.8 1.2 %copy-start.2 = (f32[1,16,128]{2,1,0:T(8,128)S(1)}, f32[1,16,128]{2,1,0:T(8,128)}, u32[]{:S(2)}) copy-start(f32[1,16,128]{2,1,0:T(8,128)} %warmth.1) | copy-start | bytes 24580
  33.8 1.2 %copy-start.3 = (f32[1,16,128]{2,1,0:T(8,128)S(1)}, f32[1,16,128]{2,1,0:T(8,128)}, u32[]{:S(2)}) copy-start(f32[1,16,128]{2,1,0:T(8,128)} %north.1) | copy-start | bytes 24580
  33.8 1.2 %copy-start.4 = (f32[1,16,128]{2,1,0:T(8,128)S(1)}, f32[1,16,128]{2,1,0:T(8,128)}, u32[]{:S(2)}) copy-start(f32[1,16,128]{2,1,0:T(8,128)} %east.1) | copy-start | bytes 24580
  33.8 1.2 %copy-start.6 = (f32[1,16,128]{2,1,0:T(8,128)S(1)}, f32[1,16,128]{2,1,0:T(8,128)}, u32[]{:S(2)}) copy-start(f32[1,16,128]{2,1,0:T(8,128)} %density.1) | copy-start | bytes 24580
